TPU v7x, 32 devices: a whole 2x2x4 slice. The times are simulated.
32 devices in a mesh: rep: 4 (over y, x), row: 2 (over core), col: 4 (over z).
Axes of the slice: x: 2, y: 2, z: 4, core: 2. Of those that a mesh axis runs over, the one named last changes fastest.
Arguments:
- tokens: bfloat16 [6144, 4096], P('rep', 'row'), may hold values from -6 to 6
- cotangent: bfloat16 [6144, 512], P(('rep', 'row'), 'col'), may hold values from -4 to 4
- weight: float32 [4, 4096, 512], P('rep', 'row', 'col'), may hold values from -0.09375 to 0.09375
- first_moment: float32 [4, 4096, 512], P('rep', 'row', 'col'), may hold values from -6 to 6
- second_moment: float32 [4, 4096, 512], P('rep', 'row', 'col'), may hold values from 1 to 10
- outer_delta: float32 [4, 1310720], P('rep', ('row', 'col')), may hold values from -6 to 6
- global_params: float32 [2, 1310720], P(None, ('row', 'col')), may hold values from -6 to 6
- outer_moment: float32 [2, 1310720], P(None, ('row', 'col')), may hold values from -6 to 6
- group_slot: int32 [1], replicated, may hold values from 0 to 1
Outputs:
- keys_values: bfloat16 [6144, 512], P(('rep', 'row'), 'col')
- input_grad: bfloat16 [6144, 4096], P(('rep', 'col'), 'row')
- new_weight: float32 [4, 4096, 512], P('rep', 'row', 'col')
- new_first: float32 [4, 4096, 512], P('rep', 'row', 'col')
- new_second: float32 [4, 4096, 512], P('rep', 'row', 'col')
- new_global: float32 [1310720], P(('row', 'col'))
- new_outer: float32 [1310720], P(('row', 'col'))
Inputs may be any that keep to these rules, and one draw needn't show every extreme that they name: `group_slot`: the held group that the outer delta belongs to.
All inputs are finite; a program needn't handle non-finite values.
Results may differ from a plain program's by a relative error of at most 0.015.
Values may be sent and summed in bfloat16 or wider, within the bound.
No kernel may reach another device: no remote copies, remote signals or barrier semaphores. Data moves between devices by JAX's collectives and lax.ppermute only.
A program may use at most 64 MiB of HBM per device.

v0:
```python
import jax
import jax.numpy as jnp
from jax import lax
from jax.sharding import PartitionSpec as P

BETA_ONE = 0.9
BETA_TWO = 0.95
INNER_RATE = 0.0003
WEIGHT_DECAY = 0.1
EPSILON = 1e-08
OUTER_RATE = 0.7
NESTEROV = 0.9


def nesterov_merge(average, held_group, prior_moment):
    new_outer = NESTEROV * prior_moment + average
    new_global = held_group - OUTER_RATE * (average + NESTEROV * new_outer)
    return (new_global, new_outer)


def outer_step(outer_delta, global_params, outer_moment, group_slot):
    chosen = group_slot[0]
    held_group = lax.dynamic_index_in_dim(global_params, chosen, 0, keepdims=False)
    prior_moment = lax.dynamic_index_in_dim(outer_moment, chosen, 0, keepdims=False)
    replicas = lax.axis_size("rep")
    average = lax.psum(outer_delta[0].astype(jnp.bfloat16), "rep").astype(jnp.float32) / replicas
    new_global, new_outer = nesterov_merge(average, held_group, prior_moment)
    return (new_global, new_outer)


def inner_step(tokens, cotangent, weight, first_moment, second_moment):
    weight_bf = weight[0].astype(jnp.bfloat16)
    columns = lax.axis_size("col")
    head_size = weight_bf.shape[1]
    weight_all = lax.all_gather(weight_bf, "col", axis=1, tiled=True)
    keys_values = lax.psum_scatter(
        jnp.dot(tokens, weight_bf, preferred_element_type=jnp.float32).astype(jnp.bfloat16),
        "row",
        scatter_dimension=0,
        tiled=True,
    )
    cot_full = lax.all_gather(cotangent, "row", axis=0, tiled=True)
    gradient = jnp.einsum("td,tc->dc", tokens, cot_full, preferred_element_type=jnp.float32)
    cot_mine = lax.all_to_all(cot_full, "col", split_axis=0, concat_axis=1, tiled=True)
    cot_split = cot_mine.reshape(cot_mine.shape[0], columns, head_size)
    weight_split = weight_all.reshape(weight_all.shape[0], columns, head_size)
    pieces = jnp.einsum("tch,dch->ctd", cot_split, weight_split, preferred_element_type=jnp.float32)
    rounded = lax.optimization_barrier(pieces.astype(jnp.bfloat16))
    input_grad = jnp.sum(rounded.astype(jnp.float32), axis=0).astype(jnp.bfloat16)
    first_new = BETA_ONE * first_moment[0] + (1.0 - BETA_ONE) * gradient
    second_new = BETA_TWO * second_moment[0] + (1.0 - BETA_TWO) * gradient * gradient
    weight_new = weight[0] - INNER_RATE * (
        first_new / (jnp.sqrt(second_new) + EPSILON) + WEIGHT_DECAY * weight[0]
    )
    return (keys_values, input_grad, weight_new[None], first_new[None], second_new[None])


def on_device(
    tokens,
    cotangent,
    weight,
    first_moment,
    second_moment,
    outer_delta,
    global_params,
    outer_moment,
    group_slot,
):
    keys_values, input_grad, new_weight, new_first, new_second = inner_step(
        tokens, cotangent, weight, first_moment, second_moment
    )
    new_global, new_outer = outer_step(outer_delta, global_params, outer_moment, group_slot)
    return (keys_values, input_grad, new_weight, new_first, new_second, new_global, new_outer)


def solution(mesh):
    in_specs = (
        P("rep", "row"),
        P(("rep", "row"), "col"),
        P("rep", "row", "col"),
        P("rep", "row", "col"),
        P("rep", "row", "col"),
        P("rep", ("row", "col")),
        P(None, ("row", "col")),
        P(None, ("row", "col")),
        P(),
    )
    out_specs = (
        P(("rep", "row"), "col"),
        P(("rep", "col"), "row"),
        P("rep", "row", "col"),
        P("rep", "row", "col"),
        P("rep", "row", "col"),
        P(("row", "col")),
        P(("row", "col")),
    )
    return jax.shard_map(
        on_device, mesh=mesh, in_specs=in_specs, out_specs=out_specs, check_vma=False
    )
```

profile of v0, /device:TPU:0, one launch (start us, length us, event | category | flops | bytes accessed | tf_op | source)
XLA Modules:
  0.0 98.2 jit_solution(15075747876525701347)
XLA Ops:
  8.0 0.0 copy-start
  8.0 0.0 all-reduce.2.cloned.1.call-start
  8.1 8.6 %convert_reduce_fusion = bf16[163840]{0:T(1024)(128)(2,1)} fusion(f32[1,163840]{1,0:T(1,128)} %param.14), kind=kLoop, calls=%fused_computation.15 | loop fusion | flops 163840 | bytes 983040 | tf_op jit(solution)/shard_map/convert_element_type | solution.py:26
  16.6 0.0 all-reduce.2.cloned.1.call-update
  16.6 0.0 all-gather.2.cloned.1.call-start
  16.7 2.1 %bitcast_convert_fusion = bf16[2048,128]{1,0:T(8,128)(2,1)} fusion(f32[1,2048,128]{2,1,0:T(8,128)} %param.11), kind=kLoop, calls=%fused_computation.7 | loop fusion | flops 262144 | bytes 1572864 | tf_op jit(solution)/shard_map/convert_element_type | solution.py:32
  18.8 0.0 all-gather.2.cloned.1.call-update
  18.8 4.0 %all_gather.6 = bf16[1536,128]{1,0:T(8,128)(2,1)} all-gather(bf16[768,128]{1,0:T(8,128)(2,1)} %param.10), channel_id=1, replica_groups=mesh['rep'=4,'row'=2,'col'=4] {'row'}, dimensions={0}, use_global_device_ids=true | all-gather | bytes 589824 | tf_op jit(solution)/shard_map/all_gather | solution.py:42
  22.8 6.0 %all-to-all-start = ((bf16[4,384,128]{2,1,0:T(8,128)(2,1)}), bf16[4,384,128]{2,1,0:T(8,128)(2,1)S(1)}, u32[]{:S(2)}, u32[]{:S(2)}) async-start(bf16[4,384,128]{2,1,0:T(8,128)(2,1)} %bitcast.1), calls=%async_computation.1 | async-start | bytes 786432 | tf_op jit(solution)/shard_map/all_to_all | solution.py:44
  28.8 0.0 reduce-scatter.2.cloned.1.call-start
  28.8 5.6 %convolution_convert_fusion.1 = bf16[1536,128]{1,0:T(8,128)(2,1)} fusion(bf16[1536,2048]{1,0:T(8,128)(2,1)} %param.9, bf16[2048,128]{1,0:T(8,128)(2,1)} %bitcast_convert_fusion), kind=kOutput, calls=%fused_computation.1 | convolution fusion | flops 805502976 | bytes 7208960 | tf_op jit(solution)/shard_map/dot_general | solution.py:37
  34.4 0.0 reduce-scatter.2.cloned.1.call-update
  35.1 0.0 copy-done
  35.1 0.0 copy-start.1
  35.1 7.4 %fusion.7 = (f32[1,2048,128]{2,1,0:T(8,128)}, f32[1,2048,128]{2,1,0:T(8,128)}, f32[1,2048,128]{2,1,0:T(8,128)}) fusion(f32[1,2048,128]{2,1,0:T(8,128)} %param.13, f32[1,2048,128]{2,1,0:T(8,128)} %param.12, f32[1,2048,128]{2,1,0:T(8,128)S(1)} %copy-done, bf16[1536,2048]{1,0:T(8,128)(2,1)} %param.9, bf16[1536,128]{1,0:T(8,128)(2,1)} %all_gather.6), kind=kOutput, calls=%fused_computation.18 | convolution fusion | flops 808714240 | bytes 12976128 | tf_op jit(solution)/shard_map/td,tc->dc/dot_general | solution.py:43
  42.5 0.0 copy-done.1
  42.5 2.6 %dynamic-slice_multiply_fusion = (f32[1,163840]{1,0:T(1,128)S(1)}, f32[1,163840]{1,0:T(1,128)S(1)}) fusion(f32[2,163840]{1,0:T(2,128)S(1)} %copy-done.1, s32[]{:T(128)S(6)} %select_n.5, f32[2,163840]{1,0:T(2,128)} %param.15), kind=kLoop, calls=%fused_computation.12 | loop fusion | flops 163840 | bytes 2621444 | tf_op jit(solution)/shard_map/mul | solution.py:16
  45.2 17.9 %all-reduce.2.cloned.1.call-done = bf16[163840]{0:T(1024)(128)(2,1)} async-done(((bf16[163840]{0:T(1024)(128)(2,1)}), bf16[163840]{0:T(1024)(128)(2,1)}) %all-reduce.2.cloned.1.call-update) | async-done | bytes 327696 | tf_op jit(solution)/shard_map/psum | solution.py:26
  63.0 2.2 %multiply_subtract_fusion = (f32[163840]{0:T(1024)}, f32[163840]{0:T(1024)}) fusion(f32[163840]{0:T(1024)S(1)} %bitcast.48, bf16[163840]{0:T(1024)(128)(2,1)} %all-reduce.2.cloned.1.call-done, f32[163840]{0:T(1024)S(1)} %bitcast.47), kind=kLoop, calls=%fused_computation.11 | loop fusion | flops 1146880 | bytes 2949120 | tf_op jit(solution)/shard_map/sub | solution.py:17
  65.2 12.5 %all-gather.2.cloned.1.call-done = bf16[2048,512]{1,0:T(8,128)(2,1)} async-done(((bf16[2048,128]{1,0:T(8,128)(2,1)}), bf16[2048,512]{1,0:T(8,128)(2,1)}) %all-gather.2.cloned.1.call-update) | async-done | bytes 2097168 | tf_op jit(solution)/shard_map/all_gather | solution.py:35
  77.7 2.9 %copy.16 = bf16[2048,512]{0,1:T(8,128)(2,1)S(1)} copy(bf16[2048,512]{1,0:T(8,128)(2,1)} %all-gather.2.cloned.1.call-done) | data formatting | bytes 4194304 | tf_op jit(solution)/shard_map/all_gather | solution.py:35
  80.6 0.0 all-to-all-done
  80.6 4.4 %convolution_convert_fusion = bf16[4,384,2048]{2,1,0:T(8,128)(2,1)} fusion(bf16[2048,4,128]{0,2,1:T(8,128)(2,1)S(1)} %bitcast.46, bf16[4,384,128]{2,1,0:T(8,128)(2,1)S(1)} %all-to-all-done), kind=kOutput, calls=%fused_computation | convolution fusion | flops 808452096 | bytes 8781824 | tf_op jit(solution)/shard_map/tch,dch->ctd/dot_general | solution.py:47
  85.1 5.7 %reduce_sum.12 = bf16[384,2048]{1,0:T(8,128)(2,1)} reduce(bf16[4,384,2048]{2,1,0:T(8,128)(2,1)} %convolution_convert_fusion, bf16[]{:T(256)} %constant.11.clone.1), dimensions={0}, to_apply=%region_1.0 | reduce | flops 2359296 | bytes 7864322 | tf_op jit(solution)/shard_map/reduce_sum | solution.py:49
  90.7 0.0 reduce-scatter.2.cloned.1.call-done
Async XLA Ops:
  8.0 27.1 %copy-start = (f32[1,2048,128]{2,1,0:T(8,128)S(1)}, f32[1,2048,128]{2,1,0:T(8,128)}, u32[]{:S(2)}) copy-start(f32[1,2048,128]{2,1,0:T(8,128)} %param.11) | copy-start | bytes 3145732
  8.0 55.0 %all-reduce.2.cloned.1.call-start = ((), (), s32[]{:S(2)}) async-start(), calls=%async_computation.4 | async-start | bytes 655360 | tf_op jit(solution)/shard_map/psum | solution.py:26
  16.6 61.0 %all-gather.2.cloned.1.call-start = ((), (), s32[]{:S(2)}) async-start(), calls=%async_computation.3 | async-start | bytes 2621440 | tf_op jit(solution)/shard_map/all_gather | solution.py:35
  22.8 57.8 %all-to-all-start = ((bf16[4,384,128]{2,1,0:T(8,128)(2,1)}), bf16[4,384,128]{2,1,0:T(8,128)(2,1)S(1)}, u32[]{:S(2)}, u32[]{:S(2)}) async-start(bf16[4,384,128]{2,1,0:T(8,128)(2,1)} %bitcast.1), calls=%async_computation.1 | async-start | bytes 786432 | tf_op jit(solution)/shard_map/all_to_all | solution.py:44
  28.8 61.9 %reduce-scatter.2.cloned.1.call-start = ((), (), s32[]{:S(2)}) async-start(), calls=%async_computation.2 | async-start | bytes 589824 | tf_op jit(solution)/shard_map/reduce_scatter | solution.py:36
  35.1 7.4 %copy-start.1 = (f32[2,163840]{1,0:T(2,128)S(1)}, f32[2,163840]{1,0:T(2,128)}, u32[]{:S(2)}) copy-start(f32[2,163840]{1,0:T(2,128)} %param.16) | copy-start | bytes 3932164
Sparse Core Ops, SparseCore 0:
  16.8 46.2 all-reduce.1
  65.9 7.7 reduce-scatter.1
Sparse Core Ops, SparseCore 1:
  19.2 58.4 all-gather.1
where the time goes:
time: 98.6 us; the launch traced here: 98.2 us
  waiting for transfers between devices  30.4 us (31%)
  other arithmetic  21.1 us (21%)
  matrix products  17.5 us (18%)
  between operations  16.2 us (16%)
  starting transfers between devices  6.13 us (6%)
  blocking collectives  3.98 us (4%)
  local copies, waits for them, and re-layouts  2.94 us (3%)
    psum x1, waiting for transfers between devices, outer_step(): lax.psum(outer_delta[0].astype(jnp.bfloat16), 'rep').astype(jnp.float32)  17.9 us
    all_gather x1, waiting for transfers between devices, inner_step(): weight_all = lax.all_gather(weight_bf, 'col', axis=1, tiled=True)  12.5 us
    convert_element_type x1, other arithmetic, outer_step(): outer_delta[0].astype(jnp.bfloat16)  8.55 us
    dot_general x1, matrix products, inner_step(): jnp.einsum('td,tc->dc', tokens, cot_full, preferred_element_type=jnp.floa...  7.41 us
    all_to_all x1, starting transfers between devices, inner_step(): lax.all_to_all(cot_full, 'col', split_axis=0, concat_axis=1, tiled=True)  6.04 us
    reduce_sum x1, other arithmetic, inner_step(): jnp.sum(rounded.astype(jnp.float32), axis=0).astype(jnp.bfloat16)  5.66 us
    dot_general x1, matrix products, inner_step(): jnp.dot(tokens, weight_bf, preferred_element_type=jnp.float32)  5.63 us
    dot_general x1, matrix products, inner_step(): jnp.einsum('tch,dch->ctd', cot_split, weight_split, preferred_element_typ...  4.44 us
  transfers between devices with their start and end apart: 4, of which 2 were waited for; matrix products, arithmetic and copies ran while one was open for 34% of the time, Pallas kernels for 0%

commit v1 on v0

--- a/solution.py
+++ b/solution.py
@@ -12,6 +12,73 @@
 NESTEROV = 0.9
 
 
+def is_power_of_two(n):
+    return n & (n - 1) == 0
+
+
+def swap_pairs(n, bit):
+    return [(i, i ^ bit) for i in range(n)]
+
+
+def gather_offsets(block, axis):
+    n = lax.axis_size(axis)
+    have = {0: block}
+    if is_power_of_two(n):
+        bit = n // 2
+        while bit:
+            for k in list(have):
+                have[k ^ bit] = lax.ppermute(have[k], axis, swap_pairs(n, bit))
+            bit //= 2
+        owner = lambda k: lax.axis_index(axis) ^ k
+    else:
+        for k in range(1, n):
+            have[k] = lax.ppermute(have[k - 1], axis, [((i + 1) % n, i) for i in range(n)])
+        owner = lambda k: (lax.axis_index(axis) + k) % n
+    return have, owner
+
+
+def row_gather(block, axis):
+    n = lax.axis_size(axis)
+    me = lax.axis_index(axis)
+    parts = {0: block}
+    for k in range(1, n):
+        parts[k] = lax.ppermute(block, axis, [((i + k) % n, i) for i in range(n)])
+    stacked = jnp.stack([parts[k] for k in range(n)])
+    if n == 2:
+        return jnp.where(me == 0, stacked, stacked[::-1])
+    return jnp.roll(stacked, me, axis=0)
+
+
+def my_cotangent(cotangent, rows, cols):
+    per_row = cols // rows
+    chunks = cotangent.reshape(per_row, cotangent.shape[0] // per_row, cotangent.shape[1])
+    col = lax.axis_index("col")
+    got = []
+    for k in range(per_row):
+        pairs = []
+        for r in range(rows):
+            for c in range(cols):
+                pairs.append((r * cols + c, (c // per_row) * cols + r * per_row + (c + k) % per_row))
+        send = lax.dynamic_index_in_dim(chunks, (col + k) % per_row, 0, keepdims=False)
+        got.append(lax.ppermute(send, ("row", "col"), pairs))
+    stacked = jnp.stack(got)
+    ordered = jnp.take(stacked, (col - jnp.arange(per_row)) % per_row, axis=0)
+    every = row_gather(ordered, "row")
+    return every.reshape((cols,) + every.shape[2:])
+
+
+def rep_sum(x, axis):
+    n = lax.axis_size(axis)
+    if not is_power_of_two(n):
+        return lax.psum(x.astype(jnp.bfloat16), axis).astype(jnp.float32)
+    bit = 1
+    while bit < n:
+        low = x.astype(jnp.bfloat16)
+        x = low.astype(jnp.float32) + lax.ppermute(low, axis, swap_pairs(n, bit)).astype(jnp.float32)
+        bit *= 2
+    return x
+
+
 def nesterov_merge(average, held_group, prior_moment):
     new_outer = NESTEROV * prior_moment + average
     new_global = held_group - OUTER_RATE * (average + NESTEROV * new_outer)
@@ -23,35 +90,39 @@
     held_group = lax.dynamic_index_in_dim(global_params, chosen, 0, keepdims=False)
     prior_moment = lax.dynamic_index_in_dim(outer_moment, chosen, 0, keepdims=False)
     replicas = lax.axis_size("rep")
-    average = lax.psum(outer_delta[0].astype(jnp.bfloat16), "rep").astype(jnp.float32) / replicas
-    new_global, new_outer = nesterov_merge(average, held_group, prior_moment)
-    return (new_global, new_outer)
+    size = outer_delta.shape[1]
+    average = rep_sum(outer_delta.reshape(size // 128, 128), "rep").reshape(size) / replicas
+    return nesterov_merge(average, held_group, prior_moment)
 
 
 def inner_step(tokens, cotangent, weight, first_moment, second_moment):
+    rows, cols = lax.axis_size("row"), lax.axis_size("col")
+    row = lax.axis_index("row")
     weight_bf = weight[0].astype(jnp.bfloat16)
-    columns = lax.axis_size("col")
-    head_size = weight_bf.shape[1]
-    weight_all = lax.all_gather(weight_bf, "col", axis=1, tiled=True)
-    keys_values = lax.psum_scatter(
-        jnp.dot(tokens, weight_bf, preferred_element_type=jnp.float32).astype(jnp.bfloat16),
-        "row",
-        scatter_dimension=0,
-        tiled=True,
-    )
-    cot_full = lax.all_gather(cotangent, "row", axis=0, tiled=True)
+    cot_mine = my_cotangent(cotangent, rows, cols)
+    weights, owner = gather_offsets(weight_bf, "col")
+
+    cot_full = row_gather(cotangent, "row").reshape(-1, cotangent.shape[1])
+    partial = jnp.dot(tokens, weight_bf, preferred_element_type=jnp.float32)
+    partial = partial.reshape(rows, partial.shape[0] // rows, partial.shape[1])
+    keys_values = lax.dynamic_index_in_dim(partial, row, 0, keepdims=False)
+    for k in range(1, rows):
+        send = lax.dynamic_index_in_dim(partial, (row + k) % rows, 0, keepdims=False).astype(jnp.bfloat16)
+        keys_values += lax.ppermute(send, "row", [(i, (i + k) % rows) for i in range(rows)]).astype(jnp.float32)
+    keys_values = keys_values.astype(jnp.bfloat16)
+
     gradient = jnp.einsum("td,tc->dc", tokens, cot_full, preferred_element_type=jnp.float32)
-    cot_mine = lax.all_to_all(cot_full, "col", split_axis=0, concat_axis=1, tiled=True)
-    cot_split = cot_mine.reshape(cot_mine.shape[0], columns, head_size)
-    weight_split = weight_all.reshape(weight_all.shape[0], columns, head_size)
-    pieces = jnp.einsum("tch,dch->ctd", cot_split, weight_split, preferred_element_type=jnp.float32)
-    rounded = lax.optimization_barrier(pieces.astype(jnp.bfloat16))
-    input_grad = jnp.sum(rounded.astype(jnp.float32), axis=0).astype(jnp.bfloat16)
     first_new = BETA_ONE * first_moment[0] + (1.0 - BETA_ONE) * gradient
     second_new = BETA_TWO * second_moment[0] + (1.0 - BETA_TWO) * gradient * gradient
     weight_new = weight[0] - INNER_RATE * (
         first_new / (jnp.sqrt(second_new) + EPSILON) + WEIGHT_DECAY * weight[0]
     )
+
+    total = jnp.zeros((cot_mine.shape[1], weight_bf.shape[0]), jnp.float32)
+    for k, block in weights.items():
+        cot = lax.dynamic_index_in_dim(cot_mine, owner(k), 0, keepdims=False)
+        total += jnp.einsum("th,dh->td", cot, block, preferred_element_type=jnp.float32)
+    input_grad = total.astype(jnp.bfloat16)
     return (keys_values, input_grad, weight_new[None], first_new[None], second_new[None])
 
 

time: 98.6 us -> 83.6 us (0.85)
  waiting for transfers between devices: 30.4 us -> 8.09 us
  local copies, waits for them, and re-layouts: 2.94 us -> 17.8 us
  between operations: 16.2 us -> 1.47 us
  starting transfers between devices: 6.13 us -> 14.5 us
  blocking collectives: 3.98 us -> 0 us
  other arithmetic: 21.1 us -> 23.5 us
    psum x1 -> x0, waiting for transfers between devices: 17.9 us -> none  [outer_step(): lax.psum(outer_delta[0].astype(jnp.bfloat16), 'rep').astype(jnp.float32)]
    ppermute x0 -> x10, starting transfers between devices: none -> 14.5 us  [the longest x3 6.3 us: gather_offsets(): have[k ^ bit] = lax.ppermute(have[k], axis, swap_pairs(n, bit))]
    all_gather x1 -> x0, waiting for transfers between devices: 12.5 us -> none  [inner_step(): weight_all = lax.all_gather(weight_bf, 'col', axis=1, tiled=True)]
    unnamed x4 -> x20, local copies, waits for them, and re-layouts: 0.01 us -> 12.3 us
    ppermute x0 -> x10, waiting for transfers between devices: none -> 8.09 us  [the longest x2 4.67 us: rep_sum(): lax.ppermute(low, axis, swap_pairs(n, bit)).astype(jnp.float32)]
    all_to_all x1 -> x0, starting transfers between devices: 6.04 us -> none  [inner_step(): lax.all_to_all(cot_full, 'col', split_axis=0, concat_axis=1, tiled=True)]
    reduce_sum x1 -> x0, other arithmetic: 5.66 us -> none  [inner_step(): jnp.sum(rounded.astype(jnp.float32), axis=0).astype(jnp.bfloat16)]
    all_gather x1 -> x0, blocking collectives: 3.98 us -> none  [inner_step(): cot_full = lax.all_gather(cotangent, 'row', axis=0, tiled=True)]
  transfers between devices with their start and end apart: 4 -> 10, of which waited for: 2 -> 2; matrix products, arithmetic and copies ran while one was open for 34% -> 66% of each run, Pallas kernels for 0% -> 0%
where the time goes in v1:
time: 83.6 us; the launch traced here: 82.8 us
  other arithmetic  23.5 us (28%)
  local copies, waits for them, and re-layouts  17.8 us (21%)
  matrix products  17.5 us (21%)
  starting transfers between devices  14.5 us (17%)
  waiting for transfers between devices  8.09 us (10%)
  between operations  1.47 us (2%)
    unnamed x20, local copies, waits for them, and re-layouts  12.3 us
    convert_element_type x2, other arithmetic, rep_sum(): low = x.astype(jnp.bfloat16)  7.86 us
    dot_general x1, matrix products, inner_step(): jnp.einsum('td,tc->dc', tokens, cot_full, preferred_element_type=jnp.floa...  6.38 us
    ppermute x3, starting transfers between devices, gather_offsets(): have[k ^ bit] = lax.ppermute(have[k], axis, swap_pairs(n, bit))  6.3 us
    dot_general x4, matrix products, inner_step(): jnp.einsum('th,dh->td', cot, block, preferred_element_type=jnp.float32)  5.54 us
    dot_general x1, matrix products, inner_step(): partial = jnp.dot(tokens, weight_bf, preferred_element_type=jnp.float32)  5.54 us
    ppermute x2, waiting for transfers between devices, rep_sum(): lax.ppermute(low, axis, swap_pairs(n, bit)).astype(jnp.float32)  4.67 us
    mul x1, other arithmetic, nesterov_merge(): new_outer = NESTEROV * prior_moment + average  3.66 us
  transfers between devices with their start and end apart: 10, of which 2 were waited for; matrix products, arithmetic and copies ran while one was open for 66% of the time, Pallas kernels for 0%

profile of v1, /device:TPU:0, one launch (start us, length us, event | category | flops | bytes accessed | tf_op | source)
XLA Modules:
  0.0 82.8 jit_solution(1046577348841329293)
XLA Ops:
  0.6 0.0 copy-start
  0.6 1.6 %copy.16 = f32[1,2048,128]{1,2,0:T(8,128)S(1)} copy(f32[1,2048,128]{2,1,0:T(8,128)} %param.11) | data formatting | bytes 2097152 | tf_op args[2]
  2.3 0.9 %bitcast_convert_fusion = bf16[2048,128]{0,1:T(8,128)(2,1)} fusion(f32[1,2048,128]{1,2,0:T(8,128)S(1)} %copy.16), kind=kLoop, calls=%fused_computation.8 | loop fusion | flops 262144 | bytes 1572864 | tf_op jit(solution)/shard_map/convert_element_type | solution.py:101
  3.2 4.0 %collective-permute-start.4 = (bf16[2048,128]{0,1:T(8,128)(2,1)}, bf16[2048,128]{0,1:T(8,128)(2,1)}, u32[]{:S(2)}, u32[]{:S(2)}) collective-permute-start(bf16[2048,128]{0,1:T(8,128)(2,1)} %bitcast_convert_fusion), channel_id=1, source_target_pairs={{0,2},{1,3},{2,0},{3,1},{4,6},{5,7},{6,4},{7,5},{8,10},{9,11},{10,... | collective-permute-start | bytes 1572872 | tf_op jit(solution)/shard_map/ppermute | solution.py:30
  7.2 1.6 %collective-permute-start.5 = (bf16[2048,128]{0,1:T(8,128)(2,1)}, bf16[2048,128]{0,1:T(8,128)(2,1)}, u32[]{:S(2)}, u32[]{:S(2)}) collective-permute-start(bf16[2048,128]{0,1:T(8,128)(2,1)} %bitcast_convert_fusion), channel_id=1, source_target_pairs={{0,1},{1,0},{2,3},{3,2},{4,5},{5,4},{6,7},{7,6},{8,9},{9,8},{10,11... | collective-permute-start | bytes 1572872 | tf_op jit(solution)/shard_map/ppermute | solution.py:30
  8.8 0.0 collective-permute-start.7
  8.8 1.6 %dynamic-slice_bitcast_fusion.1 = (bf16[384,128]{1,0:T(8,128)(2,1)}, bf16[384,128]{1,0:T(8,128)(2,1)}) fusion(bf16[2,384,128]{2,1,0:T(8,128)(2,1)} %bitcast.5, s32[]{:T(128)S(6)} %select_n.116, s32[]{:T(128)S(6)} %select_n.118), kind=kLoop, calls=%fused_computation.50 | loop fusion | bytes 393224 | tf_op jit(solution)/shard_map/jit(dynamic_index_in_dim)/squeeze | solution.py:62
  10.4 2.1 %collective-permute-start.1 = (bf16[384,128]{1,0:T(8,128)(2,1)}, bf16[384,128]{1,0:T(8,128)(2,1)}, u32[]{:S(2)}, u32[]{:S(2)}) collective-permute-start(bf16[384,128]{1,0:T(8,128)(2,1)} %get-tuple-element.19), channel_id=1, source_target_pairs={{0,0},{1,1},{2,4},{3,5},{4,2},{5,3},{6,6},{7,7},{8,8},{9,9},{10,12... | collective-permute-start | bytes 294920 | tf_op jit(solution)/shard_map/ppermute | solution.py:63
  12.5 0.4 collective-permute-start.2
  13.0 0.0 copy-done
  13.0 0.0 copy-start.6
  13.1 5.5 %fusion.6 = f32[2,768,128]{2,1,0:T(8,128)} fusion(bf16[2,768,2048]{2,1,0:T(8,128)(2,1)} %bitcast.99, f32[1,2048,128]{2,1,0:T(8,128)S(1)} %copy-done), kind=kOutput, calls=%fused_computation.22 | convolution fusion | flops 805568512 | bytes 8126464 | tf_op jit(solution)/shard_map/dot_general | solution.py:106
  19.3 0.0 copy-done.6
  19.3 6.8 %convert_reduce_fusion = bf16[163840]{0:T(1024)(128)(2,1)S(1)} fusion(f32[1,163840]{1,0:T(1,128)S(1)} %copy-done.6), kind=kLoop, calls=%fused_computation.19 | loop fusion | flops 163840 | bytes 983040 | tf_op jit(solution)/shard_map/convert_element_type | solution.py:76
  26.1 1.6 %copy.17 = f32[1,2048,128]{1,2,0:T(8,128)S(1)} copy(f32[1,2048,128]{2,1,0:T(8,128)} %param.12) | data formatting | bytes 2097152 | tf_op args[3]
  27.6 2.5 %copy.18 = f32[1,2048,128]{1,2,0:T(8,128)} copy(f32[1,2048,128]{2,1,0:T(8,128)} %param.13) | data formatting | bytes 2097152 | tf_op args[4]
  30.2 1.7 %fusion.15 = bf16[768,128]{1,0:T(8,128)(2,1)} fusion(f32[2,768,128]{2,1,0:T(8,128)} %fusion.6, s32[]{:T(128)S(6)} %select_n.111), kind=kLoop, calls=%fused_computation.35 | loop fusion | bytes 393220 | tf_op jit(solution)/shard_map/convert_element_type | solution.py:110
  31.9 3.7 %dynamic-slice_multiply_fusion = (f32[1,163840]{1,0:T(1,128)}, f32[1,163840]{1,0:T(1,128)}) fusion(f32[2,163840]{1,0:T(2,128)} %param.16, s32[]{:T(128)S(6)} %select_n.130, f32[2,163840]{1,0:T(2,128)} %param.15), kind=kLoop, calls=%fused_computation.16 | loop fusion | flops 163840 | bytes 2621444 | tf_op jit(solution)/shard_map/mul | solution.py:83
  35.5 0.0 collective-permute-done.1
  35.5 2.5 %collective-permute-start = (bf16[768,128]{1,0:T(8,128)(2,1)}, bf16[768,128]{1,0:T(8,128)(2,1)}, u32[]{:S(2)}, u32[]{:S(2)}) collective-permute-start(bf16[768,128]{1,0:T(8,128)(2,1)} %fusion.15), channel_id=1, source_target_pairs={{0,4},{4,0},{1,5},{5,1},{2,6},{6,2},{3,7},{7,3},{8,12},{12,8},{9,1... | collective-permute-start | bytes 589832 | tf_op jit(solution)/shard_map/ppermute | solution.py:111
  38.0 0.0 collective-permute-done.2
  38.0 1.5 %collective-permute-start.8 = (bf16[1280,128]{1,0:T(8,128)(2,1)S(1)}, bf16[1280,128]{1,0:T(8,128)(2,1)}, u32[]{:S(2)}, u32[]{:S(2)}) collective-permute-start(bf16[1280,128]{1,0:T(8,128)(2,1)S(1)} %bitcast.100), channel_id=1, source_target_pairs={{0,8},{8,0},{16,24},{24,16},{1,9},{9,1},{17,25},{25,17},{2,10},{10... | collective-permute-start | bytes 983048 | tf_op jit(solution)/shard_map/ppermute | solution.py:77
  39.5 1.6 %pad_maximum_fusion.2 = bf16[2,384,128]{2,1,0:T(8,128)(2,1)} fusion(bf16[1,384,128]{2,1,0:T(8,128)(2,1)} %bitcast.9, bf16[1,384,128]{2,1,0:T(8,128)(2,1)} %bitcast.7), kind=kLoop, calls=%fused_computation.36 | loop fusion | flops 98304 | bytes 393216 | tf_op jit(solution)/shard_map/stack | solution.py:64
  41.2 2.2 %gather_fusion = bf16[2,384,128]{2,1,0:T(8,128)(2,1)} fusion(bf16[2,384,128]{2,1,0:T(8,128)(2,1)} %pad_maximum_fusion.2, s32[1024]{0:T(1024)S(1)} %pad_clamp_fusion), kind=kCustom, calls=%fused_computation | custom fusion | bytes 393224 | tf_op jit(solution)/shard_map/jit(_take)/gather | solution.py:65
  43.3 1.7 %broadcast_select_fusion = bf16[2,384,128]{2,1,0:T(8,128)(2,1)} fusion(bf16[2,384,128]{2,1,0:T(8,128)(2,1)} %gather_fusion, pred[2]{0:T(512)(128)(4,1)S(1)} %compare_and_fusion), kind=kLoop, calls=%fused_computation.38 | loop fusion | flops 98304 | bytes 393218 | tf_op jit(solution)/shard_map/jit(_take)/select_n | solution.py:65
  45.0 1.7 %bitcast_select_fusion = bf16[1,2,384,128]{3,2,1,0:T(8,128)(2,1)} fusion(bf16[2,384,128]{2,1,0:T(8,128)(2,1)} %gather_fusion, pred[2]{0:T(512)(128)(4,1)S(1)} %compare_and_fusion), kind=kLoop, calls=%fused_computation.37 | loop fusion | flops 98304 | bytes 393218 | tf_op jit(solution)/shard_map/jit(_take)/select_n | solution.py:65
  46.7 0.0 collective-permute-done.7
  46.7 0.0 collective-permute-start.3
  46.7 1.1 %pad_maximum_fusion.1 = bf16[2,768,128]{2,1,0:T(8,128)(2,1)S(1)} fusion(bf16[1,768,128]{2,1,0:T(8,128)(2,1)} %bitcast.21, bf16[1,768,128]{2,1,0:T(8,128)(2,1)} %bitcast.20), kind=kLoop, calls=%fused_computation.27 | loop fusion | flops 196608 | bytes 786432 | tf_op jit(solution)/shard_map/stack | solution.py:46
  47.8 0.1 reverse_select_fusion
  47.9 6.4 %fusion.12 = (f32[1,2048,128]{1,2,0:T(8,128)}, f32[1,2048,128]{1,2,0:T(8,128)}, f32[1,2048,128]{1,2,0:T(8,128)}) fusion(f32[1,2048,128]{1,2,0:T(8,128)} %copy.18, f32[1,2048,128]{1,2,0:T(8,128)S(1)} %copy.17, f32[1,2048,128]{1,2,0:T(8,128)S(1)} %copy.16, bf16[1536,128]{1,0:T(8,128)(2,1)S(1)} %bitcast.103, bf16[1536,2048]{1,0:T(8,128)(2,1)} %param.9), kind=kOutput, calls=%fused_computation.32 | convolution fusion | flops 808714240 | bytes 12976128 | tf_op jit(solution)/shard_map/td,tc->dc/dot_general | solution.py:114
  54.3 0.0 copy-start.1
  54.3 0.0 copy-start.4
  54.3 0.0 copy-start.5
  54.3 2.7 %copy.19 = f32[1,2048,128]{2,1,0:T(8,128)} copy(f32[1,2048,128]{1,2,0:T(8,128)} %get-tuple-element.17) | data formatting | bytes 2097152
  56.9 2.5 %copy.20 = f32[1,2048,128]{2,1,0:T(8,128)} copy(f32[1,2048,128]{1,2,0:T(8,128)} %get-tuple-element.18) | data formatting | bytes 2097152
  59.5 0.0 copy-done.1
  59.5 1.3 %copy.21 = f32[1,2048,128]{2,1,0:T(8,128)} copy(f32[1,2048,128]{1,2,0:T(8,128)S(1)} %copy-done.1) | data formatting | bytes 2097152
  60.8 0.0 collective-permute-done
  60.8 0.0 copy-done.4
  60.8 1.6 %fusion.10 = bf16[768,128]{1,0:T(8,128)(2,1)} fusion(bf16[768,128]{1,0:T(8,128)(2,1)} %collective-permute-done, f32[2,768,128]{2,1,0:T(8,128)S(1)} %copy-done.4, s32[]{:T(128)S(6)} %select_n.109), kind=kLoop, calls=%fused_computation.29 | loop fusion | flops 294912 | bytes 786436 | tf_op jit(solution)/shard_map/convert_element_type | solution.py:112
  62.4 0.0 collective-permute-done.3
  62.4 0.0 copy-done.5
  62.4 1.0 %pad_maximum_fusion = bf16[2,2,384,128]{3,2,1,0:T(8,128)(2,1)S(1)} fusion(bf16[1,2,384,128]{3,2,1,0:T(8,128)(2,1)} %bitcast.12, bf16[1,2,384,128]{3,2,1,0:T(8,128)(2,1)S(1)} %copy-done.5), kind=kLoop, calls=%fused_computation.26 | loop fusion | flops 196608 | bytes 786432 | tf_op jit(solution)/shard_map/stack | solution.py:46
  63.4 0.1 reverse_select_fusion.1
  63.5 0.6 fusion.8
  64.1 0.0 collective-permute-done.8
  64.1 1.1 %add_convert_fusion.1 = bf16[1280,128]{1,0:T(8,128)(2,1)S(1)} fusion(bf16[1280,128]{1,0:T(8,128)(2,1)} %collective-permute-done.8, bf16[163840]{0:T(1024)(128)(2,1)S(1)} %convert_reduce_fusion), kind=kLoop, calls=%fused_computation.18 | loop fusion | flops 655360 | bytes 983040 | tf_op jit(solution)/shard_map/convert_element_type | solution.py:76
  65.2 0.0 copy-start.2
  65.2 0.0 copy-start.3
  65.2 1.6 %collective-permute-start.9 = (bf16[1280,128]{1,0:T(8,128)(2,1)S(1)}, bf16[1280,128]{1,0:T(8,128)(2,1)S(1)}, u32[]{:S(2)}, u32[]{:S(2)}) collective-permute-start(bf16[1280,128]{1,0:T(8,128)(2,1)S(1)} %add_convert_fusion.1), channel_id=1, source_target_pairs={{0,16},{8,24},{16,0},{24,8},{1,17},{9,25},{17,1},{25,9},{2,18},{10... | collective-permute-start | bytes 983048 | tf_op jit(solution)/shard_map/ppermute | solution.py:77
  66.8 0.0 collective-permute-done.4
  66.8 0.7 collective-permute-start.6
  67.4 1.6 %fusion.19 = f32[384,2048]{1,0:T(8,128)S(1)} fusion(bf16[2048,128]{0,1:T(8,128)(2,1)} %collective-permute-done.4, bf16[4,384,128]{2,1,0:T(8,128)(2,1)S(1)} %bitcast.105, s32[]{:T(128)S(6)} %select_n.125), kind=kOutput, calls=%fused_computation.42 | convolution fusion | flops 201326592 | bytes 3768324 | tf_op jit(solution)/shard_map/th,dh->td/dot_general | solution.py:124
  69.1 0.0 collective-permute-done.5
  69.1 1.6 %fusion.17 = f32[384,2048]{1,0:T(8,128)S(1)} fusion(bf16[2048,128]{0,1:T(8,128)(2,1)} %collective-permute-done.5, bf16[4,384,128]{2,1,0:T(8,128)(2,1)S(1)} %bitcast.106, s32[]{:T(128)S(6)} %select_n.126), kind=kOutput, calls=%fused_computation.40 | convolution fusion | flops 201326592 | bytes 3768324 | tf_op jit(solution)/shard_map/th,dh->td/dot_general | solution.py:124
  70.7 4.7 %collective-permute-done.9 = bf16[1280,128]{1,0:T(8,128)(2,1)S(1)} collective-permute-done((bf16[1280,128]{1,0:T(8,128)(2,1)S(1)}, bf16[1280,128]{1,0:T(8,128)(2,1)S(1)}, u32[]{:S(2)}, u32[]{:S(2)}) %collective-permute-start.9) | collective-permute-done | bytes 327712 | tf_op jit(solution)/shard_map/ppermute | solution.py:77
  75.4 0.0 copy-done.2
  75.4 0.0 copy-done.3
  75.4 2.3 %fusion.5 = (f32[163840]{0:T(1024)}, f32[163840]{0:T(1024)}) fusion(f32[163840]{0:T(1024)S(1)} %bitcast.102, bf16[1280,128]{1,0:T(8,128)(2,1)S(1)} %collective-permute-done.9, f32[163840]{0:T(1024)S(1)} %bitcast.101, bf16[1280,128]{1,0:T(8,128)(2,1)} %collective-permute-done.8, bf16[163840]{0:T(1024)(128)(2,1)S(1)} %convert_reduce_fusion), kind=kLoop, calls=%fused_computation.15 | loop fusion | flops 2129920 | bytes 3604480 | tf_op jit(solution)/shard_map/sub | solution.py:84
  77.6 3.4 %collective-permute-done.6 = bf16[2048,128]{0,1:T(8,128)(2,1)S(1)} collective-permute-done((bf16[2048,128]{0,1:T(8,128)(2,1)}, bf16[2048,128]{0,1:T(8,128)(2,1)S(1)}, u32[]{:S(2)}, u32[]{:S(2)}) %collective-permute-start.6) | collective-permute-done | bytes 524320 | tf_op jit(solution)/shard_map/ppermute | solution.py:30
  81.0 1.7 %add_convert_fusion = bf16[384,2048]{1,0:T(8,128)(2,1)} fusion(f32[384,2048]{1,0:T(8,128)S(1)} %fusion.17, f32[384,2048]{1,0:T(8,128)S(1)} %fusion.8, f32[384,2048]{1,0:T(8,128)S(1)} %fusion.19, bf16[2048,128]{0,1:T(8,128)(2,1)S(1)} %collective-permute-done.6, bf16[4,384,128]{2,1,0:T(8,128)(2,1)S(1)} %bitcast.107, s32[]{:T(128)S(6)} %select_n.127), kind=kOutput, calls=%fused_computation.1 | convolution fusion | flops 204472320 | bytes 11632644 | tf_op jit(solution)/shard_map/th,dh->td/dot_general | solution.py:124
  (3 shorter events, 0.0 us)
Async XLA Ops:
  0.6 12.4 %copy-start = (f32[1,2048,128]{2,1,0:T(8,128)S(1)}, f32[1,2048,128]{2,1,0:T(8,128)}, u32[]{:S(2)}) copy-start(f32[1,2048,128]{2,1,0:T(8,128)} %param.11) | copy-start | bytes 3145732
  3.2 63.6 %collective-permute-start.4 = (bf16[2048,128]{0,1:T(8,128)(2,1)}, bf16[2048,128]{0,1:T(8,128)(2,1)}, u32[]{:S(2)}, u32[]{:S(2)}) collective-permute-start(bf16[2048,128]{0,1:T(8,128)(2,1)} %bitcast_convert_fusion), channel_id=1, source_target_pairs={{0,2},{1,3},{2,0},{3,1},{4,6},{5,7},{6,4},{7,5},{8,10},{9,11},{10,... | collective-permute-start | bytes 1572872 | tf_op jit(solution)/shard_map/ppermute | solution.py:30
  7.2 61.9 %collective-permute-start.5 = (bf16[2048,128]{0,1:T(8,128)(2,1)}, bf16[2048,128]{0,1:T(8,128)(2,1)}, u32[]{:S(2)}, u32[]{:S(2)}) collective-permute-start(bf16[2048,128]{0,1:T(8,128)(2,1)} %bitcast_convert_fusion), channel_id=1, source_target_pairs={{0,1},{1,0},{2,3},{3,2},{4,5},{5,4},{6,7},{7,6},{8,9},{9,8},{10,11... | collective-permute-start | bytes 1572872 | tf_op jit(solution)/shard_map/ppermute | solution.py:30
  8.8 38.0 %collective-permute-start.7 = (bf16[768,128]{1,0:T(8,128)(2,1)}, bf16[768,128]{1,0:T(8,128)(2,1)}, u32[]{:S(2)}, u32[]{:S(2)}) collective-permute-start(bf16[768,128]{1,0:T(8,128)(2,1)} %param.10), channel_id=1, source_target_pairs={{4,0},{0,4},{5,1},{1,5},{6,2},{2,6},{7,3},{3,7},{12,8},{8,12},{13,... | collective-permute-start | bytes 589832 | tf_op jit(solution)/shard_map/ppermute | solution.py:45
  10.4 25.1 %collective-permute-start.1 = (bf16[384,128]{1,0:T(8,128)(2,1)}, bf16[384,128]{1,0:T(8,128)(2,1)}, u32[]{:S(2)}, u32[]{:S(2)}) collective-permute-start(bf16[384,128]{1,0:T(8,128)(2,1)} %get-tuple-element.19), channel_id=1, source_target_pairs={{0,0},{1,1},{2,4},{3,5},{4,2},{5,3},{6,6},{7,7},{8,8},{9,9},{10,12... | collective-permute-start | bytes 294920 | tf_op jit(solution)/shard_map/ppermute | solution.py:63
  12.5 25.5 %collective-permute-start.2 = (bf16[384,128]{1,0:T(8,128)(2,1)}, bf16[384,128]{1,0:T(8,128)(2,1)}, u32[]{:S(2)}, u32[]{:S(2)}) collective-permute-start(bf16[384,128]{1,0:T(8,128)(2,1)} %get-tuple-element.20), channel_id=1, source_target_pairs={{0,1},{1,0},{2,5},{3,4},{4,3},{5,2},{6,7},{7,6},{8,9},{9,8},{10,13... | collective-permute-start | bytes 294920 | tf_op jit(solution)/shard_map/ppermute | solution.py:63
  13.0 6.2 %copy-start.6 = (f32[1,163840]{1,0:T(1,128)S(1)}, f32[1,163840]{1,0:T(1,128)}, u32[]{:S(2)}) copy-start(f32[1,163840]{1,0:T(1,128)} %param.14) | copy-start | bytes 1966084
  35.5 25.3 %collective-permute-start = (bf16[768,128]{1,0:T(8,128)(2,1)}, bf16[768,128]{1,0:T(8,128)(2,1)}, u32[]{:S(2)}, u32[]{:S(2)}) collective-permute-start(bf16[768,128]{1,0:T(8,128)(2,1)} %fusion.15), channel_id=1, source_target_pairs={{0,4},{4,0},{1,5},{5,1},{2,6},{6,2},{3,7},{7,3},{8,12},{12,8},{9,1... | collective-permute-start | bytes 589832 | tf_op jit(solution)/shard_map/ppermute | solution.py:111
  38.0 26.0 %collective-permute-start.8 = (bf16[1280,128]{1,0:T(8,128)(2,1)S(1)}, bf16[1280,128]{1,0:T(8,128)(2,1)}, u32[]{:S(2)}, u32[]{:S(2)}) collective-permute-start(bf16[1280,128]{1,0:T(8,128)(2,1)S(1)} %bitcast.100), channel_id=1, source_target_pairs={{0,8},{8,0},{16,24},{24,16},{1,9},{9,1},{17,25},{25,17},{2,10},{10... | collective-permute-start | bytes 983048 | tf_op jit(solution)/shard_map/ppermute | solution.py:77
  46.7 15.7 %collective-permute-start.3 = (bf16[2,384,128]{2,1,0:T(8,128)(2,1)}, bf16[2,384,128]{2,1,0:T(8,128)(2,1)}, u32[]{:S(2)}, u32[]{:S(2)}) collective-permute-start(bf16[2,384,128]{2,1,0:T(8,128)(2,1)} %broadcast_select_fusion), channel_id=1, source_target_pairs={{4,0},{0,4},{5,1},{1,5},{6,2},{2,6},{7,3},{3,7},{12,8},{8,12},{13,... | collective-permute-start | bytes 589832 | tf_op jit(solution)/shard_map/ppermute | solution.py:45
  54.3 5.2 %copy-start.1 = (f32[1,2048,128]{1,2,0:T(8,128)S(1)}, f32[1,2048,128]{1,2,0:T(8,128)}, u32[]{:S(2)}) copy-start(f32[1,2048,128]{1,2,0:T(8,128)} %get-tuple-element.16) | copy-start | bytes 3145732
  54.3 6.5 %copy-start.4 = (f32[2,768,128]{2,1,0:T(8,128)S(1)}, f32[2,768,128]{2,1,0:T(8,128)}, u32[]{:S(2)}) copy-start(f32[2,768,128]{2,1,0:T(8,128)} %fusion.6) | copy-start | bytes 2359300
  54.3 8.2 %copy-start.5 = (bf16[1,2,384,128]{3,2,1,0:T(8,128)(2,1)S(1)}, bf16[1,2,384,128]{3,2,1,0:T(8,128)(2,1)}, u32[]{:S(2)}) copy-start(bf16[1,2,384,128]{3,2,1,0:T(8,128)(2,1)} %bitcast_select_fusion) | copy-start | bytes 589828
  65.2 10.2 %copy-start.2 = (f32[1,163840]{1,0:T(1,128)S(1)}, f32[1,163840]{1,0:T(1,128)}, u32[]{:S(2)}) copy-start(f32[1,163840]{1,0:T(1,128)} %get-tuple-element.21) | copy-start | bytes 1966084
  65.2 10.2 %copy-start.3 = (f32[1,163840]{1,0:T(1,128)S(1)}, f32[1,163840]{1,0:T(1,128)}, u32[]{:S(2)}) copy-start(f32[1,163840]{1,0:T(1,128)} %get-tuple-element.22) | copy-start | bytes 1966084
  65.2 10.2 %collective-permute-start.9 = (bf16[1280,128]{1,0:T(8,128)(2,1)S(1)}, bf16[1280,128]{1,0:T(8,128)(2,1)S(1)}, u32[]{:S(2)}, u32[]{:S(2)}) collective-permute-start(bf16[1280,128]{1,0:T(8,128)(2,1)S(1)} %add_convert_fusion.1), channel_id=1, source_target_pairs={{0,16},{8,24},{16,0},{24,8},{1,17},{9,25},{17,1},{25,9},{2,18},{10... | collective-permute-start | bytes 983048 | tf_op jit(solution)/shard_map/ppermute | solution.py:77
  66.8 14.3 %collective-permute-start.6 = (bf16[2048,128]{0,1:T(8,128)(2,1)}, bf16[2048,128]{0,1:T(8,128)(2,1)S(1)}, u32[]{:S(2)}, u32[]{:S(2)}) collective-permute-start(bf16[2048,128]{0,1:T(8,128)(2,1)} %collective-permute-done.4), channel_id=1, source_target_pairs={{0,1},{1,0},{2,3},{3,2},{4,5},{5,4},{6,7},{7,6},{8,9},{9,8},{10,11... | collective-permute-start | bytes 1572872 | tf_op jit(solution)/shard_map/ppermute | solution.py:30

commit v2 on v0

v2 whole, which is shorter than its diff:
```python
import functools

import jax
import jax.numpy as jnp
from jax import lax
from jax.experimental import pallas as pl
from jax.experimental.pallas import tpu as pltpu
from jax.sharding import PartitionSpec as P

BETA_ONE = 0.9
BETA_TWO = 0.95
INNER_RATE = 0.0003
WEIGHT_DECAY = 0.1
EPSILON = 1e-08
OUTER_RATE = 0.7
NESTEROV = 0.9
LANES = 128
HALVES = 2

WHOLE = pl.BlockSpec(memory_space=pltpu.VMEM)
HBM = pl.BlockSpec(memory_space=pltpu.HBM)


def params(mebibytes):
    return pltpu.CompilerParams(vmem_limit_bytes=mebibytes * 1024 * 1024)


def after(x, others):
    return lax.optimization_barrier((x, others))


def in_hbm(x):
    return pltpu.with_memory_space_constraint(x, pltpu.HBM)


def is_power_of_two(n):
    return n & (n - 1) == 0


def swap_pairs(n, bit):
    return [(i, i ^ bit) for i in range(n)]


def shift_pairs(n, k):
    return [(i, (i + k) % n) for i in range(n)]


def mod(value, n):
    return lax.rem(value + n, n)


def gather_halves(halves, whole, axis):
    n = lax.axis_size(axis)
    have = [{0: (whole, h)} for h in range(len(halves))]
    if is_power_of_two(n):
        bit = n // 2
        for h, half in enumerate(halves):
            if bit > 1:
                have[h][bit] = (lax.ppermute(half, axis, swap_pairs(n, bit)), 0)
        while bit > 1:
            bit //= 2
            mine = lax.ppermute(whole, axis, swap_pairs(n, bit))
            for h in range(len(halves)):
                for k in list(have[h]):
                    have[h][k ^ bit] = (mine, h) if k == 0 else (lax.ppermute(have[h][k][0], axis, swap_pairs(n, bit)), 0)
        if n == 2:
            mine = lax.ppermute(whole, axis, swap_pairs(n, 1))
            for h in range(len(halves)):
                have[h][1] = (mine, h)
    else:
        moving = whole
        for k in range(1, n):
            moving = lax.ppermute(moving, axis, shift_pairs(n, n - 1))
            for h in range(len(halves)):
                have[h][k] = (moving, h)
    return [[have[h][k] for k in range(n)] for h in range(len(halves))]


def owner_of(me, k, n):
    return me ^ k if is_power_of_two(n) else mod(me + k, n)


def shifted(block, axis):
    n = lax.axis_size(axis)
    return [block] + [lax.ppermute(block, axis, shift_pairs(n, k)) for k in range(1, n)]


def chunk_pairs(rows, cols, per_row, k):
    pairs = []
    for r in range(rows):
        for c in range(cols):
            pairs.append((r * cols + c, (c // per_row) * cols + r * per_row + (c + k) % per_row))
    return pairs


def prepare_kernel(per_row, halves, weight_hbm, cot_hbm, delta_hbm, *refs):
    half_refs, whole_ref, low_ref = refs[:halves], refs[halves], refs[halves + 1]
    chunk_refs = refs[halves + 2:halves + 2 + per_row]
    weight_ref, delta_ref, weight_sems, chunk_sems, delta_sem = refs[-5:]
    depth = weight_ref.shape[0] // halves
    size = chunk_refs[0].shape[0]
    col = lax.axis_index("col")
    loads, chunks = [], []
    for h in range(halves):
        part = pl.ds(h * depth, depth)
        loads.append(pltpu.make_async_copy(weight_hbm.at[part, :], weight_ref.at[part, :], weight_sems.at[h]))
    for k in range(per_row):
        start = pl.multiple_of(lax.rem(col + k, per_row) * size, size)
        chunks.append(pltpu.make_async_copy(cot_hbm.at[pl.ds(start, size), :], chunk_refs[k], chunk_sems.at[k]))
    delta_load = pltpu.make_async_copy(delta_hbm, delta_ref, delta_sem)
    for copy in loads + chunks + [delta_load]:
        copy.start()
    for h in range(halves):
        loads[h].wait()
        part = pl.ds(h * depth, depth)
        low = weight_ref[part, :].astype(jnp.bfloat16)
        half_refs[h][...] = low
        whole_ref[part, :] = low
    delta_load.wait()
    low_ref[...] = delta_ref[...].astype(jnp.bfloat16)
    for copy in chunks:
        copy.wait()


def prepare(weight, cotangent, delta, per_row, halves):
    depth, width = weight.shape
    chunk = cotangent.shape[0] // per_row
    shape = lambda *s: jax.ShapeDtypeStruct(s, jnp.bfloat16)
    outs = [shape(depth // halves, width)] * halves + [shape(depth, width), shape(*delta.shape)] + [shape(chunk, width)] * per_row
    got = pl.pallas_call(
        functools.partial(prepare_kernel, per_row, halves),
        out_shape=outs,
        in_specs=[HBM] * 3,
        out_specs=[WHOLE] * len(outs),
        scratch_shapes=[
            pltpu.VMEM((depth, width), jnp.float32),
            pltpu.VMEM(delta.shape, jnp.float32),
            pltpu.SemaphoreType.DMA((halves,)),
            pltpu.SemaphoreType.DMA((per_row,)),
            pltpu.SemaphoreType.DMA,
        ],
        compiler_params=params(16),
        cost_estimate=pl.CostEstimate(flops=0, bytes_accessed=8 * weight.size, transcendentals=0),
        name="prepare",
    )(in_hbm(weight), in_hbm(cotangent), in_hbm(delta))
    return got[:halves], got[halves], got[halves + 1], got[halves + 2:]


def inner_kernel(rows, per_row, steps, *refs):
    tokens_hbm, weight_hbm, first_hbm, second_hbm, cot_hbm, low_weight_ref = refs[:6]
    cot_refs = refs[6:5 + rows]
    block_refs = refs[5 + rows:5 + rows + per_row]
    outs = refs[5 + rows + per_row:]
    new_weight_hbm, new_first_hbm, new_second_hbm, own_ref = outs[:4]
    message_refs = outs[4:3 + rows]
    tokens_ref, state_ref, fresh_ref, cot_ref, total_ref, turned_ref, sems, out_sems, cot_sem = refs[-9:]
    row = lax.axis_index("row")
    part = cot_ref.shape[0]
    tile = tokens_ref.shape[1] // steps
    block = [pl.ds(s * tile, tile) for s in range(steps)]
    states = (weight_hbm, first_hbm, second_hbm)
    fresh = (new_weight_hbm, new_first_hbm, new_second_hbm)

    cot_load = pltpu.make_async_copy(cot_hbm, cot_ref, cot_sem)
    token_loads, state_loads, stores = [], [], []
    for s in range(steps):
        token_loads.append(pltpu.make_async_copy(tokens_hbm.at[:, block[s]], tokens_ref.at[:, block[s]], sems.at[s, 3]))
        state_loads.append([
            pltpu.make_async_copy(state.at[block[s], :], state_ref.at[i, block[s], :], sems.at[s, i])
            for i, state in enumerate(states)
        ])
        stores.append([
            pltpu.make_async_copy(fresh_ref.at[i, block[s], :], out.at[block[s], :], out_sems.at[s, i])
            for i, out in enumerate(fresh)
        ])
    cot_load.start()
    for s in range(steps):
        token_loads[s].start()
        for load in state_loads[s]:
            load.start()

    size = block_refs[0].shape[0]
    for message_ref in message_refs:
        for k in range(per_row):
            message_ref[pl.ds(k * size, size), :] = block_refs[k][...]
    for k in range(1, rows):
        start = pl.multiple_of(mod(row - k, rows) * part, part)
        turned_ref[:, pl.ds(start, part)] = cot_refs[k - 1][...].T
    cot_load.wait()
    turned_ref[:, pl.ds(pl.multiple_of(row * part, part), part)] = cot_ref[...].T

    for s in range(steps):
        token_loads[s].wait()
        tokens = tokens_ref[:, block[s]]
        product = jnp.dot(tokens, low_weight_ref[block[s], :], preferred_element_type=jnp.float32)
        if s == 0:
            total_ref[...] = product
        else:
            total_ref[...] += product
        gradient = jnp.dot(turned_ref[...], tokens, preferred_element_type=jnp.float32).T
        for load in state_loads[s]:
            load.wait()
        weight = state_ref[0, block[s], :]
        first = BETA_ONE * state_ref[1, block[s], :] + (1.0 - BETA_ONE) * gradient
        second = BETA_TWO * state_ref[2, block[s], :] + (1.0 - BETA_TWO) * gradient * gradient
        fresh_ref[0, block[s], :] = weight - INNER_RATE * (
            first / (jnp.sqrt(second) + EPSILON) + WEIGHT_DECAY * weight
        )
        fresh_ref[1, block[s], :] = first
        fresh_ref[2, block[s], :] = second
        for store in stores[s]:
            store.start()

    own_ref[...] = total_ref[pl.ds(pl.multiple_of(row * part, part), part), :]
    for k in range(1, rows):
        start = pl.multiple_of(mod(row + k - rows, rows) * part, part)
        message_refs[k - 1][pl.ds(part, part), :] = total_ref[pl.ds(start, part), :].astype(jnp.bfloat16)
    for s in range(steps):
        for store in stores[s]:
            store.wait()


def inner(tokens, weight, first, second, cots, low_weight, blocks):
    rows, per_row = len(cots), len(blocks)
    count, depth = tokens.shape
    width = weight.shape[1]
    part = count // rows
    steps = depth // min(512, depth)
    full = jax.ShapeDtypeStruct((depth, width), jnp.float32)
    outs = [
        full,
        full,
        full,
        jax.ShapeDtypeStruct((part, width), jnp.float32),
    ] + [jax.ShapeDtypeStruct((2 * part, width), jnp.bfloat16)] * (rows - 1)
    got = pl.pallas_call(
        functools.partial(inner_kernel, rows, per_row, steps),
        in_specs=[HBM] * 5 + [WHOLE] * (rows + per_row),
        out_specs=[HBM] * 3 + [WHOLE] * rows,
        out_shape=outs,
        scratch_shapes=[
            pltpu.VMEM((count, depth), jnp.bfloat16),
            pltpu.VMEM((3, depth, width), jnp.float32),
            pltpu.VMEM((3, depth, width), jnp.float32),
            pltpu.VMEM((part, width), jnp.bfloat16),
            pltpu.VMEM((count, width), jnp.float32),
            pltpu.VMEM((width, count), jnp.bfloat16),
            pltpu.SemaphoreType.DMA((steps, 4)),
            pltpu.SemaphoreType.DMA((steps, 3)),
            pltpu.SemaphoreType.DMA,
        ],
        compiler_params=params(24),
        cost_estimate=pl.CostEstimate(
            flops=4 * count * depth * width, bytes_accessed=2 * count * depth + 24 * depth * width, transcendentals=0
        ),
        name="inner",
    )(*map(in_hbm, (tokens, weight, first, second, cots[0])), low_weight, *cots[1:], *blocks)
    return got[:3], got[3], got[4:]


def input_grad_kernel(rows, cols, *refs):
    per_row = cols // rows
    cot_refs, weight_refs = refs[:cols], refs[cols:2 * cols]
    out_ref, blocks_ref = refs[-2], refs[-1]
    row, col = lax.axis_index("row"), lax.axis_index("col")

    @pl.when(pl.program_id(0) == 0)
    def _():
        for j in range(rows):
            for k in range(per_row):
                block = mod(row - j, rows) * per_row + mod(lax.rem(col, per_row) - k, per_row)
                blocks_ref[block] = cot_refs[j * per_row + k][...]

    total = None
    pair = 2 if cols % 2 == 0 else 1
    for k in range(0, cols, pair):
        left = [blocks_ref[owner_of(col, k + i, cols)] for i in range(pair)]
        right = [weight_refs[k + i][...] for i in range(pair)]
        if pair > 1:
            left, right = [jnp.concatenate(left, axis=1)], [jnp.concatenate(right, axis=1)]
        piece = lax.dot_general(left[0], right[0], (((1,), (1,)), ((), ())), preferred_element_type=jnp.float32)
        total = piece if total is None else total + piece
    out_ref[...] = total.astype(jnp.bfloat16)


def input_grad_part(blocks, messages, weights, depth, half, before):
    per_row, rows, cols = len(blocks), len(messages) + 1, len(weights)
    chunk, width = blocks[0].shape
    tile = min(512, depth)
    steps = depth // tile
    aliased = [] if before is None else [before]
    in_specs, operands = [], []
    for source in [None] + list(messages):
        for k in range(per_row):
            in_specs.append(pl.BlockSpec((chunk, width), functools.partial(lambda k, d: (k, 0), 0 if source is None else k)))
            operands.append(blocks[k] if source is None else source)
    for array, part in weights:
        in_specs.append(pl.BlockSpec((tile, width), functools.partial(lambda first, d: (first + d, 0), part * steps)))
        operands.append(array)
    return pl.pallas_call(
        functools.partial(input_grad_kernel, rows, cols),
        grid=(steps,),
        in_specs=in_specs + [pl.BlockSpec(memory_space=pl.ANY)] * len(aliased),
        out_specs=pl.BlockSpec((chunk, tile), lambda d: (0, half * steps + d)),
        out_shape=jax.ShapeDtypeStruct((chunk, HALVES * depth), jnp.bfloat16),
        scratch_shapes=[pltpu.VMEM((cols, chunk, width), jnp.bfloat16)],
        input_output_aliases={2 * cols: 0} if aliased else {},
        compiler_params=params(16),
        cost_estimate=pl.CostEstimate(
            flops=2 * chunk * depth * width * cols, bytes_accessed=2 * (depth + chunk) * width * cols + 2 * chunk * depth,
            transcendentals=0,
        ),
        name="input_grad",
    )(*operands, *aliased)


def merge_kernel(replicas, slot_ref, sum_ref, other_ref, global_hbm, moment_hbm, new_global_hbm, new_outer_hbm, *scratch):
    global_ref, moment_ref, new_global_ref, new_outer_ref, sems = scratch
    slot = slot_ref[0]
    count = sum_ref.shape[0]
    slots = global_ref.shape[0] // count
    loads = [
        pltpu.make_async_copy(moment_hbm, moment_ref, sems.at[0]),
        pltpu.make_async_copy(global_hbm, global_ref, sems.at[1]),
    ]
    stores = [
        pltpu.make_async_copy(new_outer_ref, new_outer_hbm, sems.at[2]),
        pltpu.make_async_copy(new_global_ref, new_global_hbm, sems.at[3]),
    ]
    for load in loads:
        load.start()
    average = (sum_ref[...].astype(jnp.float32) + other_ref[...].astype(jnp.float32)) / replicas
    loads[0].wait()
    new_outer = NESTEROV * moment_ref[pl.ds(slot, count, stride=slots), :] + average
    new_outer_ref[...] = new_outer
    stores[0].start()
    loads[1].wait()
    held = global_ref[pl.ds(slot, count, stride=slots), :]
    new_global_ref[...] = held - OUTER_RATE * (average + NESTEROV * new_outer)
    stores[1].start()
    for store in stores:
        store.wait()


def interleaved(x):
    slots, size = x.shape
    return x.reshape(slots, size // LANES, LANES).transpose(1, 0, 2).reshape(slots * size // LANES, LANES)


def outer_sums(low, axis):
    n = lax.axis_size(axis)
    if not is_power_of_two(n):
        return lax.psum(low, axis), jnp.zeros_like(low)
    bit = 1
    while True:
        other = lax.ppermute(low, axis, swap_pairs(n, bit))
        bit *= 2
        if bit >= n:
            return low, other
        low = (low.astype(jnp.float32) + other.astype(jnp.float32)).astype(jnp.bfloat16)


def merge(low, other, global_params, outer_moment, group_slot, replicas):
    shape = jax.ShapeDtypeStruct(low.shape, jnp.float32)
    new_global, new_outer = pl.pallas_call(
        functools.partial(merge_kernel, replicas),
        out_shape=[shape, shape],
        in_specs=[pl.BlockSpec(memory_space=pltpu.SMEM)] + [WHOLE] * 2 + [HBM] * 2,
        out_specs=[HBM] * 2,
        scratch_shapes=[pltpu.VMEM((global_params.size // LANES, LANES), jnp.float32)] * 2
        + [pltpu.VMEM(low.shape, jnp.float32)] * 2
        + [pltpu.SemaphoreType.DMA((4,))],
        compiler_params=params(16),
        cost_estimate=pl.CostEstimate(flops=8 * low.size, bytes_accessed=28 * low.size, transcendentals=0),
        name="merge",
    )(group_slot, low, other, in_hbm(interleaved(global_params)), in_hbm(interleaved(outer_moment)))
    return new_global.reshape(-1), new_outer.reshape(-1)


def on_device(
    tokens,
    cotangent,
    weight,
    first_moment,
    second_moment,
    outer_delta,
    global_params,
    outer_moment,
    group_slot,
):
    rows, cols = lax.axis_size("row"), lax.axis_size("col")
    replicas = lax.axis_size("rep")
    per_row = cols // rows
    depth = weight.shape[1] // HALVES
    cots = shifted(cotangent, "row")
    halves, whole, low, chunks = prepare(weight[0], cotangent, outer_delta.reshape(-1, LANES), per_row, HALVES)
    received = [lax.ppermute(chunks[k], ("row", "col"), chunk_pairs(rows, cols, per_row, k)) for k in range(per_row)]
    weights = gather_halves(halves, whole, "col")

    (new_weight, new_first, new_second), own, messages = inner(
        tokens, weight[0], first_moment[0], second_moment[0], cots, whole, received
    )
    messages = [lax.ppermute(m, "row", shift_pairs(rows, k + 1)) for k, m in enumerate(messages)]
    low, received = after(low, received)
    low, other = outer_sums(low, "rep")
    new_global, new_outer = merge(low, other, global_params, outer_moment, group_slot, replicas)

    keys_values = own
    for message in messages:
        keys_values += message[own.shape[0]:].astype(jnp.float32)
    keys_values = keys_values.astype(jnp.bfloat16)

    input_grad = None
    for half in range(HALVES):
        input_grad = input_grad_part(received, messages, weights[half], depth, half, input_grad)
    return (keys_values, input_grad, new_weight[None], new_first[None], new_second[None], new_global, new_outer)


def solution(mesh):
    in_specs = (
        P("rep", "row"),
        P(("rep", "row"), "col"),
        P("rep", "row", "col"),
        P("rep", "row", "col"),
        P("rep", "row", "col"),
        P("rep", ("row", "col")),
        P(None, ("row", "col")),
        P(None, ("row", "col")),
        P(),
    )
    out_specs = (
        P(("rep", "row"), "col"),
        P(("rep", "col"), "row"),
        P("rep", "row", "col"),
        P("rep", "row", "col"),
        P("rep", "row", "col"),
        P(("row", "col")),
        P(("row", "col")),
    )
    return jax.shard_map(
        on_device, mesh=mesh, in_specs=in_specs, out_specs=out_specs, check_vma=False
    )
```

time: 98.6 us -> 60.8 us (0.62)
  other arithmetic: 21.1 us -> 0.81 us
  matrix products: 17.5 us -> 0 us
  Pallas kernels: 0 us -> 17.4 us
  between operations: 16.2 us -> 1.34 us
  starting transfers between devices: 6.13 us -> 18 us
  waiting for transfers between devices: 30.4 us -> 23.1 us
  blocking collectives: 3.98 us -> 0 us
  local copies, waits for them, and re-layouts: 2.94 us -> 0.01 us
    ppermute x0 -> x11, waiting for transfers between devices: none -> 23.1 us  [the longest x2 13 us: gather_halves(): have[h][bit] = (lax.ppermute(half, axis, swap_pairs(n, bit)), 0)]
    ppermute x0 -> x11, starting transfers between devices: none -> 18 us  [the longest x2 6.9 us: gather_halves(): have[h][bit] = (lax.ppermute(half, axis, swap_pairs(n, bit)), 0)]
    psum x1 -> x0, waiting for transfers between devices: 17.9 us -> none  [outer_step(): lax.psum(outer_delta[0].astype(jnp.bfloat16), 'rep').astype(jnp.float32)]
    dot_general x3 -> x0, matrix products: 17.5 us -> none  [the longest x1 7.41 us: inner_step(): jnp.einsum('td,tc->dc', tokens, cot_full, preferred_element_type=jnp.floa...]
    pallas_call x0 -> x5, Pallas kernels: none -> 17.4 us  [the longest x1 9.9 us: inner(): pl.pallas_call(functools.partial(inner_kernel, rows, per_row, steps), in_...]
    all_gather x1 -> x0, waiting for transfers between devices: 12.5 us -> none  [inner_step(): weight_all = lax.all_gather(weight_bf, 'col', axis=1, tiled=True)]
    convert_element_type x2, other arithmetic: 10.6 us -> 0.81 us  [the longest x1 0.72 us: on_device(): keys_values = keys_values.astype(jnp.bfloat16)]
    all_to_all x1 -> x0, starting transfers between devices: 6.04 us -> none  [inner_step(): lax.all_to_all(cot_full, 'col', split_axis=0, concat_axis=1, tiled=True)]
  transfers between devices with their start and end apart: 4 -> 11, of which waited for: 2 -> 3; matrix products, arithmetic and copies ran while one was open for 34% -> 1% of each run, Pallas kernels for 0% -> 22%
where the time goes in v2:
time: 60.8 us; the launch traced here: 60.6 us
  waiting for transfers between devices  23.1 us (38%)
  starting transfers between devices  18 us (30%)
  Pallas kernels  17.4 us (29%)
  between operations  1.34 us (2%)
  other arithmetic  0.81 us (1%)
    ppermute x2, waiting for transfers between devices, gather_halves(): have[h][bit] = (lax.ppermute(half, axis, swap_pairs(n, bit)), 0)  13 us
    ppermute x2, waiting for transfers between devices, gather_halves(): lax.ppermute(have[h][k][0], axis, swap_pairs(n, bit))  10.1 us
    pallas_call x1, Pallas kernels, inner(): pl.pallas_call(functools.partial(inner_kernel, rows, per_row, steps), in_...  9.9 us
    ppermute x2, starting transfers between devices, gather_halves(): have[h][bit] = (lax.ppermute(half, axis, swap_pairs(n, bit)), 0)  6.9 us
    ppermute x2, starting transfers between devices, on_device(): lax.ppermute(chunks[k], ('row', 'col'), chunk_pairs(rows, cols, per_row, k))  3.76 us
    ppermute x1, starting transfers between devices, shifted(): lax.ppermute(block, axis, shift_pairs(n, k))  3.39 us
    pallas_call x2, Pallas kernels, input_grad_part(): pl.pallas_call(functools.partial(input_grad_kernel, rows, cols), grid=(st...  3.23 us
    ppermute x2, starting transfers between devices, outer_sums(): other = lax.ppermute(low, axis, swap_pairs(n, bit))  3.08 us
  transfers between devices with their start and end apart: 11, of which 3 were waited for; matrix products, arithmetic and copies ran while one was open for 1% of the time, Pallas kernels for 22%

profile of v2, /device:TPU:0, one launch (start us, length us, event | category | flops | bytes accessed | tf_op | source)
XLA Modules:
  0.0 60.6 jit_solution(7126412593992994584)
XLA Ops:
  0.6 0.0 copy-start
  0.6 1.5 %prepare.1 = (bf16[1024,128]{1,0:T(8,128)(2,1)S(1)}, bf16[1024,128]{1,0:T(8,128)(2,1)S(1)}, bf16[2048,128]{1,0:T(8,128)(2,1)S(1)}, bf16[1280,128]{1,0:T(8,128)(2...) custom-call(f32[2048,128]{1,0:T(8,128)} %bitcast.19, bf16[768,128]{1,0:T(8,128)(2,1)} %refs_4_.1, ...), custom_call_target="tpu_custom_call" | custom-call | bytes 2097152 | tf_op jit(solution)/shard_map/prepare/pallas_call | solution.py:130
  2.2 0.7 %collective-permute-start.1 = (bf16[384,128]{1,0:T(8,128)(2,1)S(1)}, bf16[384,128]{1,0:T(8,128)(2,1)S(1)}, u32[]{:S(2)}, u32[]{:S(2)}) collective-permute-start(bf16[384,128]{1,0:T(8,128)(2,1)S(1)} %get-tuple-element.24), channel_id=1, source_target_pairs={{0,0},{1,1},{2,4},{3,5},{4,2},{5,3},{6,6},{7,7},{8,8},{9,9},{10,12... | collective-permute-start | bytes 294920 | tf_op jit(solution)/shard_map/ppermute | solution.py:397
  2.9 3.1 %collective-permute-start.2 = (bf16[384,128]{1,0:T(8,128)(2,1)S(1)}, bf16[384,128]{1,0:T(8,128)(2,1)S(1)}, u32[]{:S(2)}, u32[]{:S(2)}) collective-permute-start(bf16[384,128]{1,0:T(8,128)(2,1)S(1)} %get-tuple-element.25), channel_id=1, source_target_pairs={{0,1},{1,0},{2,5},{3,4},{4,3},{5,2},{6,7},{7,6},{8,9},{9,8},{10,13... | collective-permute-start | bytes 294920 | tf_op jit(solution)/shard_map/ppermute | solution.py:397
  5.9 0.0 copy-done
  5.9 3.4 %collective-permute-start = (bf16[768,128]{1,0:T(8,128)(2,1)S(1)}, bf16[768,128]{1,0:T(8,128)(2,1)S(1)}, u32[]{:S(2)}, u32[]{:S(2)}) collective-permute-start(bf16[768,128]{1,0:T(8,128)(2,1)S(1)} %copy-done), channel_id=1, source_target_pairs={{0,4},{4,0},{1,5},{5,1},{2,6},{6,2},{3,7},{7,3},{8,12},{12,8},{9,1... | collective-permute-start | bytes 589832 | tf_op jit(solution)/shard_map/ppermute | solution.py:85
  9.3 0.0 collective-permute-done.1.refs_7_.refs_0_
  9.3 0.0 collective-permute-done.2.refs_8_.refs_1_
  9.3 1.5 %collective-permute-start.9 = (bf16[1280,128]{1,0:T(8,128)(2,1)S(1)}, bf16[1280,128]{1,0:T(8,128)(2,1)S(1)}, u32[]{:S(2)}, u32[]{:S(2)}) collective-permute-start(bf16[1280,128]{1,0:T(8,128)(2,1)S(1)} %get-tuple-element.36), channel_id=1, source_target_pairs={{0,8},{8,0},{16,24},{24,16},{1,9},{9,1},{17,25},{25,17},{2,10},{10... | collective-permute-start | bytes 983048 | tf_op jit(solution)/shard_map/ppermute | solution.py:356
  10.8 6.9 %collective-permute-start.5 = (bf16[1024,128]{1,0:T(8,128)(2,1)S(1)}, bf16[1024,128]{1,0:T(8,128)(2,1)S(1)}, u32[]{:S(2)}, u32[]{:S(2)}) collective-permute-start(bf16[1024,128]{1,0:T(8,128)(2,1)S(1)} %get-tuple-element.31), channel_id=1, source_target_pairs={{0,2},{1,3},{2,0},{3,1},{4,6},{5,7},{6,4},{7,5},{8,10},{9,11},{10,... | collective-permute-start | bytes 786440 | tf_op jit(solution)/shard_map/ppermute | solution.py:59
  17.7 0.0 collective-permute-start.7
  17.7 0.4 collective-permute-start.4
  18.1 0.0 collective-permute-done.refs_6_
  18.2 9.9 %inner.1 = (f32[2048,128]{1,0:T(8,128)}, f32[2048,128]{1,0:T(8,128)}, f32[2048,128]{1,0:T(8,128)}, f32[768,128]{1,0:T(8,128)S(1)}, bf16[1536,128]{1,0:T(8,128)(2,1)S(1)}) custom-call(bf16[1536,2048]{1,0:T(8,128)(2,1)} %refs_0_.1, f32[2048,128]{1,0:T(8,128)} %bitcast.20, f32[2048,128]{1,0:T(8,128)} %bitcast.23, f32[2048,128]{1,0:T(8,128)} %bitcast.24, ...), custom_call_target="tpu_custom_call" | custom-call | flops 1610612736 | bytes 12582912 | tf_op jit(solution)/shard_map/inner/pallas_call | solution.py:236
  28.1 0.5 collective-permute-start.3
  28.6 7.6 %collective-permute-done.5.refs_6_ = bf16[1024,128]{1,0:T(8,128)(2,1)S(1)} collective-permute-done((bf16[1024,128]{1,0:T(8,128)(2,1)S(1)}, bf16[1024,128]{1,0:T(8,128)(2,1)S(1)}, u32[]{:S(2)}, u32[]{:S(2)}) %collective-permute-start.5) | collective-permute-done | bytes 262176 | tf_op jit(solution)/shard_map/ppermute | solution.py:59
  36.1 0.0 collective-permute-start.6
  36.1 5.4 %collective-permute-done.7.refs_6_ = bf16[1024,128]{1,0:T(8,128)(2,1)S(1)} collective-permute-done((bf16[1024,128]{1,0:T(8,128)(2,1)S(1)}, bf16[1024,128]{1,0:T(8,128)(2,1)S(1)}, u32[]{:S(2)}, u32[]{:S(2)}) %collective-permute-start.7) | collective-permute-done | bytes 262176 | tf_op jit(solution)/shard_map/ppermute | solution.py:59
  41.5 0.0 collective-permute-start.8
  41.5 0.0 collective-permute-done.9
  41.5 0.1 add_convert_fusion.sum_ref
  41.6 1.6 %collective-permute-start.10 = (bf16[1280,128]{1,0:T(8,128)(2,1)S(1)}, bf16[1280,128]{1,0:T(8,128)(2,1)S(1)}, u32[]{:S(2)}, u32[]{:S(2)}) collective-permute-start(bf16[1280,128]{1,0:T(8,128)(2,1)S(1)} %add_convert_fusion.sum_ref), channel_id=1, source_target_pairs={{0,16},{8,24},{16,0},{24,8},{1,17},{9,25},{17,1},{25,9},{2,18},{10... | collective-permute-start | bytes 983048 | tf_op jit(solution)/shard_map/ppermute | solution.py:356
  43.9 0.0 collective-permute-done.4.refs_5_
  43.9 10.1 %collective-permute-done.8.refs_7_ = bf16[1024,128]{1,0:T(8,128)(2,1)S(1)} collective-permute-done((bf16[1024,128]{1,0:T(8,128)(2,1)S(1)}, bf16[1024,128]{1,0:T(8,128)(2,1)S(1)}, u32[]{:S(2)}, u32[]{:S(2)}) %collective-permute-start.8) | collective-permute-done | bytes 262176 | tf_op jit(solution)/shard_map/ppermute | solution.py:65
  53.9 0.0 collective-permute-done.3.refs_2_.refs_3_
  53.9 1.6 %input_grad.2.refs_8_ = bf16[384,2048]{1,0:T(8,128)(2,1)} custom-call(bf16[384,128]{1,0:T(8,128)(2,1)S(1)} %collective-permute-done.1.refs_7_.refs_0_, bf16[384,128]{1,0:T(8,128)(2,1)S(1)} %collective-permute-done.2.refs_8_.refs_1_, bf16[1536,128]{1,0:T(8,128)(2,1)S(1)} %collective-permute-done.3.refs_2_.refs_3_, ...), custom_call_target="tpu_custom_call" | custom-call | flops 402653184 | bytes 2228224 | tf_op jit(solution)/shard_map/input_grad/pallas_call | solution.py:300
  55.6 0.0 collective-permute-done.6.refs_7_
  55.6 1.6 %input_grad.3 = bf16[384,2048]{1,0:T(8,128)(2,1)} custom-call(bf16[384,128]{1,0:T(8,128)(2,1)S(1)} %collective-permute-done.1.refs_7_.refs_0_, bf16[384,128]{1,0:T(8,128)(2,1)S(1)} %collective-permute-done.2.refs_8_.refs_1_, bf16[1536,128]{1,0:T(8,128)(2,1)S(1)} %collective-permute-done.3.refs_2_.refs_3_, ...), custom_call_target="tpu_custom_call", output_to_operand_aliasing={{}: (8, {})} | custom-call | flops 402653184 | bytes 2228224 | tf_op jit(solution)/shard_map/input_grad/pallas_call | solution.py:300
  57.2 0.7 %add_convert_fusion.1 = bf16[768,128]{1,0:T(8,128)(2,1)} fusion(f32[768,128]{1,0:T(8,128)S(1)} %get-tuple-element.26, bf16[1536,128]{1,0:T(8,128)(2,1)S(1)} %collective-permute-done.3.refs_2_.refs_3_), kind=kLoop, calls=%fused_computation.1 | loop fusion | flops 294912 | bytes 786432 | tf_op jit(solution)/shard_map/convert_element_type | solution.py:411
  57.9 0.0 collective-permute-done.10.other_ref
  57.9 2.7 %merge.1 = (f32[1280,128]{1,0:T(8,128)}, f32[1280,128]{1,0:T(8,128)}) custom-call(s32[1]{0:T(128)S(6)} %copy.20.slot_ref, bf16[1280,128]{1,0:T(8,128)(2,1)S(1)} %add_convert_fusion.sum_ref, bf16[1280,128]{1,0:T(8,128)(2,1)S(1)} %collective-permute-done.10.other_ref, f32[2560,128]{1,0:T(8,128)} %bitcast.21, f32[2560,128]{1,0:T(8,128)} %bitcast.22), custom_call_target="tpu_custom_call" | custom-call | flops 1310720 | bytes 4587520 | tf_op jit(solution)/shard_map/merge/pallas_call | solution.py:365
Async XLA Ops:
  0.6 5.3 %copy-start = (bf16[768,128]{1,0:T(8,128)(2,1)S(1)}, bf16[768,128]{1,0:T(8,128)(2,1)}, u32[]{:S(2)}) copy-start(bf16[768,128]{1,0:T(8,128)(2,1)} %refs_4_.1) | copy-start | bytes 589828
  2.2 7.2 %collective-permute-start.1 = (bf16[384,128]{1,0:T(8,128)(2,1)S(1)}, bf16[384,128]{1,0:T(8,128)(2,1)S(1)}, u32[]{:S(2)}, u32[]{:S(2)}) collective-permute-start(bf16[384,128]{1,0:T(8,128)(2,1)S(1)} %get-tuple-element.24), channel_id=1, source_target_pairs={{0,0},{1,1},{2,4},{3,5},{4,2},{5,3},{6,6},{7,7},{8,8},{9,9},{10,12... | collective-permute-start | bytes 294920 | tf_op jit(solution)/shard_map/ppermute | solution.py:397
  2.9 6.5 %collective-permute-start.2 = (bf16[384,128]{1,0:T(8,128)(2,1)S(1)}, bf16[384,128]{1,0:T(8,128)(2,1)S(1)}, u32[]{:S(2)}, u32[]{:S(2)}) collective-permute-start(bf16[384,128]{1,0:T(8,128)(2,1)S(1)} %get-tuple-element.25), channel_id=1, source_target_pairs={{0,1},{1,0},{2,5},{3,4},{4,3},{5,2},{6,7},{7,6},{8,9},{9,8},{10,13... | collective-permute-start | bytes 294920 | tf_op jit(solution)/shard_map/ppermute | solution.py:397
  5.9 12.2 %collective-permute-start = (bf16[768,128]{1,0:T(8,128)(2,1)S(1)}, bf16[768,128]{1,0:T(8,128)(2,1)S(1)}, u32[]{:S(2)}, u32[]{:S(2)}) collective-permute-start(bf16[768,128]{1,0:T(8,128)(2,1)S(1)} %copy-done), channel_id=1, source_target_pairs={{0,4},{4,0},{1,5},{5,1},{2,6},{6,2},{3,7},{7,3},{8,12},{12,8},{9,1... | collective-permute-start | bytes 589832 | tf_op jit(solution)/shard_map/ppermute | solution.py:85
  9.3 32.2 %collective-permute-start.9 = (bf16[1280,128]{1,0:T(8,128)(2,1)S(1)}, bf16[1280,128]{1,0:T(8,128)(2,1)S(1)}, u32[]{:S(2)}, u32[]{:S(2)}) collective-permute-start(bf16[1280,128]{1,0:T(8,128)(2,1)S(1)} %get-tuple-element.36), channel_id=1, source_target_pairs={{0,8},{8,0},{16,24},{24,16},{1,9},{9,1},{17,25},{25,17},{2,10},{10... | collective-permute-start | bytes 983048 | tf_op jit(solution)/shard_map/ppermute | solution.py:356
  10.8 25.3 %collective-permute-start.5 = (bf16[1024,128]{1,0:T(8,128)(2,1)S(1)}, bf16[1024,128]{1,0:T(8,128)(2,1)S(1)}, u32[]{:S(2)}, u32[]{:S(2)}) collective-permute-start(bf16[1024,128]{1,0:T(8,128)(2,1)S(1)} %get-tuple-element.31), channel_id=1, source_target_pairs={{0,2},{1,3},{2,0},{3,1},{4,6},{5,7},{6,4},{7,5},{8,10},{9,11},{10,... | collective-permute-start | bytes 786440 | tf_op jit(solution)/shard_map/ppermute | solution.py:59
  17.7 23.8 %collective-permute-start.7 = (bf16[1024,128]{1,0:T(8,128)(2,1)S(1)}, bf16[1024,128]{1,0:T(8,128)(2,1)S(1)}, u32[]{:S(2)}, u32[]{:S(2)}) collective-permute-start(bf16[1024,128]{1,0:T(8,128)(2,1)S(1)} %get-tuple-element.32), channel_id=1, source_target_pairs={{0,2},{1,3},{2,0},{3,1},{4,6},{5,7},{6,4},{7,5},{8,10},{9,11},{10,... | collective-permute-start | bytes 786440 | tf_op jit(solution)/shard_map/ppermute | solution.py:59
  17.7 26.1 %collective-permute-start.4 = (bf16[2048,128]{1,0:T(8,128)(2,1)S(1)}, bf16[2048,128]{1,0:T(8,128)(2,1)S(1)}, u32[]{:S(2)}, u32[]{:S(2)}) collective-permute-start(bf16[2048,128]{1,0:T(8,128)(2,1)S(1)} %get-tuple-element.23.refs_5_.refs_4_), channel_id=1, source_target_pairs={{0,1},{1,0},{2,3},{3,2},{4,5},{5,4},{6,7},{7,6},{8,9},{9,8},{10,11... | collective-permute-start | bytes 1572872 | tf_op jit(solution)/shard_map/ppermute | solution.py:62
  28.1 25.9 %collective-permute-start.3 = (bf16[1536,128]{1,0:T(8,128)(2,1)S(1)}, bf16[1536,128]{1,0:T(8,128)(2,1)S(1)}, u32[]{:S(2)}, u32[]{:S(2)}) collective-permute-start(bf16[1536,128]{1,0:T(8,128)(2,1)S(1)} %get-tuple-element.27), channel_id=1, source_target_pairs={{0,4},{4,0},{1,5},{5,1},{2,6},{6,2},{3,7},{7,3},{8,12},{12,8},{9,1... | collective-permute-start | bytes 1179656 | tf_op jit(solution)/shard_map/ppermute | solution.py:403
  36.1 19.4 %collective-permute-start.6 = (bf16[1024,128]{1,0:T(8,128)(2,1)S(1)}, bf16[1024,128]{1,0:T(8,128)(2,1)S(1)}, u32[]{:S(2)}, u32[]{:S(2)}) collective-permute-start(bf16[1024,128]{1,0:T(8,128)(2,1)S(1)} %collective-permute-done.5.refs_6_), channel_id=1, source_target_pairs={{0,1},{1,0},{2,3},{3,2},{4,5},{5,4},{6,7},{7,6},{8,9},{9,8},{10,11... | collective-permute-start | bytes 786440 | tf_op jit(solution)/shard_map/ppermute | solution.py:65
  41.5 12.4 %collective-permute-start.8 = (bf16[1024,128]{1,0:T(8,128)(2,1)S(1)}, bf16[1024,128]{1,0:T(8,128)(2,1)S(1)}, u32[]{:S(2)}, u32[]{:S(2)}) collective-permute-start(bf16[1024,128]{1,0:T(8,128)(2,1)S(1)} %collective-permute-done.7.refs_6_), channel_id=1, source_target_pairs={{0,1},{1,0},{2,3},{3,2},{4,5},{5,4},{6,7},{7,6},{8,9},{9,8},{10,11... | collective-permute-start | bytes 786440 | tf_op jit(solution)/shard_map/ppermute | solution.py:65
  41.6 16.3 %collective-permute-start.10 = (bf16[1280,128]{1,0:T(8,128)(2,1)S(1)}, bf16[1280,128]{1,0:T(8,128)(2,1)S(1)}, u32[]{:S(2)}, u32[]{:S(2)}) collective-permute-start(bf16[1280,128]{1,0:T(8,128)(2,1)S(1)} %add_convert_fusion.sum_ref), channel_id=1, source_target_pairs={{0,16},{8,24},{16,0},{24,8},{1,17},{9,25},{17,1},{25,9},{2,18},{10... | collective-permute-start | bytes 983048 | tf_op jit(solution)/shard_map/ppermute | solution.py:356

commit v3 on v2

v3 whole, which is shorter than its diff:
```python
import functools

import jax
import jax.numpy as jnp
from jax import lax
from jax.experimental import pallas as pl
from jax.experimental.pallas import tpu as pltpu
from jax.sharding import PartitionSpec as P

BETA_ONE = 0.9
BETA_TWO = 0.95
INNER_RATE = 0.0003
WEIGHT_DECAY = 0.1
EPSILON = 1e-08
OUTER_RATE = 0.7
NESTEROV = 0.9
LANES = 128

WHOLE = pl.BlockSpec(memory_space=pltpu.VMEM)
HBM = pl.BlockSpec(memory_space=pltpu.HBM)


def params(mebibytes):
    return pltpu.CompilerParams(vmem_limit_bytes=mebibytes * 1024 * 1024)


def after(x, others):
    return lax.optimization_barrier((x, others))


def in_hbm(x):
    return pltpu.with_memory_space_constraint(x, pltpu.HBM)


def is_power_of_two(n):
    return n & (n - 1) == 0


def swap_pairs(n, bit):
    return [(i, i ^ bit) for i in range(n)]


def shift_pairs(n, k):
    return [(i, (i + k) % n) for i in range(n)]


def mod(value, n):
    return lax.rem(value + n, n)


def gather_offsets(block, axis, early):
    n = lax.axis_size(axis)
    have = {0: block}
    if is_power_of_two(n):
        bit = n // 2
        while bit:
            for k in list(have):
                if k:
                    have[k], _ = after(have[k], (early, have[bit]))
                have[k ^ bit] = lax.ppermute(have[k], axis, swap_pairs(n, bit))
            bit //= 2
    else:
        for k in range(1, n):
            have[k] = lax.ppermute(have[k - 1], axis, shift_pairs(n, n - 1))
    return [have[k] for k in range(n)]


def owner_of(me, k, n):
    return me ^ k if is_power_of_two(n) else mod(me + k, n)


def shifted(block, axis):
    n = lax.axis_size(axis)
    return [block] + [lax.ppermute(block, axis, shift_pairs(n, k)) for k in range(1, n)]


def chunk_pairs(rows, cols, per_row, k):
    pairs = []
    for r in range(rows):
        for c in range(cols):
            pairs.append((r * cols + c, (c // per_row) * cols + r * per_row + (c + k) % per_row))
    return pairs


def prepare_kernel(per_row, weight_hbm, cot_hbm, delta_hbm, low_weight_ref, low_delta_ref, *refs):
    chunk_refs = refs[:per_row]
    weight_ref, delta_ref, sems, chunk_sems = refs[per_row:]
    size = chunk_refs[0].shape[0]
    col = lax.axis_index("col")
    loads = [
        pltpu.make_async_copy(weight_hbm, weight_ref, sems.at[0]),
        pltpu.make_async_copy(delta_hbm, delta_ref, sems.at[1]),
    ]
    chunks = []
    for k in range(per_row):
        start = pl.multiple_of(lax.rem(col + k, per_row) * size, size)
        chunks.append(pltpu.make_async_copy(cot_hbm.at[pl.ds(start, size), :], chunk_refs[k], chunk_sems.at[k]))
    for copy in loads + chunks:
        copy.start()
    loads[0].wait()
    low_weight_ref[...] = weight_ref[...].astype(jnp.bfloat16)
    loads[1].wait()
    low_delta_ref[...] = delta_ref[...].astype(jnp.bfloat16)
    for copy in chunks:
        copy.wait()


def prepare(weight, cotangent, delta, per_row):
    chunk = cotangent.shape[0] // per_row
    shape = lambda *s: jax.ShapeDtypeStruct(s, jnp.bfloat16)
    outs = [shape(*weight.shape), shape(*delta.shape)] + [shape(chunk, cotangent.shape[1])] * per_row
    got = pl.pallas_call(
        functools.partial(prepare_kernel, per_row),
        out_shape=outs,
        in_specs=[HBM] * 3,
        out_specs=[WHOLE] * len(outs),
        scratch_shapes=[
            pltpu.VMEM(weight.shape, jnp.float32),
            pltpu.VMEM(delta.shape, jnp.float32),
            pltpu.SemaphoreType.DMA((2,)),
            pltpu.SemaphoreType.DMA((per_row,)),
        ],
        compiler_params=params(16),
        cost_estimate=pl.CostEstimate(flops=0, bytes_accessed=8 * weight.size, transcendentals=0),
        name="prepare",
    )(*map(in_hbm, (weight, cotangent, delta)))
    return got[0], got[1], got[2:]


def pack_kernel(per_row, *refs):
    block_refs, sum_refs = refs[:per_row], refs[per_row:per_row + (len(refs) - per_row) // 2]
    out_refs = refs[per_row + len(sum_refs):]
    size, part = block_refs[0].shape[0], sum_refs[0].shape[0]
    for out_ref, sum_ref in zip(out_refs, sum_refs):
        for k in range(per_row):
            out_ref[pl.ds(k * size, size), :] = block_refs[k][...]
        out_ref[pl.ds(part, part), :] = sum_ref[...]


def pack(blocks, sends):
    part, width = sends[0].shape
    return pl.pallas_call(
        functools.partial(pack_kernel, len(blocks)),
        out_shape=[jax.ShapeDtypeStruct((2 * part, width), jnp.bfloat16)] * len(sends),
        in_specs=[WHOLE] * (len(blocks) + len(sends)),
        out_specs=[WHOLE] * len(sends),
        compiler_params=params(16),
        cost_estimate=pl.CostEstimate(flops=0, bytes_accessed=8 * part * width, transcendentals=0),
        name="pack",
    )(*blocks, *sends)


def inner_kernel(rows, steps, *refs):
    tokens_hbm, weight_hbm, first_hbm, second_hbm, cot_hbm, low_weight_ref = refs[:6]
    cot_refs = refs[6:5 + rows]
    new_weight_hbm, new_first_hbm, new_second_hbm, own_ref = refs[5 + rows:9 + rows]
    send_refs = refs[9 + rows:8 + 2 * rows]
    tokens_ref, state_ref, fresh_ref, cot_ref, total_ref, turned_ref, sems, out_sems, cot_sem = refs[-9:]
    row = lax.axis_index("row")
    part = cot_ref.shape[0]
    tile = tokens_ref.shape[1] // steps
    block = [pl.ds(s * tile, tile) for s in range(steps)]
    states = (weight_hbm, first_hbm, second_hbm)
    fresh = (new_weight_hbm, new_first_hbm, new_second_hbm)

    cot_load = pltpu.make_async_copy(cot_hbm, cot_ref, cot_sem)
    token_loads, state_loads, stores = [], [], []
    for s in range(steps):
        token_loads.append(pltpu.make_async_copy(tokens_hbm.at[:, block[s]], tokens_ref.at[:, block[s]], sems.at[s, 3]))
        state_loads.append([
            pltpu.make_async_copy(state.at[block[s], :], state_ref.at[i, block[s], :], sems.at[s, i])
            for i, state in enumerate(states)
        ])
        stores.append([
            pltpu.make_async_copy(fresh_ref.at[i, block[s], :], out.at[block[s], :], out_sems.at[s, i])
            for i, out in enumerate(fresh)
        ])
    cot_load.start()
    for s in range(steps):
        token_loads[s].start()
        for load in state_loads[s]:
            load.start()

    for k in range(1, rows):
        start = pl.multiple_of(mod(row - k, rows) * part, part)
        turned_ref[:, pl.ds(start, part)] = cot_refs[k - 1][...].T
    cot_load.wait()
    turned_ref[:, pl.ds(pl.multiple_of(row * part, part), part)] = cot_ref[...].T

    for s in range(steps):
        token_loads[s].wait()
        tokens = tokens_ref[:, block[s]]
        product = jnp.dot(tokens, low_weight_ref[block[s], :], preferred_element_type=jnp.float32)
        if s == 0:
            total_ref[...] = product
        else:
            total_ref[...] += product
        gradient = jnp.dot(turned_ref[...], tokens, preferred_element_type=jnp.float32).T
        for load in state_loads[s]:
            load.wait()
        weight = state_ref[0, block[s], :]
        first = BETA_ONE * state_ref[1, block[s], :] + (1.0 - BETA_ONE) * gradient
        second = BETA_TWO * state_ref[2, block[s], :] + (1.0 - BETA_TWO) * gradient * gradient
        fresh_ref[0, block[s], :] = weight - INNER_RATE * (
            first / (jnp.sqrt(second) + EPSILON) + WEIGHT_DECAY * weight
        )
        fresh_ref[1, block[s], :] = first
        fresh_ref[2, block[s], :] = second
        for store in stores[s]:
            store.start()

    own_ref[...] = total_ref[pl.ds(pl.multiple_of(row * part, part), part), :]
    for k in range(1, rows):
        start = pl.multiple_of(mod(row + k - rows, rows) * part, part)
        send_refs[k - 1][...] = total_ref[pl.ds(start, part), :].astype(jnp.bfloat16)
    for s in range(steps):
        for store in stores[s]:
            store.wait()


def inner(tokens, weight, first, second, cots, low_weight):
    rows = len(cots)
    count, depth = tokens.shape
    width = weight.shape[1]
    part = count // rows
    steps = depth // min(512, depth)
    full = jax.ShapeDtypeStruct((depth, width), jnp.float32)
    outs = [
        full,
        full,
        full,
        jax.ShapeDtypeStruct((part, width), jnp.float32),
    ] + [jax.ShapeDtypeStruct((part, width), jnp.bfloat16)] * (rows - 1)
    got = pl.pallas_call(
        functools.partial(inner_kernel, rows, steps),
        in_specs=[HBM] * 5 + [WHOLE] * rows,
        out_specs=[HBM] * 3 + [WHOLE] * rows,
        out_shape=outs,
        scratch_shapes=[
            pltpu.VMEM((count, depth), jnp.bfloat16),
            pltpu.VMEM((3, depth, width), jnp.float32),
            pltpu.VMEM((3, depth, width), jnp.float32),
            pltpu.VMEM((part, width), jnp.bfloat16),
            pltpu.VMEM((count, width), jnp.float32),
            pltpu.VMEM((width, count), jnp.bfloat16),
            pltpu.SemaphoreType.DMA((steps, 4)),
            pltpu.SemaphoreType.DMA((steps, 3)),
            pltpu.SemaphoreType.DMA,
        ],
        compiler_params=params(24),
        cost_estimate=pl.CostEstimate(
            flops=4 * count * depth * width, bytes_accessed=2 * count * depth + 24 * depth * width, transcendentals=0
        ),
        name="inner",
    )(*map(in_hbm, (tokens, weight, first, second, cots[0])), low_weight, *cots[1:])
    return got[:3], got[3], got[4:]


def times_transposed(left, right):
    return lax.dot_general(left, right, (((1,), (1,)), ((), ())), preferred_element_type=jnp.float32)


def arrived_kernel(rows, cols, tile, *refs):
    per_row = cols // rows
    block_refs, message_refs = refs[:per_row], refs[per_row:per_row + rows - 1]
    own_ref = refs[per_row + rows - 1]
    weight_refs = refs[per_row + rows:per_row + rows + cols - 1]
    sum_ref, last_ref, keys_values_hbm, blocks_ref, keys_values_ref, sem = refs[-6:]
    row, col = lax.axis_index("row"), lax.axis_index("col")
    size, part = block_refs[0].shape[0], own_ref.shape[0]
    total = own_ref[...]
    for message_ref in message_refs:
        total += message_ref[pl.ds(part, part), :].astype(jnp.float32)
    keys_values_ref[...] = total.astype(jnp.bfloat16)
    store = pltpu.make_async_copy(keys_values_ref, keys_values_hbm, sem)
    store.start()
    for k in range(per_row):
        column = mod(lax.rem(col, per_row) - k, per_row)
        blocks_ref[row * per_row + column] = block_refs[k][...]
        for j in range(1, rows):
            blocks_ref[mod(row - j, rows) * per_row + column] = message_refs[j - 1][pl.ds(k * size, size), :]
    last_ref[...] = blocks_ref[owner_of(col, cols - 1, cols)]
    left = [blocks_ref[owner_of(col, k, cols)] for k in range(cols - 1)]
    for start in range(0, weight_refs[0].shape[0], tile):
        features = pl.ds(start, tile)
        piece = None
        for k in range(0, cols - 1, 2):
            few = range(k, min(k + 2, cols - 1))
            product = times_transposed(
                jnp.concatenate([left[i] for i in few], axis=1),
                jnp.concatenate([weight_refs[i][features, :] for i in few], axis=1),
            )
            piece = product if piece is None else piece + product
        sum_ref[:, features] = piece
    store.wait()


def arrived(blocks, messages, own, weights, cols):
    rows, per_row = len(messages) + 1, len(blocks)
    size, width = blocks[0].shape
    depth = weights[0].shape[0]
    return pl.pallas_call(
        functools.partial(arrived_kernel, rows, cols, min(512, depth)),
        out_shape=[
            jax.ShapeDtypeStruct((size, depth), jnp.float32),
            jax.ShapeDtypeStruct((size, width), jnp.bfloat16),
            jax.ShapeDtypeStruct(own.shape, jnp.bfloat16),
        ],
        in_specs=[WHOLE] * (per_row + rows + cols - 1),
        out_specs=[WHOLE, WHOLE, HBM],
        scratch_shapes=[
            pltpu.VMEM((cols, size, width), jnp.bfloat16),
            pltpu.VMEM(own.shape, jnp.bfloat16),
            pltpu.SemaphoreType.DMA,
        ],
        compiler_params=params(24),
        cost_estimate=pl.CostEstimate(
            flops=2 * size * depth * width * (cols - 1), bytes_accessed=4 * size * depth, transcendentals=0
        ),
        name="arrived",
    )(*blocks, *messages, own, *weights)


def finish_kernel(tile, sum_ref, block_ref, weight_ref, out_hbm, out_ref, sems):
    stores = []
    for i, start in enumerate(range(0, weight_ref.shape[0], tile)):
        features = pl.ds(start, tile)
        piece = times_transposed(block_ref[...], weight_ref[features, :])
        out_ref[:, features] = (sum_ref[:, features] + piece).astype(jnp.bfloat16)
        stores.append(pltpu.make_async_copy(out_ref.at[:, features], out_hbm.at[:, features], sems.at[i]))
        stores[-1].start()
    for store in stores:
        store.wait()


def finish(total, block, weight):
    size, depth = total.shape
    tile = min(512, depth)
    return pl.pallas_call(
        functools.partial(finish_kernel, tile),
        out_shape=jax.ShapeDtypeStruct((size, depth), jnp.bfloat16),
        in_specs=[WHOLE] * 3,
        out_specs=HBM,
        scratch_shapes=[pltpu.VMEM((size, depth), jnp.bfloat16), pltpu.SemaphoreType.DMA((depth // tile,))],
        compiler_params=params(16),
        cost_estimate=pl.CostEstimate(
            flops=2 * size * depth * block.shape[1], bytes_accessed=6 * size * depth, transcendentals=0
        ),
        name="finish",
    )(total, block, weight)


def merge_kernel(replicas, slot_ref, sum_ref, other_ref, global_hbm, moment_hbm, new_global_hbm, new_outer_hbm, *scratch):
    global_ref, moment_ref, new_global_ref, new_outer_ref, sems = scratch
    slot = slot_ref[0]
    count = sum_ref.shape[0]
    slots = global_ref.shape[0] // count
    loads = [
        pltpu.make_async_copy(moment_hbm, moment_ref, sems.at[0]),
        pltpu.make_async_copy(global_hbm, global_ref, sems.at[1]),
    ]
    stores = [
        pltpu.make_async_copy(new_outer_ref, new_outer_hbm, sems.at[2]),
        pltpu.make_async_copy(new_global_ref, new_global_hbm, sems.at[3]),
    ]
    for load in loads:
        load.start()
    average = (sum_ref[...].astype(jnp.float32) + other_ref[...].astype(jnp.float32)) / replicas
    loads[0].wait()
    new_outer = NESTEROV * moment_ref[pl.ds(slot, count, stride=slots), :] + average
    new_outer_ref[...] = new_outer
    stores[0].start()
    loads[1].wait()
    held = global_ref[pl.ds(slot, count, stride=slots), :]
    new_global_ref[...] = held - OUTER_RATE * (average + NESTEROV * new_outer)
    stores[1].start()
    for store in stores:
        store.wait()


def interleaved(x):
    slots, size = x.shape
    return x.reshape(slots, size // LANES, LANES).transpose(1, 0, 2).reshape(slots * size // LANES, LANES)


def outer_sums(low, axis, early):
    n = lax.axis_size(axis)
    if not is_power_of_two(n):
        return lax.psum(low, axis), jnp.zeros_like(low)
    bit = 1
    while True:
        other = lax.ppermute(low, axis, swap_pairs(n, bit))
        bit *= 2
        if bit >= n:
            return low, other
        other, _ = after(other, early)
        low = (low.astype(jnp.float32) + other.astype(jnp.float32)).astype(jnp.bfloat16)


def merge(low, other, global_params, outer_moment, group_slot, replicas):
    shape = jax.ShapeDtypeStruct(low.shape, jnp.float32)
    new_global, new_outer = pl.pallas_call(
        functools.partial(merge_kernel, replicas),
        out_shape=[shape, shape],
        in_specs=[pl.BlockSpec(memory_space=pltpu.SMEM)] + [WHOLE] * 2 + [HBM] * 2,
        out_specs=[HBM] * 2,
        scratch_shapes=[pltpu.VMEM((global_params.size // LANES, LANES), jnp.float32)] * 2
        + [pltpu.VMEM(low.shape, jnp.float32)] * 2
        + [pltpu.SemaphoreType.DMA((4,))],
        compiler_params=params(16),
        cost_estimate=pl.CostEstimate(flops=8 * low.size, bytes_accessed=28 * low.size, transcendentals=0),
        name="merge",
    )(group_slot, low, other, in_hbm(interleaved(global_params)), in_hbm(interleaved(outer_moment)))
    return new_global.reshape(-1), new_outer.reshape(-1)


def on_device(
    tokens,
    cotangent,
    weight,
    first_moment,
    second_moment,
    outer_delta,
    global_params,
    outer_moment,
    group_slot,
):
    rows, cols = lax.axis_size("row"), lax.axis_size("col")
    replicas = lax.axis_size("rep")
    per_row = cols // rows
    cots = shifted(cotangent, "row")
    low_weight, low, chunks = prepare(weight[0], cotangent, outer_delta.reshape(-1, LANES), per_row)
    received = [lax.ppermute(chunks[k], ("row", "col"), chunk_pairs(rows, cols, per_row, k)) for k in range(per_row)]
    (new_weight, new_first, new_second), own, sends = inner(
        tokens, weight[0], first_moment[0], second_moment[0], cots, low_weight
    )
    weights = gather_offsets(low_weight, "col", sends)
    low, other = outer_sums(low, "rep", (sends, weights[1], weights[cols // 2]))
    received, _ = after(received, weights[cols // 2])
    messages = [lax.ppermute(m, "row", shift_pairs(rows, k + 1)) for k, m in enumerate(pack(received, sends))]
    total, block, keys_values = arrived(received, messages, own, weights[:-1], cols)
    other, _ = after(other, total)
    new_global, new_outer = merge(low, other, global_params, outer_moment, group_slot, replicas)
    last, _ = after(weights[-1], (new_outer, total))
    input_grad = finish(total, block, last)
    return (keys_values, input_grad, new_weight[None], new_first[None], new_second[None], new_global, new_outer)


def solution(mesh):
    in_specs = (
        P("rep", "row"),
        P(("rep", "row"), "col"),
        P("rep", "row", "col"),
        P("rep", "row", "col"),
        P("rep", "row", "col"),
        P("rep", ("row", "col")),
        P(None, ("row", "col")),
        P(None, ("row", "col")),
        P(),
    )
    out_specs = (
        P(("rep", "row"), "col"),
        P(("rep", "col"), "row"),
        P("rep", "row", "col"),
        P("rep", "row", "col"),
        P("rep", "row", "col"),
        P(("row", "col")),
        P(("row", "col")),
    )
    return jax.shard_map(
        on_device, mesh=mesh, in_specs=in_specs, out_specs=out_specs, check_vma=False
    )
```

time: 60.8 us -> 47.9 us (0.79)
  waiting for transfers between devices: 23.1 us -> 15.9 us
  starting transfers between devices: 18 us -> 12.9 us
  other arithmetic: 0.81 us -> 0.09 us
    ppermute x5 -> x3, waiting for transfers between devices: 23 us -> 10.2 us  [gather_offsets(): have[k ^ bit] = lax.ppermute(have[k], axis, swap_pairs(n, bit))]
    ppermute x2, waiting for transfers between devices: 0.01 us -> 5.74 us  [outer_sums(): other = lax.ppermute(low, axis, swap_pairs(n, bit))]
    ppermute x1, starting transfers between devices: 3.39 us -> 0.01 us  [shifted(): lax.ppermute(block, axis, shift_pairs(n, k))]
    ppermute x2, starting transfers between devices: 3.76 us -> 1.17 us  [on_device(): lax.ppermute(chunks[k], ('row', 'col'), chunk_pairs(rows, cols, per_row, k))]
    ppermute x1, starting transfers between devices: 0.49 us -> 1.32 us  [on_device(): lax.ppermute(m, 'row', shift_pairs(rows, k + 1))]
    convert_element_type x1 -> x0, other arithmetic: 0.72 us -> none  [on_device(): keys_values = keys_values.astype(jnp.bfloat16)]
    ppermute x5 -> x3, starting transfers between devices: 7.31 us -> 7.26 us  [gather_offsets(): have[k ^ bit] = lax.ppermute(have[k], axis, swap_pairs(n, bit))]
    pallas_call x4 -> x5, Pallas kernels: 14.7 us -> 14.7 us  [the longest x1 10.1 us: inner(): pl.pallas_call(functools.partial(inner_kernel, rows, steps), in_specs=[HB...]
  transfers between devices with their start and end apart: 11 -> 9, of which waited for: 3 -> 3; matrix products, arithmetic and copies ran while one was open for 1% -> 0% of each run, Pallas kernels for 22% -> 30%
where the time goes in v3:
time: 47.9 us; the launch traced here: 47.7 us
  Pallas kernels  17.4 us (36%)
  waiting for transfers between devices  15.9 us (33%)
  starting transfers between devices  12.9 us (27%)
  between operations  1.37 us (3%)
    ppermute x3, waiting for transfers between devices, gather_offsets(): have[k ^ bit] = lax.ppermute(have[k], axis, swap_pairs(n, bit))  10.2 us
    pallas_call x1, Pallas kernels, inner(): pl.pallas_call(functools.partial(inner_kernel, rows, steps), in_specs=[HB...  10.1 us
    ppermute x3, starting transfers between devices, gather_offsets(): have[k ^ bit] = lax.ppermute(have[k], axis, swap_pairs(n, bit))  7.26 us
    ppermute x2, waiting for transfers between devices, outer_sums(): other = lax.ppermute(low, axis, swap_pairs(n, bit))  5.74 us
    ppermute x2, starting transfers between devices, outer_sums(): other = lax.ppermute(low, axis, swap_pairs(n, bit))  3.11 us
    pallas_call x1, Pallas kernels, merge(): pl.pallas_call(functools.partial(merge_kernel, replicas), out_shape=[shap...  2.72 us
    pallas_call x1, Pallas kernels, arrived(): pl.pallas_call(functools.partial(arrived_kernel, rows, cols, min(512, dep...  1.67 us
    pallas_call x1, Pallas kernels, prepare(): pl.pallas_call(functools.partial(prepare_kernel, per_row), out_shape=outs...  1.52 us
  transfers between devices with their start and end apart: 9, of which 3 were waited for; matrix products, arithmetic and copies ran while one was open for 0% of the time, Pallas kernels for 30%

profile of v3, /device:TPU:0, one launch (start us, length us, event | category | flops | bytes accessed | tf_op | source)
XLA Modules:
  0.0 47.7 jit_solution(813836349707064609)
XLA Ops:
  0.6 0.0 copy-start
  0.6 1.5 %prepare.1 = (bf16[2048,128]{1,0:T(8,128)(2,1)S(1)}, bf16[1280,128]{1,0:T(8,128)(2,1)S(1)}, bf16[384,128]{1,0:T(8,128)(2,1)S(1)}, bf16[384,128]{1,0:T(8,128)(2,1)S(1)}) custom-call(f32[2048,128]{1,0:T(8,128)} %bitcast.19, bf16[768,128]{1,0:T(8,128)(2,1)} %refs_4_.1, f32[1280,128]{1,0:T(8,128)} %bitcast.25), custom_call_target="tpu_custom_call" | custom-call | bytes 2097152 | tf_op jit(solution)/shard_map/prepare/pallas_call | solution.py:112
  2.2 4.1 %collective-permute-start.2 = (bf16[2048,128]{1,0:T(8,128)(2,1)S(1)}, bf16[2048,128]{1,0:T(8,128)(2,1)S(1)}, u32[]{:S(2)}, u32[]{:S(2)}) collective-permute-start(bf16[2048,128]{1,0:T(8,128)(2,1)S(1)} %get-tuple-element.29.refs_5_.refs_4_), channel_id=1, source_target_pairs={{0,2},{1,3},{2,0},{3,1},{4,6},{5,7},{6,4},{7,5},{8,10},{9,11},{10,... | collective-permute-start | bytes 1572872 | tf_op jit(solution)/shard_map/ppermute | solution.py:60
  6.3 1.6 %collective-permute-start.4 = (bf16[2048,128]{1,0:T(8,128)(2,1)S(1)}, bf16[2048,128]{1,0:T(8,128)(2,1)S(1)}, u32[]{:S(2)}, u32[]{:S(2)}) collective-permute-start(bf16[2048,128]{1,0:T(8,128)(2,1)S(1)} %get-tuple-element.29.refs_5_.refs_4_), channel_id=1, source_target_pairs={{0,1},{1,0},{2,3},{3,2},{4,5},{5,4},{6,7},{7,6},{8,9},{9,8},{10,11... | collective-permute-start | bytes 1572872 | tf_op jit(solution)/shard_map/ppermute | solution.py:60
  7.8 0.0 copy-done
  7.8 0.0 collective-permute-start.3
  7.9 1.5 %collective-permute-start.7 = (bf16[1280,128]{1,0:T(8,128)(2,1)S(1)}, bf16[1280,128]{1,0:T(8,128)(2,1)S(1)}, u32[]{:S(2)}, u32[]{:S(2)}) collective-permute-start(bf16[1280,128]{1,0:T(8,128)(2,1)S(1)} %get-tuple-element.38), channel_id=1, source_target_pairs={{0,8},{8,0},{16,24},{24,16},{1,9},{9,1},{17,25},{25,17},{2,10},{10... | collective-permute-start | bytes 983048 | tf_op jit(solution)/shard_map/ppermute | solution.py:392
  9.3 0.7 %collective-permute-start = (bf16[384,128]{1,0:T(8,128)(2,1)S(1)}, bf16[384,128]{1,0:T(8,128)(2,1)S(1)}, u32[]{:S(2)}, u32[]{:S(2)}) collective-permute-start(bf16[384,128]{1,0:T(8,128)(2,1)S(1)} %get-tuple-element.27), channel_id=1, source_target_pairs={{0,0},{1,1},{2,4},{3,5},{4,2},{5,3},{6,6},{7,7},{8,8},{9,9},{10,12... | collective-permute-start | bytes 294920 | tf_op jit(solution)/shard_map/ppermute | solution.py:433
  10.0 0.0 collective-permute-done.3.refs_6_
  10.0 0.5 %collective-permute-start.1 = (bf16[384,128]{1,0:T(8,128)(2,1)S(1)}, bf16[384,128]{1,0:T(8,128)(2,1)S(1)}, u32[]{:S(2)}, u32[]{:S(2)}) collective-permute-start(bf16[384,128]{1,0:T(8,128)(2,1)S(1)} %get-tuple-element.28), channel_id=1, source_target_pairs={{0,1},{1,0},{2,5},{3,4},{4,3},{5,2},{6,7},{7,6},{8,9},{9,8},{10,13... | collective-permute-start | bytes 294920 | tf_op jit(solution)/shard_map/ppermute | solution.py:433
  10.5 10.1 %inner.1 = (f32[2048,128]{1,0:T(8,128)}, f32[2048,128]{1,0:T(8,128)}, f32[2048,128]{1,0:T(8,128)}, f32[768,128]{1,0:T(8,128)S(1)}, bf16[768,128]{1,0:T(8,128)(2,1)S(1)}) custom-call(bf16[1536,2048]{1,0:T(8,128)(2,1)} %refs_0_.1, f32[2048,128]{1,0:T(8,128)} %bitcast.20, f32[2048,128]{1,0:T(8,128)} %bitcast.23, f32[2048,128]{1,0:T(8,128)} %bitcast.24, ...), custom_call_target="tpu_custom_call" | custom-call | flops 1610612736 | bytes 12582912 | tf_op jit(solution)/shard_map/inner/pallas_call | solution.py:234
  20.6 8.9 %collective-permute-done.2.refs_6_ = bf16[2048,128]{1,0:T(8,128)(2,1)S(1)} collective-permute-done((bf16[2048,128]{1,0:T(8,128)(2,1)S(1)}, bf16[2048,128]{1,0:T(8,128)(2,1)S(1)}, u32[]{:S(2)}, u32[]{:S(2)}) %collective-permute-start.2) | collective-permute-done | bytes 524320 | tf_op jit(solution)/shard_map/ppermute | solution.py:60
  29.5 1.2 %collective-permute-done.4.refs_5_ = bf16[2048,128]{1,0:T(8,128)(2,1)S(1)} collective-permute-done((bf16[2048,128]{1,0:T(8,128)(2,1)S(1)}, bf16[2048,128]{1,0:T(8,128)(2,1)S(1)}, u32[]{:S(2)}, u32[]{:S(2)}) %collective-permute-start.4) | collective-permute-done | bytes 524320 | tf_op jit(solution)/shard_map/ppermute | solution.py:60
  30.8 1.6 %collective-permute-start.6 = (bf16[2048,128]{1,0:T(8,128)(2,1)S(1)}, bf16[2048,128]{1,0:T(8,128)(2,1)S(1)}, u32[]{:S(2)}, u32[]{:S(2)}) collective-permute-start(bf16[2048,128]{1,0:T(8,128)(2,1)S(1)} %collective-permute-done.2.refs_6_), channel_id=1, source_target_pairs={{0,1},{1,0},{2,3},{3,2},{4,5},{5,4},{6,7},{7,6},{8,9},{9,8},{10,11... | collective-permute-start | bytes 1572872 | tf_op jit(solution)/shard_map/ppermute | solution.py:60
  32.4 0.0 collective-permute-done.refs_0_
  32.4 0.0 collective-permute-done.1.refs_1_
  32.4 1.3 %collective-permute-start.5 = (bf16[1536,128]{1,0:T(8,128)(2,1)S(1)}, bf16[1536,128]{1,0:T(8,128)(2,1)S(1)}, u32[]{:S(2)}, u32[]{:S(2)}) collective-permute-start(bf16[1536,128]{1,0:T(8,128)(2,1)S(1)} %pack.1), channel_id=1, source_target_pairs={{0,4},{4,0},{1,5},{5,1},{2,6},{6,2},{3,7},{7,3},{8,12},{12,8},{9,1... | collective-permute-start | bytes 1179656 | tf_op jit(solution)/shard_map/ppermute | solution.py:440
  33.7 0.0 collective-permute-done.7
  33.7 0.1 add_convert_fusion.sum_ref
  33.8 1.6 %collective-permute-start.8 = (bf16[1280,128]{1,0:T(8,128)(2,1)S(1)}, bf16[1280,128]{1,0:T(8,128)(2,1)S(1)}, u32[]{:S(2)}, u32[]{:S(2)}) collective-permute-start(bf16[1280,128]{1,0:T(8,128)(2,1)S(1)} %add_convert_fusion.sum_ref), channel_id=1, source_target_pairs={{0,16},{8,24},{16,0},{24,8},{1,17},{9,25},{17,1},{25,9},{2,18},{10... | collective-permute-start | bytes 983048 | tf_op jit(solution)/shard_map/ppermute | solution.py:392
  36.1 0.0 collective-permute-done.5.refs_2_
  36.1 1.7 %arrived.1 = (f32[384,2048]{1,0:T(8,128)S(1)}, bf16[384,128]{1,0:T(8,128)(2,1)S(1)}, bf16[768,128]{1,0:T(8,128)(2,1)}) custom-call(bf16[384,128]{1,0:T(8,128)(2,1)S(1)} %collective-permute-done.refs_0_, bf16[384,128]{1,0:T(8,128)(2,1)S(1)} %collective-permute-done.1.refs_1_, bf16[1536,128]{1,0:T(8,128)(2,1)S(1)} %collective-permute-done.5.refs_2_, ...), custom_call_target="tpu_custom_call" | custom-call | flops 603979776 | bytes 3145728 | tf_op jit(solution)/shard_map/arrived/pallas_call | solution.py:302
  37.8 5.7 %collective-permute-done.8.other_ref = bf16[1280,128]{1,0:T(8,128)(2,1)S(1)} collective-permute-done((bf16[1280,128]{1,0:T(8,128)(2,1)S(1)}, bf16[1280,128]{1,0:T(8,128)(2,1)S(1)}, u32[]{:S(2)}, u32[]{:S(2)}) %collective-permute-start.8) | collective-permute-done | bytes 327712 | tf_op jit(solution)/shard_map/ppermute | solution.py:392
  43.5 2.7 %merge.1 = (f32[1280,128]{1,0:T(8,128)}, f32[1280,128]{1,0:T(8,128)}) custom-call(s32[1]{0:T(128)S(6)} %copy.18.slot_ref, bf16[1280,128]{1,0:T(8,128)(2,1)S(1)} %add_convert_fusion.sum_ref, bf16[1280,128]{1,0:T(8,128)(2,1)S(1)} %collective-permute-done.8.other_ref, f32[2560,128]{1,0:T(8,128)} %bitcast.21, f32[2560,128]{1,0:T(8,128)} %bitcast.22), custom_call_target="tpu_custom_call" | custom-call | flops 1310720 | bytes 4587520 | tf_op jit(solution)/shard_map/merge/pallas_call | solution.py:402
  46.3 0.0 collective-permute-done.6.weight_ref
  46.3 1.4 %finish.1 = bf16[384,2048]{1,0:T(8,128)(2,1)} custom-call(f32[384,2048]{1,0:T(8,128)S(1)} %get-tuple-element.36.sum_ref, bf16[384,128]{1,0:T(8,128)(2,1)S(1)} %get-tuple-element.37.block_ref, bf16[2048,128]{1,0:T(8,128)(2,1)S(1)} %collective-permute-done.6.weight_ref), custom_call_target="tpu_custom_call" | custom-call | flops 201326592 | bytes 4718592 | tf_op jit(solution)/shard_map/finish/pallas_call | solution.py:339
  (1 shorter events, 0.0 us)
Async XLA Ops:
  0.6 7.2 %copy-start = (bf16[768,128]{1,0:T(8,128)(2,1)S(1)}, bf16[768,128]{1,0:T(8,128)(2,1)}, u32[]{:S(2)}) copy-start(bf16[768,128]{1,0:T(8,128)(2,1)} %refs_4_.1) | copy-start | bytes 589828
  2.2 27.4 %collective-permute-start.2 = (bf16[2048,128]{1,0:T(8,128)(2,1)S(1)}, bf16[2048,128]{1,0:T(8,128)(2,1)S(1)}, u32[]{:S(2)}, u32[]{:S(2)}) collective-permute-start(bf16[2048,128]{1,0:T(8,128)(2,1)S(1)} %get-tuple-element.29.refs_5_.refs_4_), channel_id=1, source_target_pairs={{0,2},{1,3},{2,0},{3,1},{4,6},{5,7},{6,4},{7,5},{8,10},{9,11},{10,... | collective-permute-start | bytes 1572872 | tf_op jit(solution)/shard_map/ppermute | solution.py:60
  6.3 24.5 %collective-permute-start.4 = (bf16[2048,128]{1,0:T(8,128)(2,1)S(1)}, bf16[2048,128]{1,0:T(8,128)(2,1)S(1)}, u32[]{:S(2)}, u32[]{:S(2)}) collective-permute-start(bf16[2048,128]{1,0:T(8,128)(2,1)S(1)} %get-tuple-element.29.refs_5_.refs_4_), channel_id=1, source_target_pairs={{0,1},{1,0},{2,3},{3,2},{4,5},{5,4},{6,7},{7,6},{8,9},{9,8},{10,11... | collective-permute-start | bytes 1572872 | tf_op jit(solution)/shard_map/ppermute | solution.py:60
  7.8 2.2 %collective-permute-start.3 = (bf16[768,128]{1,0:T(8,128)(2,1)S(1)}, bf16[768,128]{1,0:T(8,128)(2,1)S(1)}, u32[]{:S(2)}, u32[]{:S(2)}) collective-permute-start(bf16[768,128]{1,0:T(8,128)(2,1)S(1)} %copy-done), channel_id=1, source_target_pairs={{0,4},{4,0},{1,5},{5,1},{2,6},{6,2},{3,7},{7,3},{8,12},{12,8},{9,1... | collective-permute-start | bytes 589832 | tf_op jit(solution)/shard_map/ppermute | solution.py:74
  7.9 25.9 %collective-permute-start.7 = (bf16[1280,128]{1,0:T(8,128)(2,1)S(1)}, bf16[1280,128]{1,0:T(8,128)(2,1)S(1)}, u32[]{:S(2)}, u32[]{:S(2)}) collective-permute-start(bf16[1280,128]{1,0:T(8,128)(2,1)S(1)} %get-tuple-element.38), channel_id=1, source_target_pairs={{0,8},{8,0},{16,24},{24,16},{1,9},{9,1},{17,25},{25,17},{2,10},{10... | collective-permute-start | bytes 983048 | tf_op jit(solution)/shard_map/ppermute | solution.py:392
  9.3 23.0 %collective-permute-start = (bf16[384,128]{1,0:T(8,128)(2,1)S(1)}, bf16[384,128]{1,0:T(8,128)(2,1)S(1)}, u32[]{:S(2)}, u32[]{:S(2)}) collective-permute-start(bf16[384,128]{1,0:T(8,128)(2,1)S(1)} %get-tuple-element.27), channel_id=1, source_target_pairs={{0,0},{1,1},{2,4},{3,5},{4,2},{5,3},{6,6},{7,7},{8,8},{9,9},{10,12... | collective-permute-start | bytes 294920 | tf_op jit(solution)/shard_map/ppermute | solution.py:433
  10.0 22.3 %collective-permute-start.1 = (bf16[384,128]{1,0:T(8,128)(2,1)S(1)}, bf16[384,128]{1,0:T(8,128)(2,1)S(1)}, u32[]{:S(2)}, u32[]{:S(2)}) collective-permute-start(bf16[384,128]{1,0:T(8,128)(2,1)S(1)} %get-tuple-element.28), channel_id=1, source_target_pairs={{0,1},{1,0},{2,5},{3,4},{4,3},{5,2},{6,7},{7,6},{8,9},{9,8},{10,13... | collective-permute-start | bytes 294920 | tf_op jit(solution)/shard_map/ppermute | solution.py:433
  30.8 15.5 %collective-permute-start.6 = (bf16[2048,128]{1,0:T(8,128)(2,1)S(1)}, bf16[2048,128]{1,0:T(8,128)(2,1)S(1)}, u32[]{:S(2)}, u32[]{:S(2)}) collective-permute-start(bf16[2048,128]{1,0:T(8,128)(2,1)S(1)} %collective-permute-done.2.refs_6_), channel_id=1, source_target_pairs={{0,1},{1,0},{2,3},{3,2},{4,5},{5,4},{6,7},{7,6},{8,9},{9,8},{10,11... | collective-permute-start | bytes 1572872 | tf_op jit(solution)/shard_map/ppermute | solution.py:60
  32.4 3.7 %collective-permute-start.5 = (bf16[1536,128]{1,0:T(8,128)(2,1)S(1)}, bf16[1536,128]{1,0:T(8,128)(2,1)S(1)}, u32[]{:S(2)}, u32[]{:S(2)}) collective-permute-start(bf16[1536,128]{1,0:T(8,128)(2,1)S(1)} %pack.1), channel_id=1, source_target_pairs={{0,4},{4,0},{1,5},{5,1},{2,6},{6,2},{3,7},{7,3},{8,12},{12,8},{9,1... | collective-permute-start | bytes 1179656 | tf_op jit(solution)/shard_map/ppermute | solution.py:440
  33.8 9.7 %collective-permute-start.8 = (bf16[1280,128]{1,0:T(8,128)(2,1)S(1)}, bf16[1280,128]{1,0:T(8,128)(2,1)S(1)}, u32[]{:S(2)}, u32[]{:S(2)}) collective-permute-start(bf16[1280,128]{1,0:T(8,128)(2,1)S(1)} %add_convert_fusion.sum_ref), channel_id=1, source_target_pairs={{0,16},{8,24},{16,0},{24,8},{1,17},{9,25},{17,1},{25,9},{2,18},{10... | collective-permute-start | bytes 983048 | tf_op jit(solution)/shard_map/ppermute | solution.py:392

commit v4 on v3

--- a/solution.py
+++ b/solution.py
@@ -56,7 +56,7 @@
         while bit:
             for k in list(have):
                 if k:
-                    have[k], _ = after(have[k], (early, have[bit]))
+                    have[k], _ = after(have[k], early)
                 have[k ^ bit] = lax.ppermute(have[k], axis, swap_pairs(n, bit))
             bit //= 2
     else:
@@ -265,8 +265,15 @@
     block_refs, message_refs = refs[:per_row], refs[per_row:per_row + rows - 1]
     own_ref = refs[per_row + rows - 1]
     weight_refs = refs[per_row + rows:per_row + rows + cols - 1]
-    sum_ref, last_ref, keys_values_hbm, blocks_ref, keys_values_ref, sem = refs[-6:]
+    slot_ref, global_hbm, moment_hbm, sum_ref, last_ref, held_ref, prior_ref, keys_values_hbm = refs[-14:-6]
+    blocks_ref, keys_values_ref, global_ref, moment_ref, sem, slot_sems = refs[-6:]
     row, col = lax.axis_index("row"), lax.axis_index("col")
+    loads = [
+        pltpu.make_async_copy(global_hbm, global_ref, slot_sems.at[0]),
+        pltpu.make_async_copy(moment_hbm, moment_ref, slot_sems.at[1]),
+    ]
+    for load in loads:
+        load.start()
     size, part = block_refs[0].shape[0], own_ref.shape[0]
     total = own_ref[...]
     for message_ref in message_refs:
@@ -292,33 +299,46 @@
             )
             piece = product if piece is None else piece + product
         sum_ref[:, features] = piece
+    slot, count = slot_ref[0], held_ref.shape[0]
+    slots = global_ref.shape[0] // count
+    for load, source_ref, out_ref in zip(loads, (global_ref, moment_ref), (held_ref, prior_ref)):
+        load.wait()
+        out_ref[...] = source_ref[pl.ds(slot, count, stride=slots), :]
     store.wait()
 
 
-def arrived(blocks, messages, own, weights, cols):
+def arrived(blocks, messages, own, weights, cols, global_params, outer_moment, group_slot):
     rows, per_row = len(messages) + 1, len(blocks)
     size, width = blocks[0].shape
     depth = weights[0].shape[0]
+    held = jax.ShapeDtypeStruct((global_params.shape[1] // LANES, LANES), jnp.float32)
     return pl.pallas_call(
         functools.partial(arrived_kernel, rows, cols, min(512, depth)),
         out_shape=[
             jax.ShapeDtypeStruct((size, depth), jnp.float32),
             jax.ShapeDtypeStruct((size, width), jnp.bfloat16),
+            held,
+            held,
             jax.ShapeDtypeStruct(own.shape, jnp.bfloat16),
         ],
-        in_specs=[WHOLE] * (per_row + rows + cols - 1),
-        out_specs=[WHOLE, WHOLE, HBM],
+        in_specs=[WHOLE] * (per_row + rows + cols - 1) + [pl.BlockSpec(memory_space=pltpu.SMEM), HBM, HBM],
+        out_specs=[WHOLE] * 4 + [HBM],
         scratch_shapes=[
             pltpu.VMEM((cols, size, width), jnp.bfloat16),
             pltpu.VMEM(own.shape, jnp.bfloat16),
+            pltpu.VMEM((global_params.size // LANES, LANES), jnp.float32),
+            pltpu.VMEM((global_params.size // LANES, LANES), jnp.float32),
             pltpu.SemaphoreType.DMA,
+            pltpu.SemaphoreType.DMA((2,)),
         ],
         compiler_params=params(24),
         cost_estimate=pl.CostEstimate(
             flops=2 * size * depth * width * (cols - 1), bytes_accessed=4 * size * depth, transcendentals=0
         ),
         name="arrived",
-    )(*blocks, *messages, own, *weights)
+    )(
+        *blocks, *messages, own, *weights, group_slot, in_hbm(interleaved(global_params)), in_hbm(interleaved(outer_moment))
+    )
 
 
 def finish_kernel(tile, sum_ref, block_ref, weight_ref, out_hbm, out_ref, sems):
@@ -350,32 +370,18 @@
     )(total, block, weight)
 
 
-def merge_kernel(replicas, slot_ref, sum_ref, other_ref, global_hbm, moment_hbm, new_global_hbm, new_outer_hbm, *scratch):
-    global_ref, moment_ref, new_global_ref, new_outer_ref, sems = scratch
-    slot = slot_ref[0]
-    count = sum_ref.shape[0]
-    slots = global_ref.shape[0] // count
-    loads = [
-        pltpu.make_async_copy(moment_hbm, moment_ref, sems.at[0]),
-        pltpu.make_async_copy(global_hbm, global_ref, sems.at[1]),
-    ]
-    stores = [
-        pltpu.make_async_copy(new_outer_ref, new_outer_hbm, sems.at[2]),
-        pltpu.make_async_copy(new_global_ref, new_global_hbm, sems.at[3]),
-    ]
-    for load in loads:
-        load.start()
+def merge_kernel(replicas, sum_ref, other_ref, held_ref, prior_ref, new_global_hbm, new_outer_hbm, *scratch):
+    new_global_ref, new_outer_ref, sems = scratch
     average = (sum_ref[...].astype(jnp.float32) + other_ref[...].astype(jnp.float32)) / replicas
-    loads[0].wait()
-    new_outer = NESTEROV * moment_ref[pl.ds(slot, count, stride=slots), :] + average
+    new_outer = NESTEROV * prior_ref[...] + average
     new_outer_ref[...] = new_outer
-    stores[0].start()
-    loads[1].wait()
-    held = global_ref[pl.ds(slot, count, stride=slots), :]
-    new_global_ref[...] = held - OUTER_RATE * (average + NESTEROV * new_outer)
-    stores[1].start()
-    for store in stores:
-        store.wait()
+    outer_store = pltpu.make_async_copy(new_outer_ref, new_outer_hbm, sems.at[0])
+    outer_store.start()
+    new_global_ref[...] = held_ref[...] - OUTER_RATE * (average + NESTEROV * new_outer)
+    global_store = pltpu.make_async_copy(new_global_ref, new_global_hbm, sems.at[1])
+    global_store.start()
+    outer_store.wait()
+    global_store.wait()
 
 
 def interleaved(x):
@@ -397,20 +403,18 @@
         low = (low.astype(jnp.float32) + other.astype(jnp.float32)).astype(jnp.bfloat16)
 
 
-def merge(low, other, global_params, outer_moment, group_slot, replicas):
+def merge(low, other, held, prior, replicas):
     shape = jax.ShapeDtypeStruct(low.shape, jnp.float32)
     new_global, new_outer = pl.pallas_call(
         functools.partial(merge_kernel, replicas),
         out_shape=[shape, shape],
-        in_specs=[pl.BlockSpec(memory_space=pltpu.SMEM)] + [WHOLE] * 2 + [HBM] * 2,
+        in_specs=[WHOLE] * 4,
         out_specs=[HBM] * 2,
-        scratch_shapes=[pltpu.VMEM((global_params.size // LANES, LANES), jnp.float32)] * 2
-        + [pltpu.VMEM(low.shape, jnp.float32)] * 2
-        + [pltpu.SemaphoreType.DMA((4,))],
+        scratch_shapes=[pltpu.VMEM(low.shape, jnp.float32)] * 2 + [pltpu.SemaphoreType.DMA((2,))],
         compiler_params=params(16),
-        cost_estimate=pl.CostEstimate(flops=8 * low.size, bytes_accessed=28 * low.size, transcendentals=0),
+        cost_estimate=pl.CostEstimate(flops=8 * low.size, bytes_accessed=8 * low.size, transcendentals=0),
         name="merge",
-    )(group_slot, low, other, in_hbm(interleaved(global_params)), in_hbm(interleaved(outer_moment)))
+    )(low, other, held, prior)
     return new_global.reshape(-1), new_outer.reshape(-1)
 
 
@@ -438,9 +442,10 @@
     low, other = outer_sums(low, "rep", (sends, weights[1], weights[cols // 2]))
     received, _ = after(received, weights[cols // 2])
     messages = [lax.ppermute(m, "row", shift_pairs(rows, k + 1)) for k, m in enumerate(pack(received, sends))]
-    total, block, keys_values = arrived(received, messages, own, weights[:-1], cols)
-    other, _ = after(other, total)
-    new_global, new_outer = merge(low, other, global_params, outer_moment, group_slot, replicas)
+    total, block, held, prior, keys_values = arrived(
+        received, messages, own, weights[:-1], cols, global_params, outer_moment, group_slot
+    )
+    new_global, new_outer = merge(low, other, held, prior, replicas)
     last, _ = after(weights[-1], (new_outer, total))
     input_grad = finish(total, block, last)
     return (keys_values, input_grad, new_weight[None], new_first[None], new_second[None], new_global, new_outer)

time: 47.9 us -> 46.4 us (0.969)
  waiting for transfers between devices: 15.9 us -> 14.9 us
  Pallas kernels: 17.4 us -> 16.5 us
    pallas_call x1, Pallas kernels: 2.72 us -> 1.2 us  [merge(): pl.pallas_call(functools.partial(merge_kernel, replicas), out_shape=[shap...]
    ppermute x3, waiting for transfers between devices: 10.2 us -> 8.94 us  [gather_offsets(): have[k ^ bit] = lax.ppermute(have[k], axis, swap_pairs(n, bit))]
    ppermute x2, waiting for transfers between devices: 0.01 us -> 0.78 us  [on_device(): lax.ppermute(chunks[k], ('row', 'col'), chunk_pairs(rows, cols, per_row, k))]
    pallas_call x1, Pallas kernels: 1.67 us -> 2.29 us  [arrived(): pl.pallas_call(functools.partial(arrived_kernel, rows, cols, min(512, dep...]
    ppermute x2, waiting for transfers between devices: 5.74 us -> 5.13 us  [outer_sums(): other = lax.ppermute(low, axis, swap_pairs(n, bit))]
  transfers between devices with their start and end apart: 9 -> 9, of which waited for: 3 -> 3; matrix products, arithmetic and copies ran while one was open for 0% -> 0% of each run, Pallas kernels for 30% -> 29%
where the time goes in v4:
time: 46.4 us; the launch traced here: 46.2 us
  Pallas kernels  16.5 us (36%)
  waiting for transfers between devices  14.9 us (32%)
  starting transfers between devices  13.3 us (29%)
  between operations  1.37 us (3%)
    pallas_call x1, Pallas kernels, inner(): pl.pallas_call(functools.partial(inner_kernel, rows, steps), in_specs=[HB...  10.1 us
    ppermute x3, waiting for transfers between devices, gather_offsets(): have[k ^ bit] = lax.ppermute(have[k], axis, swap_pairs(n, bit))  8.94 us
    ppermute x3, starting transfers between devices, gather_offsets(): have[k ^ bit] = lax.ppermute(have[k], axis, swap_pairs(n, bit))  7.35 us
    ppermute x2, waiting for transfers between devices, outer_sums(): other = lax.ppermute(low, axis, swap_pairs(n, bit))  5.13 us
    ppermute x2, starting transfers between devices, outer_sums(): other = lax.ppermute(low, axis, swap_pairs(n, bit))  3.11 us
    pallas_call x1, Pallas kernels, arrived(): pl.pallas_call(functools.partial(arrived_kernel, rows, cols, min(512, dep...  2.29 us
    ppermute x1, starting transfers between devices, on_device(): lax.ppermute(m, 'row', shift_pairs(rows, k + 1))  1.7 us
    pallas_call x1, Pallas kernels, prepare(): pl.pallas_call(functools.partial(prepare_kernel, per_row), out_shape=outs...  1.52 us
  transfers between devices with their start and end apart: 9, of which 3 were waited for; matrix products, arithmetic and copies ran while one was open for 0% of the time, Pallas kernels for 29%

profile of v4, /device:TPU:0, one launch (start us, length us, event | category | flops | bytes accessed | tf_op | source)
XLA Modules:
  0.0 46.2 jit_solution(16316899247018169244)
XLA Ops:
  0.6 0.0 copy-start
  0.6 1.5 %prepare.1 = (bf16[2048,128]{1,0:T(8,128)(2,1)S(1)}, bf16[1280,128]{1,0:T(8,128)(2,1)S(1)}, bf16[384,128]{1,0:T(8,128)(2,1)S(1)}, bf16[384,128]{1,0:T(8,128)(2,1)S(1)}) custom-call(f32[2048,128]{1,0:T(8,128)} %bitcast.19, bf16[768,128]{1,0:T(8,128)(2,1)} %refs_4_.1, f32[1280,128]{1,0:T(8,128)} %bitcast.25), custom_call_target="tpu_custom_call" | custom-call | bytes 2097152 | tf_op jit(solution)/shard_map/prepare/pallas_call | solution.py:112
  2.2 4.1 %collective-permute-start.2 = (bf16[2048,128]{1,0:T(8,128)(2,1)S(1)}, bf16[2048,128]{1,0:T(8,128)(2,1)S(1)}, u32[]{:S(2)}, u32[]{:S(2)}) collective-permute-start(bf16[2048,128]{1,0:T(8,128)(2,1)S(1)} %get-tuple-element.30.refs_5_.refs_4_), channel_id=1, source_target_pairs={{0,2},{1,3},{2,0},{3,1},{4,6},{5,7},{6,4},{7,5},{8,10},{9,11},{10,... | collective-permute-start | bytes 1572872 | tf_op jit(solution)/shard_map/ppermute | solution.py:60
  6.3 1.6 %collective-permute-start.5 = (bf16[2048,128]{1,0:T(8,128)(2,1)S(1)}, bf16[2048,128]{1,0:T(8,128)(2,1)S(1)}, u32[]{:S(2)}, u32[]{:S(2)}) collective-permute-start(bf16[2048,128]{1,0:T(8,128)(2,1)S(1)} %get-tuple-element.30.refs_5_.refs_4_), channel_id=1, source_target_pairs={{0,1},{1,0},{2,3},{3,2},{4,5},{5,4},{6,7},{7,6},{8,9},{9,8},{10,11... | collective-permute-start | bytes 1572872 | tf_op jit(solution)/shard_map/ppermute | solution.py:60
  7.8 0.0 copy-done
  7.8 0.0 collective-permute-start.3
  7.9 1.5 %collective-permute-start.7 = (bf16[1280,128]{1,0:T(8,128)(2,1)S(1)}, bf16[1280,128]{1,0:T(8,128)(2,1)S(1)}, u32[]{:S(2)}, u32[]{:S(2)}) collective-permute-start(bf16[1280,128]{1,0:T(8,128)(2,1)S(1)} %get-tuple-element.39), channel_id=1, source_target_pairs={{0,8},{8,0},{16,24},{24,16},{1,9},{9,1},{17,25},{25,17},{2,10},{10... | collective-permute-start | bytes 983048 | tf_op jit(solution)/shard_map/ppermute | solution.py:398
  9.3 0.7 %collective-permute-start = (bf16[384,128]{1,0:T(8,128)(2,1)S(1)}, bf16[384,128]{1,0:T(8,128)(2,1)S(1)}, u32[]{:S(2)}, u32[]{:S(2)}) collective-permute-start(bf16[384,128]{1,0:T(8,128)(2,1)S(1)} %get-tuple-element.28), channel_id=1, source_target_pairs={{0,0},{1,1},{2,4},{3,5},{4,2},{5,3},{6,6},{7,7},{8,8},{9,9},{10,12... | collective-permute-start | bytes 294920 | tf_op jit(solution)/shard_map/ppermute | solution.py:437
  10.0 0.0 collective-permute-done.3.refs_6_
  10.0 0.5 %collective-permute-start.1 = (bf16[384,128]{1,0:T(8,128)(2,1)S(1)}, bf16[384,128]{1,0:T(8,128)(2,1)S(1)}, u32[]{:S(2)}, u32[]{:S(2)}) collective-permute-start(bf16[384,128]{1,0:T(8,128)(2,1)S(1)} %get-tuple-element.29), channel_id=1, source_target_pairs={{0,1},{1,0},{2,5},{3,4},{4,3},{5,2},{6,7},{7,6},{8,9},{9,8},{10,13... | collective-permute-start | bytes 294920 | tf_op jit(solution)/shard_map/ppermute | solution.py:437
  10.5 10.1 %inner.1 = (f32[2048,128]{1,0:T(8,128)}, f32[2048,128]{1,0:T(8,128)}, f32[2048,128]{1,0:T(8,128)}, f32[768,128]{1,0:T(8,128)S(1)}, bf16[768,128]{1,0:T(8,128)(2,1)S(1)}) custom-call(bf16[1536,2048]{1,0:T(8,128)(2,1)} %refs_0_.1, f32[2048,128]{1,0:T(8,128)} %bitcast.20, f32[2048,128]{1,0:T(8,128)} %bitcast.23, f32[2048,128]{1,0:T(8,128)} %bitcast.24, ...), custom_call_target="tpu_custom_call" | custom-call | flops 1610612736 | bytes 12582912 | tf_op jit(solution)/shard_map/inner/pallas_call | solution.py:234
  20.6 8.9 %collective-permute-done.2.refs_6_ = bf16[2048,128]{1,0:T(8,128)(2,1)S(1)} collective-permute-done((bf16[2048,128]{1,0:T(8,128)(2,1)S(1)}, bf16[2048,128]{1,0:T(8,128)(2,1)S(1)}, u32[]{:S(2)}, u32[]{:S(2)}) %collective-permute-start.2) | collective-permute-done | bytes 524320 | tf_op jit(solution)/shard_map/ppermute | solution.py:60
  29.5 1.7 %collective-permute-start.6 = (bf16[2048,128]{1,0:T(8,128)(2,1)S(1)}, bf16[2048,128]{1,0:T(8,128)(2,1)S(1)}, u32[]{:S(2)}, u32[]{:S(2)}) collective-permute-start(bf16[2048,128]{1,0:T(8,128)(2,1)S(1)} %collective-permute-done.2.refs_6_), channel_id=1, source_target_pairs={{0,1},{1,0},{2,3},{3,2},{4,5},{5,4},{6,7},{7,6},{8,9},{9,8},{10,11... | collective-permute-start | bytes 1572872 | tf_op jit(solution)/shard_map/ppermute | solution.py:60
  31.2 0.0 collective-permute-done.refs_0_
  31.2 0.8 %collective-permute-done.1.refs_1_ = bf16[384,128]{1,0:T(8,128)(2,1)S(1)} collective-permute-done((bf16[384,128]{1,0:T(8,128)(2,1)S(1)}, bf16[384,128]{1,0:T(8,128)(2,1)S(1)}, u32[]{:S(2)}, u32[]{:S(2)}) %collective-permute-start.1) | collective-permute-done | bytes 98336 | tf_op jit(solution)/shard_map/ppermute | solution.py:437
  32.0 1.7 %collective-permute-start.4 = (bf16[1536,128]{1,0:T(8,128)(2,1)S(1)}, bf16[1536,128]{1,0:T(8,128)(2,1)S(1)}, u32[]{:S(2)}, u32[]{:S(2)}) collective-permute-start(bf16[1536,128]{1,0:T(8,128)(2,1)S(1)} %pack.1), channel_id=1, source_target_pairs={{0,4},{4,0},{1,5},{5,1},{2,6},{6,2},{3,7},{7,3},{8,12},{12,8},{9,1... | collective-permute-start | bytes 1179656 | tf_op jit(solution)/shard_map/ppermute | solution.py:444
  33.7 0.0 collective-permute-done.7
  33.7 0.0 collective-permute-done.5.refs_5_
  33.7 0.1 add_convert_fusion.sum_ref
  33.8 1.6 %collective-permute-start.8 = (bf16[1280,128]{1,0:T(8,128)(2,1)S(1)}, bf16[1280,128]{1,0:T(8,128)(2,1)S(1)}, u32[]{:S(2)}, u32[]{:S(2)}) collective-permute-start(bf16[1280,128]{1,0:T(8,128)(2,1)S(1)} %add_convert_fusion.sum_ref), channel_id=1, source_target_pairs={{0,16},{8,24},{16,0},{24,8},{1,17},{9,25},{17,1},{25,9},{2,18},{10... | collective-permute-start | bytes 983048 | tf_op jit(solution)/shard_map/ppermute | solution.py:398
  36.1 0.0 collective-permute-done.4.refs_2_
  36.1 2.3 %arrived.1 = (f32[384,2048]{1,0:T(8,128)S(1)}, bf16[384,128]{1,0:T(8,128)(2,1)S(1)}, f32[1280,128]{1,0:T(8,128)S(1)}, f32[1280,128]{1,0:T(8,128)S(1)}, bf16[768,128]{1,0:T(8,128)(2,1)}) custom-call(bf16[384,128]{1,0:T(8,128)(2,1)S(1)} %collective-permute-done.refs_0_, bf16[384,128]{1,0:T(8,128)(2,1)S(1)} %collective-permute-done.1.refs_1_, ...), custom_call_target="tpu_custom_call" | custom-call | flops 603979776 | bytes 3145728 | tf_op jit(solution)/shard_map/arrived/pallas_call | solution.py:315
  38.4 5.1 %collective-permute-done.8.other_ref = bf16[1280,128]{1,0:T(8,128)(2,1)S(1)} collective-permute-done((bf16[1280,128]{1,0:T(8,128)(2,1)S(1)}, bf16[1280,128]{1,0:T(8,128)(2,1)S(1)}, u32[]{:S(2)}, u32[]{:S(2)}) %collective-permute-start.8) | collective-permute-done | bytes 327712 | tf_op jit(solution)/shard_map/ppermute | solution.py:398
  43.5 1.2 %merge.1 = (f32[1280,128]{1,0:T(8,128)}, f32[1280,128]{1,0:T(8,128)}) custom-call(bf16[1280,128]{1,0:T(8,128)(2,1)S(1)} %add_convert_fusion.sum_ref, bf16[1280,128]{1,0:T(8,128)(2,1)S(1)} %collective-permute-done.8.other_ref, f32[1280,128]{1,0:T(8,128)S(1)} %get-tuple-element.41.held_ref, f32[1280,128]{1,0:T(8,128)S(1)} %get-tuple-element.42.prior_ref), custom_call_target="tpu_custom_call" | custom-call | flops 1310720 | bytes 1310720 | tf_op jit(solution)/shard_map/merge/pallas_call | solution.py:408
  44.7 0.0 collective-permute-done.6.weight_ref
  44.7 1.4 %finish.1 = bf16[384,2048]{1,0:T(8,128)(2,1)} custom-call(f32[384,2048]{1,0:T(8,128)S(1)} %get-tuple-element.37.sum_ref, bf16[384,128]{1,0:T(8,128)(2,1)S(1)} %get-tuple-element.38.block_ref, bf16[2048,128]{1,0:T(8,128)(2,1)S(1)} %collective-permute-done.6.weight_ref), custom_call_target="tpu_custom_call" | custom-call | flops 201326592 | bytes 4718592 | tf_op jit(solution)/shard_map/finish/pallas_call | solution.py:359
  (1 shorter events, 0.0 us)
Async XLA Ops:
  0.6 7.2 %copy-start = (bf16[768,128]{1,0:T(8,128)(2,1)S(1)}, bf16[768,128]{1,0:T(8,128)(2,1)}, u32[]{:S(2)}) copy-start(bf16[768,128]{1,0:T(8,128)(2,1)} %refs_4_.1) | copy-start | bytes 589828
  2.2 27.4 %collective-permute-start.2 = (bf16[2048,128]{1,0:T(8,128)(2,1)S(1)}, bf16[2048,128]{1,0:T(8,128)(2,1)S(1)}, u32[]{:S(2)}, u32[]{:S(2)}) collective-permute-start(bf16[2048,128]{1,0:T(8,128)(2,1)S(1)} %get-tuple-element.30.refs_5_.refs_4_), channel_id=1, source_target_pairs={{0,2},{1,3},{2,0},{3,1},{4,6},{5,7},{6,4},{7,5},{8,10},{9,11},{10,... | collective-permute-start | bytes 1572872 | tf_op jit(solution)/shard_map/ppermute | solution.py:60
  6.3 27.5 %collective-permute-start.5 = (bf16[2048,128]{1,0:T(8,128)(2,1)S(1)}, bf16[2048,128]{1,0:T(8,128)(2,1)S(1)}, u32[]{:S(2)}, u32[]{:S(2)}) collective-permute-start(bf16[2048,128]{1,0:T(8,128)(2,1)S(1)} %get-tuple-element.30.refs_5_.refs_4_), channel_id=1, source_target_pairs={{0,1},{1,0},{2,3},{3,2},{4,5},{5,4},{6,7},{7,6},{8,9},{9,8},{10,11... | collective-permute-start | bytes 1572872 | tf_op jit(solution)/shard_map/ppermute | solution.py:60
  7.8 2.2 %collective-permute-start.3 = (bf16[768,128]{1,0:T(8,128)(2,1)S(1)}, bf16[768,128]{1,0:T(8,128)(2,1)S(1)}, u32[]{:S(2)}, u32[]{:S(2)}) collective-permute-start(bf16[768,128]{1,0:T(8,128)(2,1)S(1)} %copy-done), channel_id=1, source_target_pairs={{0,4},{4,0},{1,5},{5,1},{2,6},{6,2},{3,7},{7,3},{8,12},{12,8},{9,1... | collective-permute-start | bytes 589832 | tf_op jit(solution)/shard_map/ppermute | solution.py:74
  7.9 25.9 %collective-permute-start.7 = (bf16[1280,128]{1,0:T(8,128)(2,1)S(1)}, bf16[1280,128]{1,0:T(8,128)(2,1)S(1)}, u32[]{:S(2)}, u32[]{:S(2)}) collective-permute-start(bf16[1280,128]{1,0:T(8,128)(2,1)S(1)} %get-tuple-element.39), channel_id=1, source_target_pairs={{0,8},{8,0},{16,24},{24,16},{1,9},{9,1},{17,25},{25,17},{2,10},{10... | collective-permute-start | bytes 983048 | tf_op jit(solution)/shard_map/ppermute | solution.py:398
  9.3 21.9 %collective-permute-start = (bf16[384,128]{1,0:T(8,128)(2,1)S(1)}, bf16[384,128]{1,0:T(8,128)(2,1)S(1)}, u32[]{:S(2)}, u32[]{:S(2)}) collective-permute-start(bf16[384,128]{1,0:T(8,128)(2,1)S(1)} %get-tuple-element.28), channel_id=1, source_target_pairs={{0,0},{1,1},{2,4},{3,5},{4,2},{5,3},{6,6},{7,7},{8,8},{9,9},{10,12... | collective-permute-start | bytes 294920 | tf_op jit(solution)/shard_map/ppermute | solution.py:437
  10.0 22.0 %collective-permute-start.1 = (bf16[384,128]{1,0:T(8,128)(2,1)S(1)}, bf16[384,128]{1,0:T(8,128)(2,1)S(1)}, u32[]{:S(2)}, u32[]{:S(2)}) collective-permute-start(bf16[384,128]{1,0:T(8,128)(2,1)S(1)} %get-tuple-element.29), channel_id=1, source_target_pairs={{0,1},{1,0},{2,5},{3,4},{4,3},{5,2},{6,7},{7,6},{8,9},{9,8},{10,13... | collective-permute-start | bytes 294920 | tf_op jit(solution)/shard_map/ppermute | solution.py:437
  29.5 15.2 %collective-permute-start.6 = (bf16[2048,128]{1,0:T(8,128)(2,1)S(1)}, bf16[2048,128]{1,0:T(8,128)(2,1)S(1)}, u32[]{:S(2)}, u32[]{:S(2)}) collective-permute-start(bf16[2048,128]{1,0:T(8,128)(2,1)S(1)} %collective-permute-done.2.refs_6_), channel_id=1, source_target_pairs={{0,1},{1,0},{2,3},{3,2},{4,5},{5,4},{6,7},{7,6},{8,9},{9,8},{10,11... | collective-permute-start | bytes 1572872 | tf_op jit(solution)/shard_map/ppermute | solution.py:60
  32.0 4.1 %collective-permute-start.4 = (bf16[1536,128]{1,0:T(8,128)(2,1)S(1)}, bf16[1536,128]{1,0:T(8,128)(2,1)S(1)}, u32[]{:S(2)}, u32[]{:S(2)}) collective-permute-start(bf16[1536,128]{1,0:T(8,128)(2,1)S(1)} %pack.1), channel_id=1, source_target_pairs={{0,4},{4,0},{1,5},{5,1},{2,6},{6,2},{3,7},{7,3},{8,12},{12,8},{9,1... | collective-permute-start | bytes 1179656 | tf_op jit(solution)/shard_map/ppermute | solution.py:444
  33.8 9.7 %collective-permute-start.8 = (bf16[1280,128]{1,0:T(8,128)(2,1)S(1)}, bf16[1280,128]{1,0:T(8,128)(2,1)S(1)}, u32[]{:S(2)}, u32[]{:S(2)}) collective-permute-start(bf16[1280,128]{1,0:T(8,128)(2,1)S(1)} %add_convert_fusion.sum_ref), channel_id=1, source_target_pairs={{0,16},{8,24},{16,0},{24,8},{1,17},{9,25},{17,1},{25,9},{2,18},{10... | collective-permute-start | bytes 983048 | tf_op jit(solution)/shard_map/ppermute | solution.py:398

commit v5 on v4

--- a/solution.py
+++ b/solution.py
@@ -15,6 +15,7 @@
 OUTER_RATE = 0.7
 NESTEROV = 0.9
 LANES = 128
+PARTS = 1
 
 WHOLE = pl.BlockSpec(memory_space=pltpu.VMEM)
 HBM = pl.BlockSpec(memory_space=pltpu.HBM)
@@ -48,20 +49,21 @@
     return lax.rem(value + n, n)
 
 
-def gather_offsets(block, axis, early):
+def gather_offsets(whole, parts, axis, early):
     n = lax.axis_size(axis)
-    have = {0: block}
+    have = {0: [whole]}
     if is_power_of_two(n):
         bit = n // 2
         while bit:
             for k in list(have):
+                sent = have[k] if k else parts if bit > 1 else [whole]
                 if k:
-                    have[k], _ = after(have[k], early)
-                have[k ^ bit] = lax.ppermute(have[k], axis, swap_pairs(n, bit))
+                    sent, _ = after(sent, early)
+                have[k ^ bit] = [lax.ppermute(part, axis, swap_pairs(n, bit)) for part in sent]
             bit //= 2
     else:
         for k in range(1, n):
-            have[k] = lax.ppermute(have[k - 1], axis, shift_pairs(n, n - 1))
+            have[k] = [lax.ppermute(part, axis, shift_pairs(n, n - 1)) for part in have[k - 1]]
     return [have[k] for k in range(n)]
 
 
@@ -82,72 +84,94 @@
     return pairs
 
 
-def prepare_kernel(per_row, weight_hbm, cot_hbm, delta_hbm, low_weight_ref, low_delta_ref, *refs):
+def round_kernel(pieces, source_hbm, *refs):
+    whole_ref, part_refs, source_ref, sems = refs[0], refs[1:-2], refs[-2], refs[-1]
+    size, part = source_ref.shape[0] // pieces, source_ref.shape[0] // len(part_refs)
+    loads = []
+    for i in range(pieces):
+        some = pl.ds(i * size, size)
+        loads.append(pltpu.make_async_copy(source_hbm.at[some, :], source_ref.at[some, :], sems.at[i]))
+        loads[-1].start()
+    for i in range(pieces):
+        loads[i].wait()
+        start = i * size
+        low = source_ref[pl.ds(start, size), :].astype(jnp.bfloat16)
+        whole_ref[pl.ds(start, size), :] = low
+        part_refs[start // part][pl.ds(start % part, size), :] = low
+
+
+def rounded(x, parts):
+    pieces = 2 * parts
+    shape = lambda rows: jax.ShapeDtypeStruct((rows, x.shape[1]), jnp.bfloat16)
+    got = pl.pallas_call(
+        functools.partial(round_kernel, pieces),
+        out_shape=[shape(x.shape[0])] + [shape(x.shape[0] // parts)] * parts,
+        in_specs=[HBM],
+        out_specs=[WHOLE] * (1 + parts),
+        scratch_shapes=[pltpu.VMEM(x.shape, jnp.float32), pltpu.SemaphoreType.DMA((pieces,))],
+        compiler_params=params(16),
+        cost_estimate=pl.CostEstimate(flops=0, bytes_accessed=8 * x.size, transcendentals=0),
+        name="rounded",
+    )(in_hbm(x))
+    return got[0], got[1:]
+
+
+def prepare_kernel(per_row, cot_hbm, delta_hbm, low_delta_ref, *refs):
     chunk_refs = refs[:per_row]
-    weight_ref, delta_ref, sems, chunk_sems = refs[per_row:]
+    delta_ref, sem, chunk_sems = refs[per_row:]
     size = chunk_refs[0].shape[0]
     col = lax.axis_index("col")
-    loads = [
-        pltpu.make_async_copy(weight_hbm, weight_ref, sems.at[0]),
-        pltpu.make_async_copy(delta_hbm, delta_ref, sems.at[1]),
-    ]
+    load = pltpu.make_async_copy(delta_hbm, delta_ref, sem)
+    load.start()
     chunks = []
     for k in range(per_row):
         start = pl.multiple_of(lax.rem(col + k, per_row) * size, size)
         chunks.append(pltpu.make_async_copy(cot_hbm.at[pl.ds(start, size), :], chunk_refs[k], chunk_sems.at[k]))
-    for copy in loads + chunks:
-        copy.start()
-    loads[0].wait()
-    low_weight_ref[...] = weight_ref[...].astype(jnp.bfloat16)
-    loads[1].wait()
+        chunks[-1].start()
+    load.wait()
     low_delta_ref[...] = delta_ref[...].astype(jnp.bfloat16)
     for copy in chunks:
         copy.wait()
 
 
-def prepare(weight, cotangent, delta, per_row):
+def prepare(cotangent, delta, per_row):
     chunk = cotangent.shape[0] // per_row
     shape = lambda *s: jax.ShapeDtypeStruct(s, jnp.bfloat16)
-    outs = [shape(*weight.shape), shape(*delta.shape)] + [shape(chunk, cotangent.shape[1])] * per_row
+    outs = [shape(*delta.shape)] + [shape(chunk, cotangent.shape[1])] * per_row
     got = pl.pallas_call(
         functools.partial(prepare_kernel, per_row),
         out_shape=outs,
-        in_specs=[HBM] * 3,
+        in_specs=[HBM] * 2,
         out_specs=[WHOLE] * len(outs),
         scratch_shapes=[
-            pltpu.VMEM(weight.shape, jnp.float32),
             pltpu.VMEM(delta.shape, jnp.float32),
-            pltpu.SemaphoreType.DMA((2,)),
+            pltpu.SemaphoreType.DMA,
             pltpu.SemaphoreType.DMA((per_row,)),
         ],
         compiler_params=params(16),
-        cost_estimate=pl.CostEstimate(flops=0, bytes_accessed=8 * weight.size, transcendentals=0),
+        cost_estimate=pl.CostEstimate(flops=0, bytes_accessed=6 * delta.size, transcendentals=0),
         name="prepare",
-    )(*map(in_hbm, (weight, cotangent, delta)))
-    return got[0], got[1], got[2:]
-
-
-def pack_kernel(per_row, *refs):
-    block_refs, sum_refs = refs[:per_row], refs[per_row:per_row + (len(refs) - per_row) // 2]
-    out_refs = refs[per_row + len(sum_refs):]
-    size, part = block_refs[0].shape[0], sum_refs[0].shape[0]
-    for out_ref, sum_ref in zip(out_refs, sum_refs):
-        for k in range(per_row):
-            out_ref[pl.ds(k * size, size), :] = block_refs[k][...]
-        out_ref[pl.ds(part, part), :] = sum_ref[...]
-
-
-def pack(blocks, sends):
-    part, width = sends[0].shape
+    )(*map(in_hbm, (cotangent, delta)))
+    return got[0], got[1:]
+
+
+def pack_kernel(*refs):
+    size = refs[0].shape[0]
+    for k, block_ref in enumerate(refs[:-1]):
+        refs[-1][pl.ds(k * size, size), :] = block_ref[...]
+
+
+def pack(blocks):
+    size, width = blocks[0].shape
     return pl.pallas_call(
-        functools.partial(pack_kernel, len(blocks)),
-        out_shape=[jax.ShapeDtypeStruct((2 * part, width), jnp.bfloat16)] * len(sends),
-        in_specs=[WHOLE] * (len(blocks) + len(sends)),
-        out_specs=[WHOLE] * len(sends),
+        pack_kernel,
+        out_shape=jax.ShapeDtypeStruct((len(blocks) * size, width), jnp.bfloat16),
+        in_specs=[WHOLE] * len(blocks),
+        out_specs=WHOLE,
         compiler_params=params(16),
-        cost_estimate=pl.CostEstimate(flops=0, bytes_accessed=8 * part * width, transcendentals=0),
+        cost_estimate=pl.CostEstimate(flops=0, bytes_accessed=4 * len(blocks) * size * width, transcendentals=0),
         name="pack",
-    )(*blocks, *sends)
+    )(*blocks)
 
 
 def inner_kernel(rows, steps, *refs):
@@ -260,11 +284,15 @@
     return lax.dot_general(left, right, (((1,), (1,)), ((), ())), preferred_element_type=jnp.float32)
 
 
-def arrived_kernel(rows, cols, tile, *refs):
+def arrived_kernel(rows, cols, counts, tile, *refs):
     per_row = cols // rows
+    held_parts = sum(counts)
     block_refs, message_refs = refs[:per_row], refs[per_row:per_row + rows - 1]
+    refs = refs[:per_row] + refs[per_row + rows - 1:]
+    sum_refs = refs[per_row:per_row + rows - 1]
     own_ref = refs[per_row + rows - 1]
-    weight_refs = refs[per_row + rows:per_row + rows + cols - 1]
+    part_refs = list(refs[per_row + rows:per_row + rows + held_parts])
+    weight_refs = [[part_refs.pop(0) for _ in range(count)] for count in counts]
     slot_ref, global_hbm, moment_hbm, sum_ref, last_ref, held_ref, prior_ref, keys_values_hbm = refs[-14:-6]
     blocks_ref, keys_values_ref, global_ref, moment_ref, sem, slot_sems = refs[-6:]
     row, col = lax.axis_index("row"), lax.axis_index("col")
@@ -276,8 +304,8 @@
         load.start()
     size, part = block_refs[0].shape[0], own_ref.shape[0]
     total = own_ref[...]
-    for message_ref in message_refs:
-        total += message_ref[pl.ds(part, part), :].astype(jnp.float32)
+    for other_ref in sum_refs:
+        total += other_ref[...].astype(jnp.float32)
     keys_values_ref[...] = total.astype(jnp.bfloat16)
     store = pltpu.make_async_copy(keys_values_ref, keys_values_hbm, sem)
     store.start()
@@ -288,14 +316,18 @@
             blocks_ref[mod(row - j, rows) * per_row + column] = message_refs[j - 1][pl.ds(k * size, size), :]
     last_ref[...] = blocks_ref[owner_of(col, cols - 1, cols)]
     left = [blocks_ref[owner_of(col, k, cols)] for k in range(cols - 1)]
-    for start in range(0, weight_refs[0].shape[0], tile):
+    for start in range(0, sum_ref.shape[1], tile):
         features = pl.ds(start, tile)
+        tiles = []
+        for parts in weight_refs:
+            size = parts[0].shape[0]
+            tiles.append(parts[start // size][pl.ds(start % size, tile), :])
         piece = None
         for k in range(0, cols - 1, 2):
             few = range(k, min(k + 2, cols - 1))
             product = times_transposed(
                 jnp.concatenate([left[i] for i in few], axis=1),
-                jnp.concatenate([weight_refs[i][features, :] for i in few], axis=1),
+                jnp.concatenate([tiles[i] for i in few], axis=1),
             )
             piece = product if piece is None else piece + product
         sum_ref[:, features] = piece
@@ -307,13 +339,14 @@
     store.wait()
 
 
-def arrived(blocks, messages, own, weights, cols, global_params, outer_moment, group_slot):
+def arrived(blocks, messages, sums, own, weights, cols, global_params, outer_moment, group_slot):
     rows, per_row = len(messages) + 1, len(blocks)
     size, width = blocks[0].shape
-    depth = weights[0].shape[0]
+    depth = sum(part.shape[0] for part in weights[0])
+    parts = [part for block in weights for part in block]
     held = jax.ShapeDtypeStruct((global_params.shape[1] // LANES, LANES), jnp.float32)
     return pl.pallas_call(
-        functools.partial(arrived_kernel, rows, cols, min(512, depth)),
+        functools.partial(arrived_kernel, rows, cols, tuple(map(len, weights)), min(512, depth // PARTS)),
         out_shape=[
             jax.ShapeDtypeStruct((size, depth), jnp.float32),
             jax.ShapeDtypeStruct((size, width), jnp.bfloat16),
@@ -321,7 +354,7 @@
             held,
             jax.ShapeDtypeStruct(own.shape, jnp.bfloat16),
         ],
-        in_specs=[WHOLE] * (per_row + rows + cols - 1) + [pl.BlockSpec(memory_space=pltpu.SMEM), HBM, HBM],
+        in_specs=[WHOLE] * (per_row + 2 * rows - 1 + len(parts)) + [pl.BlockSpec(memory_space=pltpu.SMEM), HBM, HBM],
         out_specs=[WHOLE] * 4 + [HBM],
         scratch_shapes=[
             pltpu.VMEM((cols, size, width), jnp.bfloat16),
@@ -337,37 +370,41 @@
         ),
         name="arrived",
     )(
-        *blocks, *messages, own, *weights, group_slot, in_hbm(interleaved(global_params)), in_hbm(interleaved(outer_moment))
+        *blocks, *messages, *sums, own, *parts, group_slot, in_hbm(interleaved(global_params)), in_hbm(interleaved(outer_moment))
     )
 
 
-def finish_kernel(tile, sum_ref, block_ref, weight_ref, out_hbm, out_ref, sems):
+def finish_kernel(tile, first, sum_ref, block_ref, weight_ref, *refs):
+    out_hbm, out_ref, sems = refs[-3:]
     stores = []
     for i, start in enumerate(range(0, weight_ref.shape[0], tile)):
-        features = pl.ds(start, tile)
+        features, target = pl.ds(start, tile), pl.ds(first + start, tile)
         piece = times_transposed(block_ref[...], weight_ref[features, :])
-        out_ref[:, features] = (sum_ref[:, features] + piece).astype(jnp.bfloat16)
-        stores.append(pltpu.make_async_copy(out_ref.at[:, features], out_hbm.at[:, features], sems.at[i]))
+        out_ref[:, features] = (sum_ref[:, target] + piece).astype(jnp.bfloat16)
+        stores.append(pltpu.make_async_copy(out_ref.at[:, features], out_hbm.at[:, target], sems.at[i]))
         stores[-1].start()
     for store in stores:
         store.wait()
 
 
-def finish(total, block, weight):
+def finish(total, block, weight, part, before):
     size, depth = total.shape
-    tile = min(512, depth)
+    count = weight.shape[0]
+    tile = min(512, count)
+    kept = [] if before is None else [before]
     return pl.pallas_call(
-        functools.partial(finish_kernel, tile),
+        functools.partial(finish_kernel, tile, part * count),
         out_shape=jax.ShapeDtypeStruct((size, depth), jnp.bfloat16),
-        in_specs=[WHOLE] * 3,
+        in_specs=[WHOLE] * 3 + [HBM] * len(kept),
         out_specs=HBM,
-        scratch_shapes=[pltpu.VMEM((size, depth), jnp.bfloat16), pltpu.SemaphoreType.DMA((depth // tile,))],
+        scratch_shapes=[pltpu.VMEM((size, count), jnp.bfloat16), pltpu.SemaphoreType.DMA((count // tile,))],
+        input_output_aliases={3: 0} if kept else {},
         compiler_params=params(16),
         cost_estimate=pl.CostEstimate(
-            flops=2 * size * depth * block.shape[1], bytes_accessed=6 * size * depth, transcendentals=0
+            flops=2 * size * count * block.shape[1], bytes_accessed=6 * size * count, transcendentals=0
         ),
         name="finish",
-    )(total, block, weight)
+    )(total, block, weight, *kept)
 
 
 def merge_kernel(replicas, sum_ref, other_ref, held_ref, prior_ref, new_global_hbm, new_outer_hbm, *scratch):
@@ -433,21 +470,25 @@
     replicas = lax.axis_size("rep")
     per_row = cols // rows
     cots = shifted(cotangent, "row")
-    low_weight, low, chunks = prepare(weight[0], cotangent, outer_delta.reshape(-1, LANES), per_row)
+    low_weight, low_parts = rounded(weight[0], PARTS)
+    low, chunks = prepare(cotangent, outer_delta.reshape(-1, LANES), per_row)
     received = [lax.ppermute(chunks[k], ("row", "col"), chunk_pairs(rows, cols, per_row, k)) for k in range(per_row)]
     (new_weight, new_first, new_second), own, sends = inner(
         tokens, weight[0], first_moment[0], second_moment[0], cots, low_weight
     )
-    weights = gather_offsets(low_weight, "col", sends)
+    weights = gather_offsets(low_weight, low_parts, "col", sends)
     low, other = outer_sums(low, "rep", (sends, weights[1], weights[cols // 2]))
     received, _ = after(received, weights[cols // 2])
-    messages = [lax.ppermute(m, "row", shift_pairs(rows, k + 1)) for k, m in enumerate(pack(received, sends))]
+    sums = [lax.ppermute(m, "row", shift_pairs(rows, k + 1)) for k, m in enumerate(sends)]
+    messages = [lax.ppermute(pack(received), "row", shift_pairs(rows, k)) for k in range(1, rows)]
     total, block, held, prior, keys_values = arrived(
-        received, messages, own, weights[:-1], cols, global_params, outer_moment, group_slot
+        received, messages, sums, own, weights[:-1], cols, global_params, outer_moment, group_slot
     )
     new_global, new_outer = merge(low, other, held, prior, replicas)
-    last, _ = after(weights[-1], (new_outer, total))
-    input_grad = finish(total, block, last)
+    input_grad = None
+    for part, last in enumerate(weights[-1]):
+        last, _ = after(last, total if input_grad is None else (new_outer, input_grad))
+        input_grad = finish(total, block, last, part, input_grad)
     return (keys_values, input_grad, new_weight[None], new_first[None], new_second[None], new_global, new_outer)
 
 

time: 46.4 us -> 45.5 us (0.981)
  starting transfers between devices: 13.3 us -> 12.1 us
  Pallas kernels: 16.5 us -> 17.7 us
  waiting for transfers between devices: 14.9 us -> 14 us
    ppermute x2, waiting for transfers between devices: 5.13 us -> 1.92 us  [outer_sums(): other = lax.ppermute(low, axis, swap_pairs(n, bit))]
    ppermute x3 -> x4, waiting for transfers between devices: 8.94 us -> 11.9 us  [the longest x3 11.6 us: gather_offsets(): lax.ppermute(part, axis, swap_pairs(n, bit))]
    ppermute x1, starting transfers between devices: 1.7 us -> 0.01 us  [on_device(): lax.ppermute(m, 'row', shift_pairs(rows, k + 1))]
    pallas_call x3 -> x4, Pallas kernels: 3.75 us -> 5.28 us  [the longest x1 2.58 us: arrived(): pl.pallas_call(functools.partial(arrived_kernel, rows, cols, tuple(map(le...]
    ppermute x2, waiting for transfers between devices: 0.78 us -> 0.01 us  [on_device(): lax.ppermute(chunks[k], ('row', 'col'), chunk_pairs(rows, cols, per_row, k))]
    ppermute x3 -> x4, starting transfers between devices: 7.35 us -> 7.82 us  [the longest x3 7.26 us: gather_offsets(): lax.ppermute(part, axis, swap_pairs(n, bit))]
  transfers between devices with their start and end apart: 9 -> 10, of which waited for: 3 -> 6; matrix products, arithmetic and copies ran while one was open for 0% -> 0% of each run, Pallas kernels for 29% -> 33%
where the time goes in v5:
time: 45.5 us; the launch traced here: 45.3 us
  Pallas kernels  17.7 us (39%)
  waiting for transfers between devices  14 us (31%)
  starting transfers between devices  12.1 us (27%)
  between operations  1.37 us (3%)
    ppermute x3, waiting for transfers between devices, gather_offsets(): lax.ppermute(part, axis, swap_pairs(n, bit))  11.6 us
    pallas_call x1, Pallas kernels, inner(): pl.pallas_call(functools.partial(inner_kernel, rows, steps), in_specs=[HB...  10 us
    ppermute x3, starting transfers between devices, gather_offsets(): lax.ppermute(part, axis, swap_pairs(n, bit))  7.26 us
    ppermute x2, starting transfers between devices, outer_sums(): other = lax.ppermute(low, axis, swap_pairs(n, bit))  3.14 us
    pallas_call x1, Pallas kernels, arrived(): pl.pallas_call(functools.partial(arrived_kernel, rows, cols, tuple(map(le...  2.58 us
    ppermute x2, waiting for transfers between devices, outer_sums(): other = lax.ppermute(low, axis, swap_pairs(n, bit))  1.92 us
    pallas_call x1, Pallas kernels, finish(): pl.pallas_call(functools.partial(finish_kernel, tile, part * count), out_...  1.43 us
    pallas_call x1, Pallas kernels, rounded(): pl.pallas_call(functools.partial(round_kernel, pieces), out_shape=[shape(...  1.26 us
  transfers between devices with their start and end apart: 10, of which 6 were waited for; matrix products, arithmetic and copies ran while one was open for 0% of the time, Pallas kernels for 33%

profile of v5, /device:TPU:0, one launch (start us, length us, event | category | flops | bytes accessed | tf_op | source)
XLA Modules:
  0.0 45.3 jit_solution(3896722822635080618)
XLA Ops:
  0.6 1.3 %rounded.1 = (bf16[2048,128]{1,0:T(8,128)(2,1)S(1)}, bf16[2048,128]{1,0:T(8,128)(2,1)S(1)}) custom-call(f32[2048,128]{1,0:T(8,128)} %bitcast.19), custom_call_target="tpu_custom_call" | custom-call | bytes 2097152 | tf_op jit(solution)/shard_map/rounded/pallas_call | solution.py:106
  1.9 4.1 %collective-permute-start.2 = (bf16[2048,128]{1,0:T(8,128)(2,1)S(1)}, bf16[2048,128]{1,0:T(8,128)(2,1)S(1)}, u32[]{:S(2)}, u32[]{:S(2)}) collective-permute-start(bf16[2048,128]{1,0:T(8,128)(2,1)S(1)} %get-tuple-element.31), channel_id=1, source_target_pairs={{0,2},{1,3},{2,0},{3,1},{4,6},{5,7},{6,4},{7,5},{8,10},{9,11},{10,... | collective-permute-start | bytes 1572872 | tf_op jit(solution)/shard_map/ppermute | solution.py:62
  6.0 1.6 %collective-permute-start.6 = (bf16[2048,128]{1,0:T(8,128)(2,1)S(1)}, bf16[2048,128]{1,0:T(8,128)(2,1)S(1)}, u32[]{:S(2)}, u32[]{:S(2)}) collective-permute-start(bf16[2048,128]{1,0:T(8,128)(2,1)S(1)} %get-tuple-element.34.refs_5_), channel_id=1, source_target_pairs={{0,1},{1,0},{2,3},{3,2},{4,5},{5,4},{6,7},{7,6},{8,9},{9,8},{10,11... | collective-permute-start | bytes 1572872 | tf_op jit(solution)/shard_map/ppermute | solution.py:62
  7.6 0.0 collective-permute-start.4
  7.6 1.1 %prepare.1 = (bf16[1280,128]{1,0:T(8,128)(2,1)S(1)}, bf16[384,128]{1,0:T(8,128)(2,1)S(1)}, bf16[384,128]{1,0:T(8,128)(2,1)S(1)}) custom-call(bf16[768,128]{1,0:T(8,128)(2,1)} %refs_4_.1, f32[1280,128]{1,0:T(8,128)} %bitcast.25), custom_call_target="tpu_custom_call" | custom-call | bytes 983040 | tf_op jit(solution)/shard_map/prepare/pallas_call | solution.py:141
  8.7 1.6 %collective-permute-start.8 = (bf16[1280,128]{1,0:T(8,128)(2,1)S(1)}, bf16[1280,128]{1,0:T(8,128)(2,1)S(1)}, u32[]{:S(2)}, u32[]{:S(2)}) collective-permute-start(bf16[1280,128]{1,0:T(8,128)(2,1)S(1)} %get-tuple-element.45), channel_id=1, source_target_pairs={{0,8},{8,0},{16,24},{24,16},{1,9},{9,1},{17,25},{25,17},{2,10},{10... | collective-permute-start | bytes 983048 | tf_op jit(solution)/shard_map/ppermute | solution.py:435
  10.3 0.7 %collective-permute-start = (bf16[384,128]{1,0:T(8,128)(2,1)S(1)}, bf16[384,128]{1,0:T(8,128)(2,1)S(1)}, u32[]{:S(2)}, u32[]{:S(2)}) collective-permute-start(bf16[384,128]{1,0:T(8,128)(2,1)S(1)} %get-tuple-element.29), channel_id=1, source_target_pairs={{0,0},{1,1},{2,4},{3,5},{4,2},{5,3},{6,6},{7,7},{8,8},{9,9},{10,12... | collective-permute-start | bytes 294920 | tf_op jit(solution)/shard_map/ppermute | solution.py:475
  11.0 0.0 collective-permute-done.4.refs_6_
  11.0 0.5 %collective-permute-start.1 = (bf16[384,128]{1,0:T(8,128)(2,1)S(1)}, bf16[384,128]{1,0:T(8,128)(2,1)S(1)}, u32[]{:S(2)}, u32[]{:S(2)}) collective-permute-start(bf16[384,128]{1,0:T(8,128)(2,1)S(1)} %get-tuple-element.30), channel_id=1, source_target_pairs={{0,1},{1,0},{2,5},{3,4},{4,3},{5,2},{6,7},{7,6},{8,9},{9,8},{10,13... | collective-permute-start | bytes 294920 | tf_op jit(solution)/shard_map/ppermute | solution.py:475
  11.5 10.0 %inner.1 = (f32[2048,128]{1,0:T(8,128)}, f32[2048,128]{1,0:T(8,128)}, f32[2048,128]{1,0:T(8,128)}, f32[768,128]{1,0:T(8,128)S(1)}, bf16[768,128]{1,0:T(8,128)(2,1)S(1)}) custom-call(bf16[1536,2048]{1,0:T(8,128)(2,1)} %refs_0_.1, f32[2048,128]{1,0:T(8,128)} %bitcast.20, f32[2048,128]{1,0:T(8,128)} %bitcast.23, f32[2048,128]{1,0:T(8,128)} %bitcast.24, ...), custom_call_target="tpu_custom_call" | custom-call | flops 1610612736 | bytes 12582912 | tf_op jit(solution)/shard_map/inner/pallas_call | solution.py:258
  21.5 0.0 collective-permute-done.8
  21.5 7.7 %collective-permute-done.2.refs_7_ = bf16[2048,128]{1,0:T(8,128)(2,1)S(1)} collective-permute-done((bf16[2048,128]{1,0:T(8,128)(2,1)S(1)}, bf16[2048,128]{1,0:T(8,128)(2,1)S(1)}, u32[]{:S(2)}, u32[]{:S(2)}) %collective-permute-start.2) | collective-permute-done | bytes 524320 | tf_op jit(solution)/shard_map/ppermute | solution.py:62
  29.3 1.2 %collective-permute-done.6.refs_6_ = bf16[2048,128]{1,0:T(8,128)(2,1)S(1)} collective-permute-done((bf16[2048,128]{1,0:T(8,128)(2,1)S(1)}, bf16[2048,128]{1,0:T(8,128)(2,1)S(1)}, u32[]{:S(2)}, u32[]{:S(2)}) %collective-permute-start.6) | collective-permute-done | bytes 524320 | tf_op jit(solution)/shard_map/ppermute | solution.py:62
  30.5 1.6 %collective-permute-start.7 = (bf16[2048,128]{1,0:T(8,128)(2,1)S(1)}, bf16[2048,128]{1,0:T(8,128)(2,1)S(1)}, u32[]{:S(2)}, u32[]{:S(2)}) collective-permute-start(bf16[2048,128]{1,0:T(8,128)(2,1)S(1)} %collective-permute-done.2.refs_7_), channel_id=1, source_target_pairs={{0,1},{1,0},{2,3},{3,2},{4,5},{5,4},{6,7},{7,6},{8,9},{9,8},{10,11... | collective-permute-start | bytes 1572872 | tf_op jit(solution)/shard_map/ppermute | solution.py:62
  32.1 0.1 add_convert_fusion.sum_ref
  32.2 1.6 %collective-permute-start.9 = (bf16[1280,128]{1,0:T(8,128)(2,1)S(1)}, bf16[1280,128]{1,0:T(8,128)(2,1)S(1)}, u32[]{:S(2)}, u32[]{:S(2)}) collective-permute-start(bf16[1280,128]{1,0:T(8,128)(2,1)S(1)} %add_convert_fusion.sum_ref), channel_id=1, source_target_pairs={{0,16},{8,24},{16,0},{24,8},{1,17},{9,25},{17,1},{25,9},{2,18},{10... | collective-permute-start | bytes 983048 | tf_op jit(solution)/shard_map/ppermute | solution.py:435
  33.8 0.0 collective-permute-start.5
  33.8 0.0 collective-permute-done.refs_0_
  33.8 0.0 collective-permute-done.1.refs_1_
  33.8 0.6 %collective-permute-start.3 = (bf16[768,128]{1,0:T(8,128)(2,1)S(1)}, bf16[768,128]{1,0:T(8,128)(2,1)S(1)}, u32[]{:S(2)}, u32[]{:S(2)}) collective-permute-start(bf16[768,128]{1,0:T(8,128)(2,1)S(1)} %pack.1), channel_id=1, source_target_pairs={{0,4},{4,0},{1,5},{5,1},{2,6},{6,2},{3,7},{7,3},{8,12},{12,8},{9,1... | collective-permute-start | bytes 589832 | tf_op jit(solution)/shard_map/ppermute | solution.py:483
  35.0 0.2 collective-permute-done.5.refs_3_
  35.2 0.3 collective-permute-done.3.refs_2_
  35.5 2.6 %arrived.1 = (f32[384,2048]{1,0:T(8,128)S(1)}, bf16[384,128]{1,0:T(8,128)(2,1)S(1)}, f32[1280,128]{1,0:T(8,128)S(1)}, f32[1280,128]{1,0:T(8,128)S(1)}, bf16[768,128]{1,0:T(8,128)(2,1)}) custom-call(bf16[384,128]{1,0:T(8,128)(2,1)S(1)} %collective-permute-done.refs_0_, bf16[384,128]{1,0:T(8,128)(2,1)S(1)} %collective-permute-done.1.refs_1_, ...), custom_call_target="tpu_custom_call" | custom-call | flops 603979776 | bytes 3145728 | tf_op jit(solution)/shard_map/arrived/pallas_call | solution.py:348
  38.1 1.9 %collective-permute-done.9.other_ref = bf16[1280,128]{1,0:T(8,128)(2,1)S(1)} collective-permute-done((bf16[1280,128]{1,0:T(8,128)(2,1)S(1)}, bf16[1280,128]{1,0:T(8,128)(2,1)S(1)}, u32[]{:S(2)}, u32[]{:S(2)}) %collective-permute-start.9) | collective-permute-done | bytes 327712 | tf_op jit(solution)/shard_map/ppermute | solution.py:435
  40.0 1.2 %merge.1 = (f32[1280,128]{1,0:T(8,128)}, f32[1280,128]{1,0:T(8,128)}) custom-call(bf16[1280,128]{1,0:T(8,128)(2,1)S(1)} %add_convert_fusion.sum_ref, bf16[1280,128]{1,0:T(8,128)(2,1)S(1)} %collective-permute-done.9.other_ref, f32[1280,128]{1,0:T(8,128)S(1)} %get-tuple-element.47.held_ref, f32[1280,128]{1,0:T(8,128)S(1)} %get-tuple-element.48.prior_ref), custom_call_target="tpu_custom_call" | custom-call | flops 1310720 | bytes 1310720 | tf_op jit(solution)/shard_map/merge/pallas_call | solution.py:445
  41.2 2.6 %collective-permute-done.7.weight_ref = bf16[2048,128]{1,0:T(8,128)(2,1)S(1)} collective-permute-done((bf16[2048,128]{1,0:T(8,128)(2,1)S(1)}, bf16[2048,128]{1,0:T(8,128)(2,1)S(1)}, u32[]{:S(2)}, u32[]{:S(2)}) %collective-permute-start.7) | collective-permute-done | bytes 524320 | tf_op jit(solution)/shard_map/ppermute | solution.py:62
  43.8 1.4 %finish.1 = bf16[384,2048]{1,0:T(8,128)(2,1)} custom-call(f32[384,2048]{1,0:T(8,128)S(1)} %get-tuple-element.38.sum_ref, bf16[384,128]{1,0:T(8,128)(2,1)S(1)} %get-tuple-element.39.block_ref, bf16[2048,128]{1,0:T(8,128)(2,1)S(1)} %collective-permute-done.7.weight_ref), custom_call_target="tpu_custom_call" | custom-call | flops 201326592 | bytes 4718592 | tf_op jit(solution)/shard_map/finish/pallas_call | solution.py:395
  (1 shorter events, 0.0 us)
Async XLA Ops:
  1.9 27.4 %collective-permute-start.2 = (bf16[2048,128]{1,0:T(8,128)(2,1)S(1)}, bf16[2048,128]{1,0:T(8,128)(2,1)S(1)}, u32[]{:S(2)}, u32[]{:S(2)}) collective-permute-start(bf16[2048,128]{1,0:T(8,128)(2,1)S(1)} %get-tuple-element.31), channel_id=1, source_target_pairs={{0,2},{1,3},{2,0},{3,1},{4,6},{5,7},{6,4},{7,5},{8,10},{9,11},{10,... | collective-permute-start | bytes 1572872 | tf_op jit(solution)/shard_map/ppermute | solution.py:62
  6.0 24.5 %collective-permute-start.6 = (bf16[2048,128]{1,0:T(8,128)(2,1)S(1)}, bf16[2048,128]{1,0:T(8,128)(2,1)S(1)}, u32[]{:S(2)}, u32[]{:S(2)}) collective-permute-start(bf16[2048,128]{1,0:T(8,128)(2,1)S(1)} %get-tuple-element.34.refs_5_), channel_id=1, source_target_pairs={{0,1},{1,0},{2,3},{3,2},{4,5},{5,4},{6,7},{7,6},{8,9},{9,8},{10,11... | collective-permute-start | bytes 1572872 | tf_op jit(solution)/shard_map/ppermute | solution.py:62
  7.6 3.4 %collective-permute-start.4 = (bf16[768,128]{1,0:T(8,128)(2,1)}, bf16[768,128]{1,0:T(8,128)(2,1)S(1)}, u32[]{:S(2)}, u32[]{:S(2)}) collective-permute-start(bf16[768,128]{1,0:T(8,128)(2,1)} %refs_4_.1), channel_id=1, source_target_pairs={{0,4},{4,0},{1,5},{5,1},{2,6},{6,2},{3,7},{7,3},{8,12},{12,8},{9,1... | collective-permute-start | bytes 589832 | tf_op jit(solution)/shard_map/ppermute | solution.py:76
  8.7 12.8 %collective-permute-start.8 = (bf16[1280,128]{1,0:T(8,128)(2,1)S(1)}, bf16[1280,128]{1,0:T(8,128)(2,1)S(1)}, u32[]{:S(2)}, u32[]{:S(2)}) collective-permute-start(bf16[1280,128]{1,0:T(8,128)(2,1)S(1)} %get-tuple-element.45), channel_id=1, source_target_pairs={{0,8},{8,0},{16,24},{24,16},{1,9},{9,1},{17,25},{25,17},{2,10},{10... | collective-permute-start | bytes 983048 | tf_op jit(solution)/shard_map/ppermute | solution.py:435
  10.3 23.5 %collective-permute-start = (bf16[384,128]{1,0:T(8,128)(2,1)S(1)}, bf16[384,128]{1,0:T(8,128)(2,1)S(1)}, u32[]{:S(2)}, u32[]{:S(2)}) collective-permute-start(bf16[384,128]{1,0:T(8,128)(2,1)S(1)} %get-tuple-element.29), channel_id=1, source_target_pairs={{0,0},{1,1},{2,4},{3,5},{4,2},{5,3},{6,6},{7,7},{8,8},{9,9},{10,12... | collective-permute-start | bytes 294920 | tf_op jit(solution)/shard_map/ppermute | solution.py:475
  11.0 22.8 %collective-permute-start.1 = (bf16[384,128]{1,0:T(8,128)(2,1)S(1)}, bf16[384,128]{1,0:T(8,128)(2,1)S(1)}, u32[]{:S(2)}, u32[]{:S(2)}) collective-permute-start(bf16[384,128]{1,0:T(8,128)(2,1)S(1)} %get-tuple-element.30), channel_id=1, source_target_pairs={{0,1},{1,0},{2,5},{3,4},{4,3},{5,2},{6,7},{7,6},{8,9},{9,8},{10,13... | collective-permute-start | bytes 294920 | tf_op jit(solution)/shard_map/ppermute | solution.py:475
  30.5 13.3 %collective-permute-start.7 = (bf16[2048,128]{1,0:T(8,128)(2,1)S(1)}, bf16[2048,128]{1,0:T(8,128)(2,1)S(1)}, u32[]{:S(2)}, u32[]{:S(2)}) collective-permute-start(bf16[2048,128]{1,0:T(8,128)(2,1)S(1)} %collective-permute-done.2.refs_7_), channel_id=1, source_target_pairs={{0,1},{1,0},{2,3},{3,2},{4,5},{5,4},{6,7},{7,6},{8,9},{9,8},{10,11... | collective-permute-start | bytes 1572872 | tf_op jit(solution)/shard_map/ppermute | solution.py:62
  32.2 7.8 %collective-permute-start.9 = (bf16[1280,128]{1,0:T(8,128)(2,1)S(1)}, bf16[1280,128]{1,0:T(8,128)(2,1)S(1)}, u32[]{:S(2)}, u32[]{:S(2)}) collective-permute-start(bf16[1280,128]{1,0:T(8,128)(2,1)S(1)} %add_convert_fusion.sum_ref), channel_id=1, source_target_pairs={{0,16},{8,24},{16,0},{24,8},{1,17},{9,25},{17,1},{25,9},{2,18},{10... | collective-permute-start | bytes 983048 | tf_op jit(solution)/shard_map/ppermute | solution.py:435
  33.8 1.4 %collective-permute-start.5 = (bf16[768,128]{1,0:T(8,128)(2,1)S(1)}, bf16[768,128]{1,0:T(8,128)(2,1)S(1)}, u32[]{:S(2)}, u32[]{:S(2)}) collective-permute-start(bf16[768,128]{1,0:T(8,128)(2,1)S(1)} %get-tuple-element.35), channel_id=1, source_target_pairs={{0,4},{4,0},{1,5},{5,1},{2,6},{6,2},{3,7},{7,3},{8,12},{12,8},{9,1... | collective-permute-start | bytes 589832 | tf_op jit(solution)/shard_map/ppermute | solution.py:482
  33.8 1.7 %collective-permute-start.3 = (bf16[768,128]{1,0:T(8,128)(2,1)S(1)}, bf16[768,128]{1,0:T(8,128)(2,1)S(1)}, u32[]{:S(2)}, u32[]{:S(2)}) collective-permute-start(bf16[768,128]{1,0:T(8,128)(2,1)S(1)} %pack.1), channel_id=1, source_target_pairs={{0,4},{4,0},{1,5},{5,1},{2,6},{6,2},{3,7},{7,3},{8,12},{12,8},{9,1... | collective-permute-start | bytes 589832 | tf_op jit(solution)/shard_map/ppermute | solution.py:483

commit v6 on v4

--- a/solution.py
+++ b/solution.py
@@ -82,72 +82,87 @@
     return pairs
 
 
-def prepare_kernel(per_row, weight_hbm, cot_hbm, delta_hbm, low_weight_ref, low_delta_ref, *refs):
+def round_kernel(pieces, source_hbm, out_ref, source_ref, sems):
+    size = source_ref.shape[0] // pieces
+    parts = [pl.ds(i * size, size) for i in range(pieces)]
+    loads = [pltpu.make_async_copy(source_hbm.at[p, :], source_ref.at[p, :], sems.at[i]) for i, p in enumerate(parts)]
+    for load in loads:
+        load.start()
+    for load, part in zip(loads, parts):
+        load.wait()
+        out_ref[part, :] = source_ref[part, :].astype(jnp.bfloat16)
+
+
+def rounded(x):
+    pieces = 2
+    return pl.pallas_call(
+        functools.partial(round_kernel, pieces),
+        out_shape=jax.ShapeDtypeStruct(x.shape, jnp.bfloat16),
+        in_specs=[HBM],
+        out_specs=WHOLE,
+        scratch_shapes=[pltpu.VMEM(x.shape, jnp.float32), pltpu.SemaphoreType.DMA((pieces,))],
+        compiler_params=params(16),
+        cost_estimate=pl.CostEstimate(flops=0, bytes_accessed=6 * x.size, transcendentals=0),
+        name="rounded",
+    )(in_hbm(x))
+
+
+def prepare_kernel(per_row, cot_hbm, delta_hbm, low_delta_ref, *refs):
     chunk_refs = refs[:per_row]
-    weight_ref, delta_ref, sems, chunk_sems = refs[per_row:]
+    delta_ref, sem, chunk_sems = refs[per_row:]
     size = chunk_refs[0].shape[0]
     col = lax.axis_index("col")
-    loads = [
-        pltpu.make_async_copy(weight_hbm, weight_ref, sems.at[0]),
-        pltpu.make_async_copy(delta_hbm, delta_ref, sems.at[1]),
-    ]
+    load = pltpu.make_async_copy(delta_hbm, delta_ref, sem)
+    load.start()
     chunks = []
     for k in range(per_row):
         start = pl.multiple_of(lax.rem(col + k, per_row) * size, size)
         chunks.append(pltpu.make_async_copy(cot_hbm.at[pl.ds(start, size), :], chunk_refs[k], chunk_sems.at[k]))
-    for copy in loads + chunks:
-        copy.start()
-    loads[0].wait()
-    low_weight_ref[...] = weight_ref[...].astype(jnp.bfloat16)
-    loads[1].wait()
+        chunks[-1].start()
+    load.wait()
     low_delta_ref[...] = delta_ref[...].astype(jnp.bfloat16)
     for copy in chunks:
         copy.wait()
 
 
-def prepare(weight, cotangent, delta, per_row):
+def prepare(cotangent, delta, per_row):
     chunk = cotangent.shape[0] // per_row
     shape = lambda *s: jax.ShapeDtypeStruct(s, jnp.bfloat16)
-    outs = [shape(*weight.shape), shape(*delta.shape)] + [shape(chunk, cotangent.shape[1])] * per_row
+    outs = [shape(*delta.shape)] + [shape(chunk, cotangent.shape[1])] * per_row
     got = pl.pallas_call(
         functools.partial(prepare_kernel, per_row),
         out_shape=outs,
-        in_specs=[HBM] * 3,
+        in_specs=[HBM] * 2,
         out_specs=[WHOLE] * len(outs),
         scratch_shapes=[
-            pltpu.VMEM(weight.shape, jnp.float32),
             pltpu.VMEM(delta.shape, jnp.float32),
-            pltpu.SemaphoreType.DMA((2,)),
+            pltpu.SemaphoreType.DMA,
             pltpu.SemaphoreType.DMA((per_row,)),
         ],
         compiler_params=params(16),
-        cost_estimate=pl.CostEstimate(flops=0, bytes_accessed=8 * weight.size, transcendentals=0),
+        cost_estimate=pl.CostEstimate(flops=0, bytes_accessed=6 * delta.size, transcendentals=0),
         name="prepare",
-    )(*map(in_hbm, (weight, cotangent, delta)))
-    return got[0], got[1], got[2:]
-
-
-def pack_kernel(per_row, *refs):
-    block_refs, sum_refs = refs[:per_row], refs[per_row:per_row + (len(refs) - per_row) // 2]
-    out_refs = refs[per_row + len(sum_refs):]
-    size, part = block_refs[0].shape[0], sum_refs[0].shape[0]
-    for out_ref, sum_ref in zip(out_refs, sum_refs):
-        for k in range(per_row):
-            out_ref[pl.ds(k * size, size), :] = block_refs[k][...]
-        out_ref[pl.ds(part, part), :] = sum_ref[...]
-
-
-def pack(blocks, sends):
-    part, width = sends[0].shape
+    )(*map(in_hbm, (cotangent, delta)))
+    return got[0], got[1:]
+
+
+def pack_kernel(*refs):
+    size = refs[0].shape[0]
+    for k, block_ref in enumerate(refs[:-1]):
+        refs[-1][pl.ds(k * size, size), :] = block_ref[...]
+
+
+def pack(blocks):
+    size, width = blocks[0].shape
     return pl.pallas_call(
-        functools.partial(pack_kernel, len(blocks)),
-        out_shape=[jax.ShapeDtypeStruct((2 * part, width), jnp.bfloat16)] * len(sends),
-        in_specs=[WHOLE] * (len(blocks) + len(sends)),
-        out_specs=[WHOLE] * len(sends),
+        pack_kernel,
+        out_shape=jax.ShapeDtypeStruct((len(blocks) * size, width), jnp.bfloat16),
+        in_specs=[WHOLE] * len(blocks),
+        out_specs=WHOLE,
         compiler_params=params(16),
-        cost_estimate=pl.CostEstimate(flops=0, bytes_accessed=8 * part * width, transcendentals=0),
+        cost_estimate=pl.CostEstimate(flops=0, bytes_accessed=4 * len(blocks) * size * width, transcendentals=0),
         name="pack",
-    )(*blocks, *sends)
+    )(*blocks)
 
 
 def inner_kernel(rows, steps, *refs):
@@ -263,6 +278,8 @@
 def arrived_kernel(rows, cols, tile, *refs):
     per_row = cols // rows
     block_refs, message_refs = refs[:per_row], refs[per_row:per_row + rows - 1]
+    refs = refs[:per_row] + refs[per_row + rows - 1:]
+    sum_refs = refs[per_row:per_row + rows - 1]
     own_ref = refs[per_row + rows - 1]
     weight_refs = refs[per_row + rows:per_row + rows + cols - 1]
     slot_ref, global_hbm, moment_hbm, sum_ref, last_ref, held_ref, prior_ref, keys_values_hbm = refs[-14:-6]
@@ -276,8 +293,8 @@
         load.start()
     size, part = block_refs[0].shape[0], own_ref.shape[0]
     total = own_ref[...]
-    for message_ref in message_refs:
-        total += message_ref[pl.ds(part, part), :].astype(jnp.float32)
+    for other_ref in sum_refs:
+        total += other_ref[...].astype(jnp.float32)
     keys_values_ref[...] = total.astype(jnp.bfloat16)
     store = pltpu.make_async_copy(keys_values_ref, keys_values_hbm, sem)
     store.start()
@@ -307,7 +324,7 @@
     store.wait()
 
 
-def arrived(blocks, messages, own, weights, cols, global_params, outer_moment, group_slot):
+def arrived(blocks, messages, sums, own, weights, cols, global_params, outer_moment, group_slot):
     rows, per_row = len(messages) + 1, len(blocks)
     size, width = blocks[0].shape
     depth = weights[0].shape[0]
@@ -321,7 +338,7 @@
             held,
             jax.ShapeDtypeStruct(own.shape, jnp.bfloat16),
         ],
-        in_specs=[WHOLE] * (per_row + rows + cols - 1) + [pl.BlockSpec(memory_space=pltpu.SMEM), HBM, HBM],
+        in_specs=[WHOLE] * (per_row + 2 * rows - 1 + cols - 1) + [pl.BlockSpec(memory_space=pltpu.SMEM), HBM, HBM],
         out_specs=[WHOLE] * 4 + [HBM],
         scratch_shapes=[
             pltpu.VMEM((cols, size, width), jnp.bfloat16),
@@ -337,7 +354,7 @@
         ),
         name="arrived",
     )(
-        *blocks, *messages, own, *weights, group_slot, in_hbm(interleaved(global_params)), in_hbm(interleaved(outer_moment))
+        *blocks, *messages, *sums, own, *weights, group_slot, in_hbm(interleaved(global_params)), in_hbm(interleaved(outer_moment))
     )
 
 
@@ -433,7 +450,8 @@
     replicas = lax.axis_size("rep")
     per_row = cols // rows
     cots = shifted(cotangent, "row")
-    low_weight, low, chunks = prepare(weight[0], cotangent, outer_delta.reshape(-1, LANES), per_row)
+    low_weight = rounded(weight[0])
+    low, chunks = prepare(cotangent, outer_delta.reshape(-1, LANES), per_row)
     received = [lax.ppermute(chunks[k], ("row", "col"), chunk_pairs(rows, cols, per_row, k)) for k in range(per_row)]
     (new_weight, new_first, new_second), own, sends = inner(
         tokens, weight[0], first_moment[0], second_moment[0], cots, low_weight
@@ -441,9 +459,10 @@
     weights = gather_offsets(low_weight, "col", sends)
     low, other = outer_sums(low, "rep", (sends, weights[1], weights[cols // 2]))
     received, _ = after(received, weights[cols // 2])
-    messages = [lax.ppermute(m, "row", shift_pairs(rows, k + 1)) for k, m in enumerate(pack(received, sends))]
+    sums = [lax.ppermute(m, "row", shift_pairs(rows, k + 1)) for k, m in enumerate(sends)]
+    messages = [lax.ppermute(pack(received), "row", shift_pairs(rows, k)) for k in range(1, rows)]
     total, block, held, prior, keys_values = arrived(
-        received, messages, own, weights[:-1], cols, global_params, outer_moment, group_slot
+        received, messages, sums, own, weights[:-1], cols, global_params, outer_moment, group_slot
     )
     new_global, new_outer = merge(low, other, held, prior, replicas)
     last, _ = after(weights[-1], (new_outer, total))

time: 46.4 us -> 45.5 us (0.981)
  waiting for transfers between devices: 14.9 us -> 13.7 us
  Pallas kernels: 16.5 us -> 17.7 us
  starting transfers between devices: 13.3 us -> 12.4 us
    ppermute x2, waiting for transfers between devices: 5.13 us -> 2.92 us  [outer_sums(): other = lax.ppermute(low, axis, swap_pairs(n, bit))]
    ppermute x1, starting transfers between devices: 1.7 us -> 0.01 us  [on_device(): lax.ppermute(m, 'row', shift_pairs(rows, k + 1))]
    ppermute x3, waiting for transfers between devices: 8.94 us -> 10.4 us  [gather_offsets(): have[k ^ bit] = lax.ppermute(have[k], axis, swap_pairs(n, bit))]
    pallas_call x1 -> x2, Pallas kernels: 0.03 us -> 1.3 us  [the longest x1 1.28 us: rounded(): pl.pallas_call(functools.partial(round_kernel, pieces), out_shape=jax.Sha...]
    ppermute x0 -> x1, starting transfers between devices: none -> 0.79 us  [on_device(): lax.ppermute(pack(received), 'row', shift_pairs(rows, k))]
    ppermute x2, waiting for transfers between devices: 0.78 us -> 0.01 us  [on_device(): lax.ppermute(chunks[k], ('row', 'col'), chunk_pairs(rows, cols, per_row, k))]
  transfers between devices with their start and end apart: 9 -> 10, of which waited for: 3 -> 4; matrix products, arithmetic and copies ran while one was open for 0% -> 0% of each run, Pallas kernels for 29% -> 33%
where the time goes in v6:
time: 45.5 us; the launch traced here: 45.3 us
  Pallas kernels  17.7 us (39%)
  waiting for transfers between devices  13.7 us (30%)
  starting transfers between devices  12.4 us (27%)
  between operations  1.38 us (3%)
    ppermute x3, waiting for transfers between devices, gather_offsets(): have[k ^ bit] = lax.ppermute(have[k], axis, swap_pairs(n, bit))  10.4 us
    pallas_call x1, Pallas kernels, inner(): pl.pallas_call(functools.partial(inner_kernel, rows, steps), in_specs=[HB...  10 us
    ppermute x3, starting transfers between devices, gather_offsets(): have[k ^ bit] = lax.ppermute(have[k], axis, swap_pairs(n, bit))  7.35 us
    ppermute x2, starting transfers between devices, outer_sums(): other = lax.ppermute(low, axis, swap_pairs(n, bit))  3.14 us
    ppermute x2, waiting for transfers between devices, outer_sums(): other = lax.ppermute(low, axis, swap_pairs(n, bit))  2.92 us
    pallas_call x1, Pallas kernels, arrived(): pl.pallas_call(functools.partial(arrived_kernel, rows, cols, min(512, dep...  2.57 us
    pallas_call x1, Pallas kernels, finish(): pl.pallas_call(functools.partial(finish_kernel, tile), out_shape=jax.Shap...  1.43 us
    pallas_call x1, Pallas kernels, rounded(): pl.pallas_call(functools.partial(round_kernel, pieces), out_shape=jax.Sha...  1.28 us
  transfers between devices with their start and end apart: 10, of which 4 were waited for; matrix products, arithmetic and copies ran while one was open for 0% of the time, Pallas kernels for 33%

profile of v6, /device:TPU:0, one launch (start us, length us, event | category | flops | bytes accessed | tf_op | source)
XLA Modules:
  0.0 45.3 jit_solution(12552786044496940305)
XLA Ops:
  0.6 0.0 copy-start
  0.6 1.3 %rounded.1.refs_5_ = bf16[2048,128]{1,0:T(8,128)(2,1)S(1)} custom-call(f32[2048,128]{1,0:T(8,128)} %bitcast.19), custom_call_target="tpu_custom_call" | custom-call | bytes 1572864 | tf_op jit(solution)/shard_map/rounded/pallas_call | solution.py:98
  1.9 4.1 %collective-permute-start.2 = (bf16[2048,128]{1,0:T(8,128)(2,1)S(1)}, bf16[2048,128]{1,0:T(8,128)(2,1)S(1)}, u32[]{:S(2)}, u32[]{:S(2)}) collective-permute-start(bf16[2048,128]{1,0:T(8,128)(2,1)S(1)} %rounded.1.refs_5_), channel_id=1, source_target_pairs={{0,2},{1,3},{2,0},{3,1},{4,6},{5,7},{6,4},{7,5},{8,10},{9,11},{10,... | collective-permute-start | bytes 1572872 | tf_op jit(solution)/shard_map/ppermute | solution.py:60
  6.0 1.6 %collective-permute-start.6 = (bf16[2048,128]{1,0:T(8,128)(2,1)S(1)}, bf16[2048,128]{1,0:T(8,128)(2,1)S(1)}, u32[]{:S(2)}, u32[]{:S(2)}) collective-permute-start(bf16[2048,128]{1,0:T(8,128)(2,1)S(1)} %rounded.1.refs_5_), channel_id=1, source_target_pairs={{0,1},{1,0},{2,3},{3,2},{4,5},{5,4},{6,7},{7,6},{8,9},{9,8},{10,11... | collective-permute-start | bytes 1572872 | tf_op jit(solution)/shard_map/ppermute | solution.py:60
  7.6 0.0 copy-done
  7.6 0.0 collective-permute-start.3
  7.6 1.1 %prepare.1 = (bf16[1280,128]{1,0:T(8,128)(2,1)S(1)}, bf16[384,128]{1,0:T(8,128)(2,1)S(1)}, bf16[384,128]{1,0:T(8,128)(2,1)S(1)}) custom-call(bf16[768,128]{1,0:T(8,128)(2,1)} %refs_4_.1, f32[1280,128]{1,0:T(8,128)} %bitcast.25), custom_call_target="tpu_custom_call" | custom-call | bytes 983040 | tf_op jit(solution)/shard_map/prepare/pallas_call | solution.py:132
  8.8 1.6 %collective-permute-start.8 = (bf16[1280,128]{1,0:T(8,128)(2,1)S(1)}, bf16[1280,128]{1,0:T(8,128)(2,1)S(1)}, u32[]{:S(2)}, u32[]{:S(2)}) collective-permute-start(bf16[1280,128]{1,0:T(8,128)(2,1)S(1)} %get-tuple-element.37), channel_id=1, source_target_pairs={{0,8},{8,0},{16,24},{24,16},{1,9},{9,1},{17,25},{25,17},{2,10},{10... | collective-permute-start | bytes 983048 | tf_op jit(solution)/shard_map/ppermute | solution.py:415
  10.3 0.7 %collective-permute-start = (bf16[384,128]{1,0:T(8,128)(2,1)S(1)}, bf16[384,128]{1,0:T(8,128)(2,1)S(1)}, u32[]{:S(2)}, u32[]{:S(2)}) collective-permute-start(bf16[384,128]{1,0:T(8,128)(2,1)S(1)} %get-tuple-element.27), channel_id=1, source_target_pairs={{0,0},{1,1},{2,4},{3,5},{4,2},{5,3},{6,6},{7,7},{8,8},{9,9},{10,12... | collective-permute-start | bytes 294920 | tf_op jit(solution)/shard_map/ppermute | solution.py:455
  11.0 0.0 collective-permute-done.3.refs_6_
  11.0 0.5 %collective-permute-start.1 = (bf16[384,128]{1,0:T(8,128)(2,1)S(1)}, bf16[384,128]{1,0:T(8,128)(2,1)S(1)}, u32[]{:S(2)}, u32[]{:S(2)}) collective-permute-start(bf16[384,128]{1,0:T(8,128)(2,1)S(1)} %get-tuple-element.28), channel_id=1, source_target_pairs={{0,1},{1,0},{2,5},{3,4},{4,3},{5,2},{6,7},{7,6},{8,9},{9,8},{10,13... | collective-permute-start | bytes 294920 | tf_op jit(solution)/shard_map/ppermute | solution.py:455
  11.5 10.0 %inner.1 = (f32[2048,128]{1,0:T(8,128)}, f32[2048,128]{1,0:T(8,128)}, f32[2048,128]{1,0:T(8,128)}, f32[768,128]{1,0:T(8,128)S(1)}, bf16[768,128]{1,0:T(8,128)(2,1)S(1)}) custom-call(bf16[1536,2048]{1,0:T(8,128)(2,1)} %refs_0_.1, f32[2048,128]{1,0:T(8,128)} %bitcast.20, f32[2048,128]{1,0:T(8,128)} %bitcast.23, f32[2048,128]{1,0:T(8,128)} %bitcast.24, ...), custom_call_target="tpu_custom_call" | custom-call | flops 1610612736 | bytes 12582912 | tf_op jit(solution)/shard_map/inner/pallas_call | solution.py:249
  21.6 7.7 %collective-permute-done.2.refs_7_ = bf16[2048,128]{1,0:T(8,128)(2,1)S(1)} collective-permute-done((bf16[2048,128]{1,0:T(8,128)(2,1)S(1)}, bf16[2048,128]{1,0:T(8,128)(2,1)S(1)}, u32[]{:S(2)}, u32[]{:S(2)}) %collective-permute-start.2) | collective-permute-done | bytes 524320 | tf_op jit(solution)/shard_map/ppermute | solution.py:60
  29.3 1.7 %collective-permute-start.7 = (bf16[2048,128]{1,0:T(8,128)(2,1)S(1)}, bf16[2048,128]{1,0:T(8,128)(2,1)S(1)}, u32[]{:S(2)}, u32[]{:S(2)}) collective-permute-start(bf16[2048,128]{1,0:T(8,128)(2,1)S(1)} %collective-permute-done.2.refs_7_), channel_id=1, source_target_pairs={{0,1},{1,0},{2,3},{3,2},{4,5},{5,4},{6,7},{7,6},{8,9},{9,8},{10,11... | collective-permute-start | bytes 1572872 | tf_op jit(solution)/shard_map/ppermute | solution.py:60
  31.0 0.0 collective-permute-done.8
  31.0 0.0 collective-permute-done.6.refs_6_
  31.0 0.1 add_convert_fusion.sum_ref
  31.1 1.6 %collective-permute-start.9 = (bf16[1280,128]{1,0:T(8,128)(2,1)S(1)}, bf16[1280,128]{1,0:T(8,128)(2,1)S(1)}, u32[]{:S(2)}, u32[]{:S(2)}) collective-permute-start(bf16[1280,128]{1,0:T(8,128)(2,1)S(1)} %add_convert_fusion.sum_ref), channel_id=1, source_target_pairs={{0,16},{8,24},{16,0},{24,8},{1,17},{9,25},{17,1},{25,9},{2,18},{10... | collective-permute-start | bytes 983048 | tf_op jit(solution)/shard_map/ppermute | solution.py:415
  32.7 0.0 collective-permute-start.5
  32.7 0.0 collective-permute-done.refs_0_
  32.7 0.0 collective-permute-done.1.refs_1_
  32.7 0.8 %collective-permute-start.4 = (bf16[768,128]{1,0:T(8,128)(2,1)S(1)}, bf16[768,128]{1,0:T(8,128)(2,1)S(1)}, u32[]{:S(2)}, u32[]{:S(2)}) collective-permute-start(bf16[768,128]{1,0:T(8,128)(2,1)S(1)} %pack.1), channel_id=1, source_target_pairs={{0,4},{4,0},{1,5},{5,1},{2,6},{6,2},{3,7},{7,3},{8,12},{12,8},{9,1... | collective-permute-start | bytes 589832 | tf_op jit(solution)/shard_map/ppermute | solution.py:463
  34.1 0.0 collective-permute-done.5.refs_3_
  34.1 0.4 collective-permute-done.4.refs_2_
  34.5 2.6 %arrived.1 = (f32[384,2048]{1,0:T(8,128)S(1)}, bf16[384,128]{1,0:T(8,128)(2,1)S(1)}, f32[1280,128]{1,0:T(8,128)S(1)}, f32[1280,128]{1,0:T(8,128)S(1)}, bf16[768,128]{1,0:T(8,128)(2,1)}) custom-call(bf16[384,128]{1,0:T(8,128)(2,1)S(1)} %collective-permute-done.refs_0_, bf16[384,128]{1,0:T(8,128)(2,1)S(1)} %collective-permute-done.1.refs_1_, ...), custom_call_target="tpu_custom_call" | custom-call | flops 603979776 | bytes 3145728 | tf_op jit(solution)/shard_map/arrived/pallas_call | solution.py:332
  37.1 2.9 %collective-permute-done.9.other_ref = bf16[1280,128]{1,0:T(8,128)(2,1)S(1)} collective-permute-done((bf16[1280,128]{1,0:T(8,128)(2,1)S(1)}, bf16[1280,128]{1,0:T(8,128)(2,1)S(1)}, u32[]{:S(2)}, u32[]{:S(2)}) %collective-permute-start.9) | collective-permute-done | bytes 327712 | tf_op jit(solution)/shard_map/ppermute | solution.py:415
  40.0 1.2 %merge.1 = (f32[1280,128]{1,0:T(8,128)}, f32[1280,128]{1,0:T(8,128)}) custom-call(bf16[1280,128]{1,0:T(8,128)(2,1)S(1)} %add_convert_fusion.sum_ref, bf16[1280,128]{1,0:T(8,128)(2,1)S(1)} %collective-permute-done.9.other_ref, f32[1280,128]{1,0:T(8,128)S(1)} %get-tuple-element.39.held_ref, f32[1280,128]{1,0:T(8,128)S(1)} %get-tuple-element.40.prior_ref), custom_call_target="tpu_custom_call" | custom-call | flops 1310720 | bytes 1310720 | tf_op jit(solution)/shard_map/merge/pallas_call | solution.py:425
  41.2 2.6 %collective-permute-done.7.weight_ref = bf16[2048,128]{1,0:T(8,128)(2,1)S(1)} collective-permute-done((bf16[2048,128]{1,0:T(8,128)(2,1)S(1)}, bf16[2048,128]{1,0:T(8,128)(2,1)S(1)}, u32[]{:S(2)}, u32[]{:S(2)}) %collective-permute-start.7) | collective-permute-done | bytes 524320 | tf_op jit(solution)/shard_map/ppermute | solution.py:60
  43.9 1.4 %finish.1 = bf16[384,2048]{1,0:T(8,128)(2,1)} custom-call(f32[384,2048]{1,0:T(8,128)S(1)} %get-tuple-element.35.sum_ref, bf16[384,128]{1,0:T(8,128)(2,1)S(1)} %get-tuple-element.36.block_ref, bf16[2048,128]{1,0:T(8,128)(2,1)S(1)} %collective-permute-done.7.weight_ref), custom_call_target="tpu_custom_call" | custom-call | flops 201326592 | bytes 4718592 | tf_op jit(solution)/shard_map/finish/pallas_call | solution.py:376
  (1 shorter events, 0.0 us)
Async XLA Ops:
  0.6 7.0 %copy-start = (bf16[768,128]{1,0:T(8,128)(2,1)S(1)}, bf16[768,128]{1,0:T(8,128)(2,1)}, u32[]{:S(2)}) copy-start(bf16[768,128]{1,0:T(8,128)(2,1)} %refs_4_.1) | copy-start | bytes 589828
  1.9 27.4 %collective-permute-start.2 = (bf16[2048,128]{1,0:T(8,128)(2,1)S(1)}, bf16[2048,128]{1,0:T(8,128)(2,1)S(1)}, u32[]{:S(2)}, u32[]{:S(2)}) collective-permute-start(bf16[2048,128]{1,0:T(8,128)(2,1)S(1)} %rounded.1.refs_5_), channel_id=1, source_target_pairs={{0,2},{1,3},{2,0},{3,1},{4,6},{5,7},{6,4},{7,5},{8,10},{9,11},{10,... | collective-permute-start | bytes 1572872 | tf_op jit(solution)/shard_map/ppermute | solution.py:60
  6.0 24.9 %collective-permute-start.6 = (bf16[2048,128]{1,0:T(8,128)(2,1)S(1)}, bf16[2048,128]{1,0:T(8,128)(2,1)S(1)}, u32[]{:S(2)}, u32[]{:S(2)}) collective-permute-start(bf16[2048,128]{1,0:T(8,128)(2,1)S(1)} %rounded.1.refs_5_), channel_id=1, source_target_pairs={{0,1},{1,0},{2,3},{3,2},{4,5},{5,4},{6,7},{7,6},{8,9},{9,8},{10,11... | collective-permute-start | bytes 1572872 | tf_op jit(solution)/shard_map/ppermute | solution.py:60
  7.6 3.4 %collective-permute-start.3 = (bf16[768,128]{1,0:T(8,128)(2,1)S(1)}, bf16[768,128]{1,0:T(8,128)(2,1)S(1)}, u32[]{:S(2)}, u32[]{:S(2)}) collective-permute-start(bf16[768,128]{1,0:T(8,128)(2,1)S(1)} %copy-done), channel_id=1, source_target_pairs={{0,4},{4,0},{1,5},{5,1},{2,6},{6,2},{3,7},{7,3},{8,12},{12,8},{9,1... | collective-permute-start | bytes 589832 | tf_op jit(solution)/shard_map/ppermute | solution.py:74
  8.8 22.2 %collective-permute-start.8 = (bf16[1280,128]{1,0:T(8,128)(2,1)S(1)}, bf16[1280,128]{1,0:T(8,128)(2,1)S(1)}, u32[]{:S(2)}, u32[]{:S(2)}) collective-permute-start(bf16[1280,128]{1,0:T(8,128)(2,1)S(1)} %get-tuple-element.37), channel_id=1, source_target_pairs={{0,8},{8,0},{16,24},{24,16},{1,9},{9,1},{17,25},{25,17},{2,10},{10... | collective-permute-start | bytes 983048 | tf_op jit(solution)/shard_map/ppermute | solution.py:415
  10.3 22.3 %collective-permute-start = (bf16[384,128]{1,0:T(8,128)(2,1)S(1)}, bf16[384,128]{1,0:T(8,128)(2,1)S(1)}, u32[]{:S(2)}, u32[]{:S(2)}) collective-permute-start(bf16[384,128]{1,0:T(8,128)(2,1)S(1)} %get-tuple-element.27), channel_id=1, source_target_pairs={{0,0},{1,1},{2,4},{3,5},{4,2},{5,3},{6,6},{7,7},{8,8},{9,9},{10,12... | collective-permute-start | bytes 294920 | tf_op jit(solution)/shard_map/ppermute | solution.py:455
  11.0 21.7 %collective-permute-start.1 = (bf16[384,128]{1,0:T(8,128)(2,1)S(1)}, bf16[384,128]{1,0:T(8,128)(2,1)S(1)}, u32[]{:S(2)}, u32[]{:S(2)}) collective-permute-start(bf16[384,128]{1,0:T(8,128)(2,1)S(1)} %get-tuple-element.28), channel_id=1, source_target_pairs={{0,1},{1,0},{2,5},{3,4},{4,3},{5,2},{6,7},{7,6},{8,9},{9,8},{10,13... | collective-permute-start | bytes 294920 | tf_op jit(solution)/shard_map/ppermute | solution.py:455
  29.3 14.6 %collective-permute-start.7 = (bf16[2048,128]{1,0:T(8,128)(2,1)S(1)}, bf16[2048,128]{1,0:T(8,128)(2,1)S(1)}, u32[]{:S(2)}, u32[]{:S(2)}) collective-permute-start(bf16[2048,128]{1,0:T(8,128)(2,1)S(1)} %collective-permute-done.2.refs_7_), channel_id=1, source_target_pairs={{0,1},{1,0},{2,3},{3,2},{4,5},{5,4},{6,7},{7,6},{8,9},{9,8},{10,11... | collective-permute-start | bytes 1572872 | tf_op jit(solution)/shard_map/ppermute | solution.py:60
  31.1 9.0 %collective-permute-start.9 = (bf16[1280,128]{1,0:T(8,128)(2,1)S(1)}, bf16[1280,128]{1,0:T(8,128)(2,1)S(1)}, u32[]{:S(2)}, u32[]{:S(2)}) collective-permute-start(bf16[1280,128]{1,0:T(8,128)(2,1)S(1)} %add_convert_fusion.sum_ref), channel_id=1, source_target_pairs={{0,16},{8,24},{16,0},{24,8},{1,17},{9,25},{17,1},{25,9},{2,18},{10... | collective-permute-start | bytes 983048 | tf_op jit(solution)/shard_map/ppermute | solution.py:415
  32.7 1.5 %collective-permute-start.5 = (bf16[768,128]{1,0:T(8,128)(2,1)S(1)}, bf16[768,128]{1,0:T(8,128)(2,1)S(1)}, u32[]{:S(2)}, u32[]{:S(2)}) collective-permute-start(bf16[768,128]{1,0:T(8,128)(2,1)S(1)} %get-tuple-element.29), channel_id=1, source_target_pairs={{0,4},{4,0},{1,5},{5,1},{2,6},{6,2},{3,7},{7,3},{8,12},{12,8},{9,1... | collective-permute-start | bytes 589832 | tf_op jit(solution)/shard_map/ppermute | solution.py:462
  32.7 1.9 %collective-permute-start.4 = (bf16[768,128]{1,0:T(8,128)(2,1)S(1)}, bf16[768,128]{1,0:T(8,128)(2,1)S(1)}, u32[]{:S(2)}, u32[]{:S(2)}) collective-permute-start(bf16[768,128]{1,0:T(8,128)(2,1)S(1)} %pack.1), channel_id=1, source_target_pairs={{0,4},{4,0},{1,5},{5,1},{2,6},{6,2},{3,7},{7,3},{8,12},{12,8},{9,1... | collective-permute-start | bytes 589832 | tf_op jit(solution)/shard_map/ppermute | solution.py:463

commit v7 on v6

--- a/solution.py
+++ b/solution.py
@@ -320,7 +320,10 @@
     slots = global_ref.shape[0] // count
     for load, source_ref, out_ref in zip(loads, (global_ref, moment_ref), (held_ref, prior_ref)):
         load.wait()
-        out_ref[...] = source_ref[pl.ds(slot, count, stride=slots), :]
+        picked = source_ref[pl.ds(0, count, stride=slots), :]
+        for i in range(1, slots):
+            picked = jnp.where(slot == i, source_ref[pl.ds(i, count, stride=slots), :], picked)
+        out_ref[...] = picked
     store.wait()
 
 

time: 45.5 us -> 45.5 us (level)
  no operation moved by 1% of the time
where the time goes in v7:
time: 45.5 us; the launch traced here: 45.3 us
  Pallas kernels  17.7 us (39%)
  waiting for transfers between devices  13.7 us (30%)
  starting transfers between devices  12.4 us (27%)
  between operations  1.38 us (3%)
    ppermute x3, waiting for transfers between devices, gather_offsets(): have[k ^ bit] = lax.ppermute(have[k], axis, swap_pairs(n, bit))  10.4 us
    pallas_call x1, Pallas kernels, inner(): pl.pallas_call(functools.partial(inner_kernel, rows, steps), in_specs=[HB...  10 us
    ppermute x3, starting transfers between devices, gather_offsets(): have[k ^ bit] = lax.ppermute(have[k], axis, swap_pairs(n, bit))  7.35 us
    ppermute x2, starting transfers between devices, outer_sums(): other = lax.ppermute(low, axis, swap_pairs(n, bit))  3.14 us
    ppermute x2, waiting for transfers between devices, outer_sums(): other = lax.ppermute(low, axis, swap_pairs(n, bit))  2.88 us
    pallas_call x1, Pallas kernels, arrived(): pl.pallas_call(functools.partial(arrived_kernel, rows, cols, min(512, dep...  2.61 us
    pallas_call x1, Pallas kernels, finish(): pl.pallas_call(functools.partial(finish_kernel, tile), out_shape=jax.Shap...  1.43 us
    pallas_call x1, Pallas kernels, rounded(): pl.pallas_call(functools.partial(round_kernel, pieces), out_shape=jax.Sha...  1.28 us
  transfers between devices with their start and end apart: 10, of which 4 were waited for; matrix products, arithmetic and copies ran while one was open for 0% of the time, Pallas kernels for 33%

profile of v7, /device:TPU:0, one launch (start us, length us, event | category | flops | bytes accessed | tf_op | source)
XLA Modules:
  0.0 45.3 jit_solution(2966243599275189572)
XLA Ops:
  0.6 0.0 copy-start
  0.6 1.3 %rounded.1.refs_5_ = bf16[2048,128]{1,0:T(8,128)(2,1)S(1)} custom-call(f32[2048,128]{1,0:T(8,128)} %bitcast.19), custom_call_target="tpu_custom_call" | custom-call | bytes 1572864 | tf_op jit(solution)/shard_map/rounded/pallas_call | solution.py:98
  1.9 4.1 %collective-permute-start.2 = (bf16[2048,128]{1,0:T(8,128)(2,1)S(1)}, bf16[2048,128]{1,0:T(8,128)(2,1)S(1)}, u32[]{:S(2)}, u32[]{:S(2)}) collective-permute-start(bf16[2048,128]{1,0:T(8,128)(2,1)S(1)} %rounded.1.refs_5_), channel_id=1, source_target_pairs={{0,2},{1,3},{2,0},{3,1},{4,6},{5,7},{6,4},{7,5},{8,10},{9,11},{10,... | collective-permute-start | bytes 1572872 | tf_op jit(solution)/shard_map/ppermute | solution.py:60
  6.0 1.6 %collective-permute-start.6 = (bf16[2048,128]{1,0:T(8,128)(2,1)S(1)}, bf16[2048,128]{1,0:T(8,128)(2,1)S(1)}, u32[]{:S(2)}, u32[]{:S(2)}) collective-permute-start(bf16[2048,128]{1,0:T(8,128)(2,1)S(1)} %rounded.1.refs_5_), channel_id=1, source_target_pairs={{0,1},{1,0},{2,3},{3,2},{4,5},{5,4},{6,7},{7,6},{8,9},{9,8},{10,11... | collective-permute-start | bytes 1572872 | tf_op jit(solution)/shard_map/ppermute | solution.py:60
  7.6 0.0 copy-done
  7.6 0.0 collective-permute-start.3
  7.6 1.1 %prepare.1 = (bf16[1280,128]{1,0:T(8,128)(2,1)S(1)}, bf16[384,128]{1,0:T(8,128)(2,1)S(1)}, bf16[384,128]{1,0:T(8,128)(2,1)S(1)}) custom-call(bf16[768,128]{1,0:T(8,128)(2,1)} %refs_4_.1, f32[1280,128]{1,0:T(8,128)} %bitcast.25), custom_call_target="tpu_custom_call" | custom-call | bytes 983040 | tf_op jit(solution)/shard_map/prepare/pallas_call | solution.py:132
  8.8 1.6 %collective-permute-start.8 = (bf16[1280,128]{1,0:T(8,128)(2,1)S(1)}, bf16[1280,128]{1,0:T(8,128)(2,1)S(1)}, u32[]{:S(2)}, u32[]{:S(2)}) collective-permute-start(bf16[1280,128]{1,0:T(8,128)(2,1)S(1)} %get-tuple-element.37), channel_id=1, source_target_pairs={{0,8},{8,0},{16,24},{24,16},{1,9},{9,1},{17,25},{25,17},{2,10},{10... | collective-permute-start | bytes 983048 | tf_op jit(solution)/shard_map/ppermute | solution.py:418
  10.3 0.7 %collective-permute-start = (bf16[384,128]{1,0:T(8,128)(2,1)S(1)}, bf16[384,128]{1,0:T(8,128)(2,1)S(1)}, u32[]{:S(2)}, u32[]{:S(2)}) collective-permute-start(bf16[384,128]{1,0:T(8,128)(2,1)S(1)} %get-tuple-element.27), channel_id=1, source_target_pairs={{0,0},{1,1},{2,4},{3,5},{4,2},{5,3},{6,6},{7,7},{8,8},{9,9},{10,12... | collective-permute-start | bytes 294920 | tf_op jit(solution)/shard_map/ppermute | solution.py:458
  11.0 0.0 collective-permute-done.3.refs_6_
  11.0 0.5 %collective-permute-start.1 = (bf16[384,128]{1,0:T(8,128)(2,1)S(1)}, bf16[384,128]{1,0:T(8,128)(2,1)S(1)}, u32[]{:S(2)}, u32[]{:S(2)}) collective-permute-start(bf16[384,128]{1,0:T(8,128)(2,1)S(1)} %get-tuple-element.28), channel_id=1, source_target_pairs={{0,1},{1,0},{2,5},{3,4},{4,3},{5,2},{6,7},{7,6},{8,9},{9,8},{10,13... | collective-permute-start | bytes 294920 | tf_op jit(solution)/shard_map/ppermute | solution.py:458
  11.5 10.0 %inner.1 = (f32[2048,128]{1,0:T(8,128)}, f32[2048,128]{1,0:T(8,128)}, f32[2048,128]{1,0:T(8,128)}, f32[768,128]{1,0:T(8,128)S(1)}, bf16[768,128]{1,0:T(8,128)(2,1)S(1)}) custom-call(bf16[1536,2048]{1,0:T(8,128)(2,1)} %refs_0_.1, f32[2048,128]{1,0:T(8,128)} %bitcast.20, f32[2048,128]{1,0:T(8,128)} %bitcast.23, f32[2048,128]{1,0:T(8,128)} %bitcast.24, ...), custom_call_target="tpu_custom_call" | custom-call | flops 1610612736 | bytes 12582912 | tf_op jit(solution)/shard_map/inner/pallas_call | solution.py:249
  21.6 7.7 %collective-permute-done.2.refs_7_ = bf16[2048,128]{1,0:T(8,128)(2,1)S(1)} collective-permute-done((bf16[2048,128]{1,0:T(8,128)(2,1)S(1)}, bf16[2048,128]{1,0:T(8,128)(2,1)S(1)}, u32[]{:S(2)}, u32[]{:S(2)}) %collective-permute-start.2) | collective-permute-done | bytes 524320 | tf_op jit(solution)/shard_map/ppermute | solution.py:60
  29.3 1.7 %collective-permute-start.7 = (bf16[2048,128]{1,0:T(8,128)(2,1)S(1)}, bf16[2048,128]{1,0:T(8,128)(2,1)S(1)}, u32[]{:S(2)}, u32[]{:S(2)}) collective-permute-start(bf16[2048,128]{1,0:T(8,128)(2,1)S(1)} %collective-permute-done.2.refs_7_), channel_id=1, source_target_pairs={{0,1},{1,0},{2,3},{3,2},{4,5},{5,4},{6,7},{7,6},{8,9},{9,8},{10,11... | collective-permute-start | bytes 1572872 | tf_op jit(solution)/shard_map/ppermute | solution.py:60
  31.0 0.0 collective-permute-done.8
  31.0 0.0 collective-permute-done.6.refs_6_
  31.0 0.1 add_convert_fusion.sum_ref
  31.1 1.6 %collective-permute-start.9 = (bf16[1280,128]{1,0:T(8,128)(2,1)S(1)}, bf16[1280,128]{1,0:T(8,128)(2,1)S(1)}, u32[]{:S(2)}, u32[]{:S(2)}) collective-permute-start(bf16[1280,128]{1,0:T(8,128)(2,1)S(1)} %add_convert_fusion.sum_ref), channel_id=1, source_target_pairs={{0,16},{8,24},{16,0},{24,8},{1,17},{9,25},{17,1},{25,9},{2,18},{10... | collective-permute-start | bytes 983048 | tf_op jit(solution)/shard_map/ppermute | solution.py:418
  32.7 0.0 collective-permute-start.5
  32.7 0.0 collective-permute-done.refs_0_
  32.7 0.0 collective-permute-done.1.refs_1_
  32.7 0.8 %collective-permute-start.4 = (bf16[768,128]{1,0:T(8,128)(2,1)S(1)}, bf16[768,128]{1,0:T(8,128)(2,1)S(1)}, u32[]{:S(2)}, u32[]{:S(2)}) collective-permute-start(bf16[768,128]{1,0:T(8,128)(2,1)S(1)} %pack.1), channel_id=1, source_target_pairs={{0,4},{4,0},{1,5},{5,1},{2,6},{6,2},{3,7},{7,3},{8,12},{12,8},{9,1... | collective-permute-start | bytes 589832 | tf_op jit(solution)/shard_map/ppermute | solution.py:466
  34.1 0.0 collective-permute-done.5.refs_3_
  34.1 0.4 collective-permute-done.4.refs_2_
  34.5 2.6 %arrived.1 = (f32[384,2048]{1,0:T(8,128)S(1)}, bf16[384,128]{1,0:T(8,128)(2,1)S(1)}, f32[1280,128]{1,0:T(8,128)S(1)}, f32[1280,128]{1,0:T(8,128)S(1)}, bf16[768,128]{1,0:T(8,128)(2,1)}) custom-call(bf16[384,128]{1,0:T(8,128)(2,1)S(1)} %collective-permute-done.refs_0_, bf16[384,128]{1,0:T(8,128)(2,1)S(1)} %collective-permute-done.1.refs_1_, ...), custom_call_target="tpu_custom_call" | custom-call | flops 603979776 | bytes 3145728 | tf_op jit(solution)/shard_map/arrived/pallas_call | solution.py:335
  37.2 2.9 %collective-permute-done.9.other_ref = bf16[1280,128]{1,0:T(8,128)(2,1)S(1)} collective-permute-done((bf16[1280,128]{1,0:T(8,128)(2,1)S(1)}, bf16[1280,128]{1,0:T(8,128)(2,1)S(1)}, u32[]{:S(2)}, u32[]{:S(2)}) %collective-permute-start.9) | collective-permute-done | bytes 327712 | tf_op jit(solution)/shard_map/ppermute | solution.py:418
  40.0 1.2 %merge.1 = (f32[1280,128]{1,0:T(8,128)}, f32[1280,128]{1,0:T(8,128)}) custom-call(bf16[1280,128]{1,0:T(8,128)(2,1)S(1)} %add_convert_fusion.sum_ref, bf16[1280,128]{1,0:T(8,128)(2,1)S(1)} %collective-permute-done.9.other_ref, f32[1280,128]{1,0:T(8,128)S(1)} %get-tuple-element.39.held_ref, f32[1280,128]{1,0:T(8,128)S(1)} %get-tuple-element.40.prior_ref), custom_call_target="tpu_custom_call" | custom-call | flops 1310720 | bytes 1310720 | tf_op jit(solution)/shard_map/merge/pallas_call | solution.py:428
  41.2 2.6 %collective-permute-done.7.weight_ref = bf16[2048,128]{1,0:T(8,128)(2,1)S(1)} collective-permute-done((bf16[2048,128]{1,0:T(8,128)(2,1)S(1)}, bf16[2048,128]{1,0:T(8,128)(2,1)S(1)}, u32[]{:S(2)}, u32[]{:S(2)}) %collective-permute-start.7) | collective-permute-done | bytes 524320 | tf_op jit(solution)/shard_map/ppermute | solution.py:60
  43.9 1.4 %finish.1 = bf16[384,2048]{1,0:T(8,128)(2,1)} custom-call(f32[384,2048]{1,0:T(8,128)S(1)} %get-tuple-element.35.sum_ref, bf16[384,128]{1,0:T(8,128)(2,1)S(1)} %get-tuple-element.36.block_ref, bf16[2048,128]{1,0:T(8,128)(2,1)S(1)} %collective-permute-done.7.weight_ref), custom_call_target="tpu_custom_call" | custom-call | flops 201326592 | bytes 4718592 | tf_op jit(solution)/shard_map/finish/pallas_call | solution.py:379
  (1 shorter events, 0.0 us)
Async XLA Ops:
  0.6 7.0 %copy-start = (bf16[768,128]{1,0:T(8,128)(2,1)S(1)}, bf16[768,128]{1,0:T(8,128)(2,1)}, u32[]{:S(2)}) copy-start(bf16[768,128]{1,0:T(8,128)(2,1)} %refs_4_.1) | copy-start | bytes 589828
  1.9 27.4 %collective-permute-start.2 = (bf16[2048,128]{1,0:T(8,128)(2,1)S(1)}, bf16[2048,128]{1,0:T(8,128)(2,1)S(1)}, u32[]{:S(2)}, u32[]{:S(2)}) collective-permute-start(bf16[2048,128]{1,0:T(8,128)(2,1)S(1)} %rounded.1.refs_5_), channel_id=1, source_target_pairs={{0,2},{1,3},{2,0},{3,1},{4,6},{5,7},{6,4},{7,5},{8,10},{9,11},{10,... | collective-permute-start | bytes 1572872 | tf_op jit(solution)/shard_map/ppermute | solution.py:60
  6.0 24.9 %collective-permute-start.6 = (bf16[2048,128]{1,0:T(8,128)(2,1)S(1)}, bf16[2048,128]{1,0:T(8,128)(2,1)S(1)}, u32[]{:S(2)}, u32[]{:S(2)}) collective-permute-start(bf16[2048,128]{1,0:T(8,128)(2,1)S(1)} %rounded.1.refs_5_), channel_id=1, source_target_pairs={{0,1},{1,0},{2,3},{3,2},{4,5},{5,4},{6,7},{7,6},{8,9},{9,8},{10,11... | collective-permute-start | bytes 1572872 | tf_op jit(solution)/shard_map/ppermute | solution.py:60
  7.6 3.4 %collective-permute-start.3 = (bf16[768,128]{1,0:T(8,128)(2,1)S(1)}, bf16[768,128]{1,0:T(8,128)(2,1)S(1)}, u32[]{:S(2)}, u32[]{:S(2)}) collective-permute-start(bf16[768,128]{1,0:T(8,128)(2,1)S(1)} %copy-done), channel_id=1, source_target_pairs={{0,4},{4,0},{1,5},{5,1},{2,6},{6,2},{3,7},{7,3},{8,12},{12,8},{9,1... | collective-permute-start | bytes 589832 | tf_op jit(solution)/shard_map/ppermute | solution.py:74
  8.8 22.2 %collective-permute-start.8 = (bf16[1280,128]{1,0:T(8,128)(2,1)S(1)}, bf16[1280,128]{1,0:T(8,128)(2,1)S(1)}, u32[]{:S(2)}, u32[]{:S(2)}) collective-permute-start(bf16[1280,128]{1,0:T(8,128)(2,1)S(1)} %get-tuple-element.37), channel_id=1, source_target_pairs={{0,8},{8,0},{16,24},{24,16},{1,9},{9,1},{17,25},{25,17},{2,10},{10... | collective-permute-start | bytes 983048 | tf_op jit(solution)/shard_map/ppermute | solution.py:418
  10.3 22.3 %collective-permute-start = (bf16[384,128]{1,0:T(8,128)(2,1)S(1)}, bf16[384,128]{1,0:T(8,128)(2,1)S(1)}, u32[]{:S(2)}, u32[]{:S(2)}) collective-permute-start(bf16[384,128]{1,0:T(8,128)(2,1)S(1)} %get-tuple-element.27), channel_id=1, source_target_pairs={{0,0},{1,1},{2,4},{3,5},{4,2},{5,3},{6,6},{7,7},{8,8},{9,9},{10,12... | collective-permute-start | bytes 294920 | tf_op jit(solution)/shard_map/ppermute | solution.py:458
  11.0 21.7 %collective-permute-start.1 = (bf16[384,128]{1,0:T(8,128)(2,1)S(1)}, bf16[384,128]{1,0:T(8,128)(2,1)S(1)}, u32[]{:S(2)}, u32[]{:S(2)}) collective-permute-start(bf16[384,128]{1,0:T(8,128)(2,1)S(1)} %get-tuple-element.28), channel_id=1, source_target_pairs={{0,1},{1,0},{2,5},{3,4},{4,3},{5,2},{6,7},{7,6},{8,9},{9,8},{10,13... | collective-permute-start | bytes 294920 | tf_op jit(solution)/shard_map/ppermute | solution.py:458
  29.3 14.6 %collective-permute-start.7 = (bf16[2048,128]{1,0:T(8,128)(2,1)S(1)}, bf16[2048,128]{1,0:T(8,128)(2,1)S(1)}, u32[]{:S(2)}, u32[]{:S(2)}) collective-permute-start(bf16[2048,128]{1,0:T(8,128)(2,1)S(1)} %collective-permute-done.2.refs_7_), channel_id=1, source_target_pairs={{0,1},{1,0},{2,3},{3,2},{4,5},{5,4},{6,7},{7,6},{8,9},{9,8},{10,11... | collective-permute-start | bytes 1572872 | tf_op jit(solution)/shard_map/ppermute | solution.py:60
  31.1 9.0 %collective-permute-start.9 = (bf16[1280,128]{1,0:T(8,128)(2,1)S(1)}, bf16[1280,128]{1,0:T(8,128)(2,1)S(1)}, u32[]{:S(2)}, u32[]{:S(2)}) collective-permute-start(bf16[1280,128]{1,0:T(8,128)(2,1)S(1)} %add_convert_fusion.sum_ref), channel_id=1, source_target_pairs={{0,16},{8,24},{16,0},{24,8},{1,17},{9,25},{17,1},{25,9},{2,18},{10... | collective-permute-start | bytes 983048 | tf_op jit(solution)/shard_map/ppermute | solution.py:418
  32.7 1.5 %collective-permute-start.5 = (bf16[768,128]{1,0:T(8,128)(2,1)S(1)}, bf16[768,128]{1,0:T(8,128)(2,1)S(1)}, u32[]{:S(2)}, u32[]{:S(2)}) collective-permute-start(bf16[768,128]{1,0:T(8,128)(2,1)S(1)} %get-tuple-element.29), channel_id=1, source_target_pairs={{0,4},{4,0},{1,5},{5,1},{2,6},{6,2},{3,7},{7,3},{8,12},{12,8},{9,1... | collective-permute-start | bytes 589832 | tf_op jit(solution)/shard_map/ppermute | solution.py:465
  32.7 1.9 %collective-permute-start.4 = (bf16[768,128]{1,0:T(8,128)(2,1)S(1)}, bf16[768,128]{1,0:T(8,128)(2,1)S(1)}, u32[]{:S(2)}, u32[]{:S(2)}) collective-permute-start(bf16[768,128]{1,0:T(8,128)(2,1)S(1)} %pack.1), channel_id=1, source_target_pairs={{0,4},{4,0},{1,5},{5,1},{2,6},{6,2},{3,7},{7,3},{8,12},{12,8},{9,1... | collective-permute-start | bytes 589832 | tf_op jit(solution)/shard_map/ppermute | solution.py:466

commit v8 on v7

--- a/solution.py
+++ b/solution.py
@@ -48,25 +48,31 @@
     return lax.rem(value + n, n)
 
 
-def gather_offsets(block, axis, early):
+FIRST_CYCLE = [(0, 2), (2, 3), (3, 1), (1, 0)]
+SECOND_CYCLE = [(0, 1), (1, 3), (3, 2), (2, 0)]
+TO_ENDS = [(1, 0), (2, 3)]
+INNER = [(1, 2), (2, 1)]
+
+
+def gather_blocks(block, axis, early):
     n = lax.axis_size(axis)
-    have = {0: block}
-    if is_power_of_two(n):
-        bit = n // 2
-        while bit:
-            for k in list(have):
-                if k:
-                    have[k], _ = after(have[k], early)
-                have[k ^ bit] = lax.ppermute(have[k], axis, swap_pairs(n, bit))
-            bit //= 2
-    else:
-        for k in range(1, n):
-            have[k] = lax.ppermute(have[k - 1], axis, shift_pairs(n, n - 1))
-    return [have[k] for k in range(n)]
+    if n == len(FIRST_CYCLE):
+        near = lax.ppermute(block, axis, FIRST_CYCLE)
+        far = lax.ppermute(block, axis, SECOND_CYCLE)
+        passed, _ = after(near, early)
+        ends = lax.ppermute(passed, axis, TO_ENDS)
+        own, _ = after(block, passed)
+        return [block, near, far], [ends, lax.ppermute(own, axis, INNER)]
+    have = [block]
+    for k in range(1, n):
+        have.append(lax.ppermute(have[k - 1], axis, shift_pairs(n, n - 1)))
+    return have[:-1], have[-1:]
 
 
 def owner_of(me, k, n):
-    return me ^ k if is_power_of_two(n) else mod(me + k, n)
+    if n == len(FIRST_CYCLE):
+        return lax.rem((k + 1) * (me + 1), n + 1) - 1
+    return mod(me + k, n)
 
 
 def shifted(block, axis):
@@ -361,11 +367,18 @@
     )
 
 
-def finish_kernel(tile, sum_ref, block_ref, weight_ref, out_hbm, out_ref, sems):
+def finish_kernel(tile, count, sum_ref, block_ref, *refs):
+    weight_refs = refs[:count]
+    out_hbm, out_ref, sems = refs[count:]
+    col = lax.axis_index("col")
+    outside = (col == 0) | (col == lax.axis_size("col") - 1)
     stores = []
-    for i, start in enumerate(range(0, weight_ref.shape[0], tile)):
+    for i, start in enumerate(range(0, sum_ref.shape[1], tile)):
         features = pl.ds(start, tile)
-        piece = times_transposed(block_ref[...], weight_ref[features, :])
+        weight = weight_refs[0][features, :]
+        if count > 1:
+            weight = jnp.where(outside, weight, weight_refs[1][features, :])
+        piece = times_transposed(block_ref[...], weight)
         out_ref[:, features] = (sum_ref[:, features] + piece).astype(jnp.bfloat16)
         stores.append(pltpu.make_async_copy(out_ref.at[:, features], out_hbm.at[:, features], sems.at[i]))
         stores[-1].start()
@@ -373,13 +386,13 @@
         store.wait()
 
 
-def finish(total, block, weight):
+def finish(total, block, weights):
     size, depth = total.shape
     tile = min(512, depth)
     return pl.pallas_call(
-        functools.partial(finish_kernel, tile),
+        functools.partial(finish_kernel, tile, len(weights)),
         out_shape=jax.ShapeDtypeStruct((size, depth), jnp.bfloat16),
-        in_specs=[WHOLE] * 3,
+        in_specs=[WHOLE] * (2 + len(weights)),
         out_specs=HBM,
         scratch_shapes=[pltpu.VMEM((size, depth), jnp.bfloat16), pltpu.SemaphoreType.DMA((depth // tile,))],
         compiler_params=params(16),
@@ -387,7 +400,7 @@
             flops=2 * size * depth * block.shape[1], bytes_accessed=6 * size * depth, transcendentals=0
         ),
         name="finish",
-    )(total, block, weight)
+    )(total, block, *weights)
 
 
 def merge_kernel(replicas, sum_ref, other_ref, held_ref, prior_ref, new_global_hbm, new_outer_hbm, *scratch):
@@ -459,16 +472,16 @@
     (new_weight, new_first, new_second), own, sends = inner(
         tokens, weight[0], first_moment[0], second_moment[0], cots, low_weight
     )
-    weights = gather_offsets(low_weight, "col", sends)
-    low, other = outer_sums(low, "rep", (sends, weights[1], weights[cols // 2]))
-    received, _ = after(received, weights[cols // 2])
+    weights, last = gather_blocks(low_weight, "col", sends)
+    low, other = outer_sums(low, "rep", (sends, weights[1:]))
+    received, _ = after(received, weights[1])
     sums = [lax.ppermute(m, "row", shift_pairs(rows, k + 1)) for k, m in enumerate(sends)]
     messages = [lax.ppermute(pack(received), "row", shift_pairs(rows, k)) for k in range(1, rows)]
     total, block, held, prior, keys_values = arrived(
-        received, messages, sums, own, weights[:-1], cols, global_params, outer_moment, group_slot
+        received, messages, sums, own, weights, cols, global_params, outer_moment, group_slot
     )
     new_global, new_outer = merge(low, other, held, prior, replicas)
-    last, _ = after(weights[-1], (new_outer, total))
+    last, _ = after(last, (new_outer, total))
     input_grad = finish(total, block, last)
     return (keys_values, input_grad, new_weight[None], new_first[None], new_second[None], new_global, new_outer)
 

time: 45.5 us -> 45.2 us (level)
  starting transfers between devices: 12.4 us -> 13.3 us
  Pallas kernels: 17.7 us -> 17 us
  waiting for transfers between devices: 13.7 us -> 13.1 us
    ppermute x2, starting transfers between devices: 1.17 us -> 2.62 us  [on_device(): lax.ppermute(chunks[k], ('row', 'col'), chunk_pairs(rows, cols, per_row, k))]
    ppermute x3 -> x4, waiting for transfers between devices: 10.4 us -> 9.08 us  [the longest x1 6.87 us: gather_blocks(): far = lax.ppermute(block, axis, SECOND_CYCLE)]
    ppermute x3 -> x4, starting transfers between devices: 7.35 us -> 6.08 us  [the longest x1 4.09 us: gather_blocks(): near = lax.ppermute(block, axis, FIRST_CYCLE)]
    pallas_call x1, Pallas kernels: 2.61 us -> 1.87 us  [arrived(): pl.pallas_call(functools.partial(arrived_kernel, rows, cols, min(512, dep...]
    ppermute x1, starting transfers between devices: 0.79 us -> 1.5 us  [on_device(): lax.ppermute(pack(received), 'row', shift_pairs(rows, k))]
    ppermute x2, waiting for transfers between devices: 2.88 us -> 3.58 us  [outer_sums(): other = lax.ppermute(low, axis, swap_pairs(n, bit))]
  transfers between devices with their start and end apart: 10 -> 11, of which waited for: 4 -> 4; matrix products, arithmetic and copies ran while one was open for 0% -> 0% of each run, Pallas kernels for 33% -> 32%
where the time goes in v8:
time: 45.2 us; the launch traced here: 44.9 us
  Pallas kernels  17 us (38%)
  starting transfers between devices  13.3 us (29%)
  waiting for transfers between devices  13.1 us (29%)
  between operations  1.41 us (3%)
    pallas_call x1, Pallas kernels, inner(): pl.pallas_call(functools.partial(inner_kernel, rows, steps), in_specs=[HB...  10 us
    ppermute x1, waiting for transfers between devices, gather_blocks(): far = lax.ppermute(block, axis, SECOND_CYCLE)  6.87 us
    ppermute x1, starting transfers between devices, gather_blocks(): near = lax.ppermute(block, axis, FIRST_CYCLE)  4.09 us
    ppermute x2, waiting for transfers between devices, outer_sums(): other = lax.ppermute(low, axis, swap_pairs(n, bit))  3.58 us
    ppermute x2, starting transfers between devices, outer_sums(): other = lax.ppermute(low, axis, swap_pairs(n, bit))  3.14 us
    ppermute x2, starting transfers between devices, on_device(): lax.ppermute(chunks[k], ('row', 'col'), chunk_pairs(rows, cols, per_row, k))  2.62 us
    ppermute x1, waiting for transfers between devices, gather_blocks(): ends = lax.ppermute(passed, axis, TO_ENDS)  2.2 us
    pallas_call x1, Pallas kernels, arrived(): pl.pallas_call(functools.partial(arrived_kernel, rows, cols, min(512, dep...  1.87 us
  transfers between devices with their start and end apart: 11, of which 4 were waited for; matrix products, arithmetic and copies ran while one was open for 0% of the time, Pallas kernels for 32%

profile of v8, /device:TPU:0, one launch (start us, length us, event | category | flops | bytes accessed | tf_op | source)
XLA Modules:
  0.0 44.9 jit_solution(9675492670993396526)
XLA Ops:
  0.6 0.0 copy-start
  0.6 1.3 %rounded.1.refs_5_ = bf16[2048,128]{1,0:T(8,128)(2,1)S(1)} custom-call(f32[2048,128]{1,0:T(8,128)} %bitcast.19), custom_call_target="tpu_custom_call" | custom-call | bytes 1572864 | tf_op jit(solution)/shard_map/rounded/pallas_call | solution.py:104
  1.9 4.1 %collective-permute-start.2 = (bf16[2048,128]{1,0:T(8,128)(2,1)S(1)}, bf16[2048,128]{1,0:T(8,128)(2,1)S(1)}, u32[]{:S(2)}, u32[]{:S(2)}) collective-permute-start(bf16[2048,128]{1,0:T(8,128)(2,1)S(1)} %rounded.1.refs_5_), channel_id=1, source_target_pairs={{0,2},{2,3},{3,1},{1,0},{4,6},{6,7},{7,5},{5,4},{8,10},{10,11},{11... | collective-permute-start | bytes 1572872 | tf_op jit(solution)/shard_map/ppermute | solution.py:60
  6.0 0.0 collective-permute-start.6
  6.0 0.0 copy-done
  6.0 0.0 collective-permute-start.4
  6.0 1.2 %prepare.1 = (bf16[1280,128]{1,0:T(8,128)(2,1)S(1)}, bf16[384,128]{1,0:T(8,128)(2,1)S(1)}, bf16[384,128]{1,0:T(8,128)(2,1)S(1)}) custom-call(bf16[768,128]{1,0:T(8,128)(2,1)} %refs_4_.1, f32[1280,128]{1,0:T(8,128)} %bitcast.25), custom_call_target="tpu_custom_call" | custom-call | bytes 983040 | tf_op jit(solution)/shard_map/prepare/pallas_call | solution.py:138
  7.2 1.6 %collective-permute-start.9 = (bf16[1280,128]{1,0:T(8,128)(2,1)S(1)}, bf16[1280,128]{1,0:T(8,128)(2,1)S(1)}, u32[]{:S(2)}, u32[]{:S(2)}) collective-permute-start(bf16[1280,128]{1,0:T(8,128)(2,1)S(1)} %get-tuple-element.40), channel_id=1, source_target_pairs={{0,8},{8,0},{16,24},{24,16},{1,9},{9,1},{17,25},{25,17},{2,10},{10... | collective-permute-start | bytes 983048 | tf_op jit(solution)/shard_map/ppermute | solution.py:431
  8.8 0.7 %collective-permute-start = (bf16[384,128]{1,0:T(8,128)(2,1)S(1)}, bf16[384,128]{1,0:T(8,128)(2,1)S(1)}, u32[]{:S(2)}, u32[]{:S(2)}) collective-permute-start(bf16[384,128]{1,0:T(8,128)(2,1)S(1)} %get-tuple-element.29), channel_id=1, source_target_pairs={{0,0},{1,1},{2,4},{3,5},{4,2},{5,3},{6,6},{7,7},{8,8},{9,9},{10,12... | collective-permute-start | bytes 294920 | tf_op jit(solution)/shard_map/ppermute | solution.py:471
  9.4 0.0 collective-permute-done.4.refs_6_
  9.4 2.0 %collective-permute-start.1 = (bf16[384,128]{1,0:T(8,128)(2,1)S(1)}, bf16[384,128]{1,0:T(8,128)(2,1)S(1)}, u32[]{:S(2)}, u32[]{:S(2)}) collective-permute-start(bf16[384,128]{1,0:T(8,128)(2,1)S(1)} %get-tuple-element.30), channel_id=1, source_target_pairs={{0,1},{1,0},{2,5},{3,4},{4,3},{5,2},{6,7},{7,6},{8,9},{9,8},{10,13... | collective-permute-start | bytes 294920 | tf_op jit(solution)/shard_map/ppermute | solution.py:471
  11.4 10.0 %inner.1 = (f32[2048,128]{1,0:T(8,128)}, f32[2048,128]{1,0:T(8,128)}, f32[2048,128]{1,0:T(8,128)}, f32[768,128]{1,0:T(8,128)S(1)}, bf16[768,128]{1,0:T(8,128)(2,1)S(1)}) custom-call(bf16[1536,2048]{1,0:T(8,128)(2,1)} %refs_0_.1, f32[2048,128]{1,0:T(8,128)} %bitcast.20, f32[2048,128]{1,0:T(8,128)} %bitcast.23, f32[2048,128]{1,0:T(8,128)} %bitcast.24, ...), custom_call_target="tpu_custom_call" | custom-call | flops 1610612736 | bytes 12582912 | tf_op jit(solution)/shard_map/inner/pallas_call | solution.py:255
  21.4 0.0 collective-permute-done.2.refs_6_
  21.5 1.3 %collective-permute-start.7 = (bf16[2048,128]{1,0:T(8,128)(2,1)S(1)}, bf16[2048,128]{1,0:T(8,128)(2,1)S(1)}, u32[]{:S(2)}, u32[]{:S(2)}) collective-permute-start(bf16[2048,128]{1,0:T(8,128)(2,1)S(1)} %collective-permute-done.2.refs_6_), channel_id=1, source_target_pairs={{1,0},{2,3},{5,4},{6,7},{9,8},{10,11},{13,12},{14,15},{17,16},{18,... | collective-permute-start | bytes 1572872 | tf_op jit(solution)/shard_map/ppermute | solution.py:63
  22.8 0.0 collective-permute-done.9
  22.8 0.7 %collective-permute-start.8 = (bf16[2048,128]{1,0:T(8,128)(2,1)S(1)}, bf16[2048,128]{1,0:T(8,128)(2,1)S(1)}, u32[]{:S(2)}, u32[]{:S(2)}) collective-permute-start(bf16[2048,128]{1,0:T(8,128)(2,1)S(1)} %rounded.1.refs_5_), channel_id=1, source_target_pairs={{1,2},{2,1},{5,6},{6,5},{9,10},{10,9},{13,14},{14,13},{17,18},{18,... | collective-permute-start | bytes 1572872 | tf_op jit(solution)/shard_map/ppermute | solution.py:65
  23.5 6.9 %collective-permute-done.6.refs_7_ = bf16[2048,128]{1,0:T(8,128)(2,1)S(1)} collective-permute-done((bf16[2048,128]{1,0:T(8,128)(2,1)S(1)}, bf16[2048,128]{1,0:T(8,128)(2,1)S(1)}, u32[]{:S(2)}, u32[]{:S(2)}) %collective-permute-start.6) | collective-permute-done | bytes 524320 | tf_op jit(solution)/shard_map/ppermute | solution.py:61
  30.3 0.1 add_convert_fusion.sum_ref
  30.4 1.6 %collective-permute-start.10 = (bf16[1280,128]{1,0:T(8,128)(2,1)S(1)}, bf16[1280,128]{1,0:T(8,128)(2,1)S(1)}, u32[]{:S(2)}, u32[]{:S(2)}) collective-permute-start(bf16[1280,128]{1,0:T(8,128)(2,1)S(1)} %add_convert_fusion.sum_ref), channel_id=1, source_target_pairs={{0,16},{8,24},{16,0},{24,8},{1,17},{9,25},{17,1},{25,9},{2,18},{10... | collective-permute-start | bytes 983048 | tf_op jit(solution)/shard_map/ppermute | solution.py:431
  32.0 0.0 collective-permute-done.refs_0_
  32.0 0.0 collective-permute-start.5
  32.0 0.0 collective-permute-done.1.refs_1_
  32.1 1.5 %collective-permute-start.3 = (bf16[768,128]{1,0:T(8,128)(2,1)S(1)}, bf16[768,128]{1,0:T(8,128)(2,1)S(1)}, u32[]{:S(2)}, u32[]{:S(2)}) collective-permute-start(bf16[768,128]{1,0:T(8,128)(2,1)S(1)} %pack.1), channel_id=1, source_target_pairs={{0,4},{4,0},{1,5},{5,1},{2,6},{6,2},{3,7},{7,3},{8,12},{12,8},{9,1... | collective-permute-start | bytes 589832 | tf_op jit(solution)/shard_map/ppermute | solution.py:479
  34.2 0.0 collective-permute-done.5.refs_3_
  34.2 0.4 collective-permute-done.3.refs_2_
  34.6 1.9 %arrived.1 = (f32[384,2048]{1,0:T(8,128)S(1)}, bf16[384,128]{1,0:T(8,128)(2,1)S(1)}, f32[1280,128]{1,0:T(8,128)S(1)}, f32[1280,128]{1,0:T(8,128)S(1)}, bf16[768,128]{1,0:T(8,128)(2,1)}) custom-call(bf16[384,128]{1,0:T(8,128)(2,1)S(1)} %collective-permute-done.refs_0_, bf16[384,128]{1,0:T(8,128)(2,1)S(1)} %collective-permute-done.1.refs_1_, ...), custom_call_target="tpu_custom_call" | custom-call | flops 603979776 | bytes 3145728 | tf_op jit(solution)/shard_map/arrived/pallas_call | solution.py:341
  36.5 3.6 %collective-permute-done.10.other_ref = bf16[1280,128]{1,0:T(8,128)(2,1)S(1)} collective-permute-done((bf16[1280,128]{1,0:T(8,128)(2,1)S(1)}, bf16[1280,128]{1,0:T(8,128)(2,1)S(1)}, u32[]{:S(2)}, u32[]{:S(2)}) %collective-permute-start.10) | collective-permute-done | bytes 327712 | tf_op jit(solution)/shard_map/ppermute | solution.py:431
  40.1 1.2 %merge.1 = (f32[1280,128]{1,0:T(8,128)}, f32[1280,128]{1,0:T(8,128)}) custom-call(bf16[1280,128]{1,0:T(8,128)(2,1)S(1)} %add_convert_fusion.sum_ref, bf16[1280,128]{1,0:T(8,128)(2,1)S(1)} %collective-permute-done.10.other_ref, f32[1280,128]{1,0:T(8,128)S(1)} %get-tuple-element.42.held_ref, f32[1280,128]{1,0:T(8,128)S(1)} %get-tuple-element.43.prior_ref), custom_call_target="tpu_custom_call" | custom-call | flops 1310720 | bytes 1310720 | tf_op jit(solution)/shard_map/merge/pallas_call | solution.py:441
  41.3 2.2 %collective-permute-done.7.refs_0_ = bf16[2048,128]{1,0:T(8,128)(2,1)S(1)} collective-permute-done((bf16[2048,128]{1,0:T(8,128)(2,1)S(1)}, bf16[2048,128]{1,0:T(8,128)(2,1)S(1)}, u32[]{:S(2)}, u32[]{:S(2)}) %collective-permute-start.7) | collective-permute-done | bytes 524320 | tf_op jit(solution)/shard_map/ppermute | solution.py:63
  43.5 0.0 collective-permute-done.8.refs_1_
  43.5 1.4 %finish.1 = bf16[384,2048]{1,0:T(8,128)(2,1)} custom-call(f32[384,2048]{1,0:T(8,128)S(1)} %get-tuple-element.36.sum_ref, bf16[384,128]{1,0:T(8,128)(2,1)S(1)} %get-tuple-element.37.block_ref, bf16[2048,128]{1,0:T(8,128)(2,1)S(1)} %collective-permute-done.7.refs_0_, bf16[2048,128]{1,0:T(8,128)(2,1)S(1)} %collective-permute-done.8.refs_1_), custom_call_target="tpu_custom_call" | custom-call | flops 201326592 | bytes 4718592 | tf_op jit(solution)/shard_map/finish/pallas_call | solution.py:392
  (1 shorter events, 0.0 us)
Async XLA Ops:
  0.6 5.4 %copy-start = (bf16[768,128]{1,0:T(8,128)(2,1)S(1)}, bf16[768,128]{1,0:T(8,128)(2,1)}, u32[]{:S(2)}) copy-start(bf16[768,128]{1,0:T(8,128)(2,1)} %refs_4_.1) | copy-start | bytes 589828
  1.9 19.5 %collective-permute-start.2 = (bf16[2048,128]{1,0:T(8,128)(2,1)S(1)}, bf16[2048,128]{1,0:T(8,128)(2,1)S(1)}, u32[]{:S(2)}, u32[]{:S(2)}) collective-permute-start(bf16[2048,128]{1,0:T(8,128)(2,1)S(1)} %rounded.1.refs_5_), channel_id=1, source_target_pairs={{0,2},{2,3},{3,1},{1,0},{4,6},{6,7},{7,5},{5,4},{8,10},{10,11},{11... | collective-permute-start | bytes 1572872 | tf_op jit(solution)/shard_map/ppermute | solution.py:60
  6.0 24.3 %collective-permute-start.6 = (bf16[2048,128]{1,0:T(8,128)(2,1)S(1)}, bf16[2048,128]{1,0:T(8,128)(2,1)S(1)}, u32[]{:S(2)}, u32[]{:S(2)}) collective-permute-start(bf16[2048,128]{1,0:T(8,128)(2,1)S(1)} %rounded.1.refs_5_), channel_id=1, source_target_pairs={{0,1},{1,3},{3,2},{2,0},{4,5},{5,7},{7,6},{6,4},{8,9},{9,11},{11,1... | collective-permute-start | bytes 1572872 | tf_op jit(solution)/shard_map/ppermute | solution.py:61
  6.0 3.4 %collective-permute-start.4 = (bf16[768,128]{1,0:T(8,128)(2,1)S(1)}, bf16[768,128]{1,0:T(8,128)(2,1)S(1)}, u32[]{:S(2)}, u32[]{:S(2)}) collective-permute-start(bf16[768,128]{1,0:T(8,128)(2,1)S(1)} %copy-done), channel_id=1, source_target_pairs={{0,4},{4,0},{1,5},{5,1},{2,6},{6,2},{3,7},{7,3},{8,12},{12,8},{9,1... | collective-permute-start | bytes 589832 | tf_op jit(solution)/shard_map/ppermute | solution.py:80
  7.2 15.6 %collective-permute-start.9 = (bf16[1280,128]{1,0:T(8,128)(2,1)S(1)}, bf16[1280,128]{1,0:T(8,128)(2,1)S(1)}, u32[]{:S(2)}, u32[]{:S(2)}) collective-permute-start(bf16[1280,128]{1,0:T(8,128)(2,1)S(1)} %get-tuple-element.40), channel_id=1, source_target_pairs={{0,8},{8,0},{16,24},{24,16},{1,9},{9,1},{17,25},{25,17},{2,10},{10... | collective-permute-start | bytes 983048 | tf_op jit(solution)/shard_map/ppermute | solution.py:431
  8.8 23.3 %collective-permute-start = (bf16[384,128]{1,0:T(8,128)(2,1)S(1)}, bf16[384,128]{1,0:T(8,128)(2,1)S(1)}, u32[]{:S(2)}, u32[]{:S(2)}) collective-permute-start(bf16[384,128]{1,0:T(8,128)(2,1)S(1)} %get-tuple-element.29), channel_id=1, source_target_pairs={{0,0},{1,1},{2,4},{3,5},{4,2},{5,3},{6,6},{7,7},{8,8},{9,9},{10,12... | collective-permute-start | bytes 294920 | tf_op jit(solution)/shard_map/ppermute | solution.py:471
  9.4 22.6 %collective-permute-start.1 = (bf16[384,128]{1,0:T(8,128)(2,1)S(1)}, bf16[384,128]{1,0:T(8,128)(2,1)S(1)}, u32[]{:S(2)}, u32[]{:S(2)}) collective-permute-start(bf16[384,128]{1,0:T(8,128)(2,1)S(1)} %get-tuple-element.30), channel_id=1, source_target_pairs={{0,1},{1,0},{2,5},{3,4},{4,3},{5,2},{6,7},{7,6},{8,9},{9,8},{10,13... | collective-permute-start | bytes 294920 | tf_op jit(solution)/shard_map/ppermute | solution.py:471
  21.5 22.0 %collective-permute-start.7 = (bf16[2048,128]{1,0:T(8,128)(2,1)S(1)}, bf16[2048,128]{1,0:T(8,128)(2,1)S(1)}, u32[]{:S(2)}, u32[]{:S(2)}) collective-permute-start(bf16[2048,128]{1,0:T(8,128)(2,1)S(1)} %collective-permute-done.2.refs_6_), channel_id=1, source_target_pairs={{1,0},{2,3},{5,4},{6,7},{9,8},{10,11},{13,12},{14,15},{17,16},{18,... | collective-permute-start | bytes 1572872 | tf_op jit(solution)/shard_map/ppermute | solution.py:63
  22.8 20.7 %collective-permute-start.8 = (bf16[2048,128]{1,0:T(8,128)(2,1)S(1)}, bf16[2048,128]{1,0:T(8,128)(2,1)S(1)}, u32[]{:S(2)}, u32[]{:S(2)}) collective-permute-start(bf16[2048,128]{1,0:T(8,128)(2,1)S(1)} %rounded.1.refs_5_), channel_id=1, source_target_pairs={{1,2},{2,1},{5,6},{6,5},{9,10},{10,9},{13,14},{14,13},{17,18},{18,... | collective-permute-start | bytes 1572872 | tf_op jit(solution)/shard_map/ppermute | solution.py:65
  30.4 9.6 %collective-permute-start.10 = (bf16[1280,128]{1,0:T(8,128)(2,1)S(1)}, bf16[1280,128]{1,0:T(8,128)(2,1)S(1)}, u32[]{:S(2)}, u32[]{:S(2)}) collective-permute-start(bf16[1280,128]{1,0:T(8,128)(2,1)S(1)} %add_convert_fusion.sum_ref), channel_id=1, source_target_pairs={{0,16},{8,24},{16,0},{24,8},{1,17},{9,25},{17,1},{25,9},{2,18},{10... | collective-permute-start | bytes 983048 | tf_op jit(solution)/shard_map/ppermute | solution.py:431
  32.0 2.2 %collective-permute-start.5 = (bf16[768,128]{1,0:T(8,128)(2,1)S(1)}, bf16[768,128]{1,0:T(8,128)(2,1)S(1)}, u32[]{:S(2)}, u32[]{:S(2)}) collective-permute-start(bf16[768,128]{1,0:T(8,128)(2,1)S(1)} %get-tuple-element.33), channel_id=1, source_target_pairs={{0,4},{4,0},{1,5},{5,1},{2,6},{6,2},{3,7},{7,3},{8,12},{12,8},{9,1... | collective-permute-start | bytes 589832 | tf_op jit(solution)/shard_map/ppermute | solution.py:478
  32.1 2.6 %collective-permute-start.3 = (bf16[768,128]{1,0:T(8,128)(2,1)S(1)}, bf16[768,128]{1,0:T(8,128)(2,1)S(1)}, u32[]{:S(2)}, u32[]{:S(2)}) collective-permute-start(bf16[768,128]{1,0:T(8,128)(2,1)S(1)} %pack.1), channel_id=1, source_target_pairs={{0,4},{4,0},{1,5},{5,1},{2,6},{6,2},{3,7},{7,3},{8,12},{12,8},{9,1... | collective-permute-start | bytes 589832 | tf_op jit(solution)/shard_map/ppermute | solution.py:479

commit v9 on v8

--- a/solution.py
+++ b/solution.py
@@ -61,7 +61,7 @@
         far = lax.ppermute(block, axis, SECOND_CYCLE)
         passed, _ = after(near, early)
         ends = lax.ppermute(passed, axis, TO_ENDS)
-        own, _ = after(block, passed)
+        own, _ = after(block, (passed, far))
         return [block, near, far], [ends, lax.ppermute(own, axis, INNER)]
     have = [block]
     for k in range(1, n):

time: 45.2 us -> 45.2 us (level)
  starting transfers between devices: 13.3 us -> 12.6 us
  waiting for transfers between devices: 13.1 us -> 13.8 us
    ppermute x1, waiting for transfers between devices: 6.87 us -> 7.59 us  [gather_blocks(): far = lax.ppermute(block, axis, SECOND_CYCLE)]
    ppermute x1, waiting for transfers between devices: 2.2 us -> 1.5 us  [gather_blocks(): ends = lax.ppermute(passed, axis, TO_ENDS)]
    ppermute x1, starting transfers between devices: 1.5 us -> 0.79 us  [on_device(): lax.ppermute(pack(received), 'row', shift_pairs(rows, k))]
    ppermute x2, waiting for transfers between devices: 3.58 us -> 4.28 us  [outer_sums(): other = lax.ppermute(low, axis, swap_pairs(n, bit))]
where the time goes in v9:
time: 45.2 us; the launch traced here: 44.9 us
  Pallas kernels  17 us (38%)
  waiting for transfers between devices  13.8 us (31%)
  starting transfers between devices  12.6 us (28%)
  between operations  1.41 us (3%)
    pallas_call x1, Pallas kernels, inner(): pl.pallas_call(functools.partial(inner_kernel, rows, steps), in_specs=[HB...  10 us
    ppermute x1, waiting for transfers between devices, gather_blocks(): far = lax.ppermute(block, axis, SECOND_CYCLE)  7.59 us
    ppermute x2, waiting for transfers between devices, outer_sums(): other = lax.ppermute(low, axis, swap_pairs(n, bit))  4.28 us
    ppermute x1, starting transfers between devices, gather_blocks(): near = lax.ppermute(block, axis, FIRST_CYCLE)  4.09 us
    ppermute x2, starting transfers between devices, outer_sums(): other = lax.ppermute(low, axis, swap_pairs(n, bit))  3.14 us
    ppermute x2, starting transfers between devices, on_device(): lax.ppermute(chunks[k], ('row', 'col'), chunk_pairs(rows, cols, per_row, k))  2.62 us
    pallas_call x1, Pallas kernels, arrived(): pl.pallas_call(functools.partial(arrived_kernel, rows, cols, min(512, dep...  1.87 us
    ppermute x1, waiting for transfers between devices, gather_blocks(): ends = lax.ppermute(passed, axis, TO_ENDS)  1.5 us
  transfers between devices with their start and end apart: 11, of which 4 were waited for; matrix products, arithmetic and copies ran while one was open for 0% of the time, Pallas kernels for 32%

profile of v9, /device:TPU:0, one launch (start us, length us, event | category | flops | bytes accessed | tf_op | source)
XLA Modules:
  0.0 44.9 jit_solution(11254363359453394814)
XLA Ops:
  0.6 0.0 copy-start
  0.6 1.3 %rounded.1.refs_5_ = bf16[2048,128]{1,0:T(8,128)(2,1)S(1)} custom-call(f32[2048,128]{1,0:T(8,128)} %bitcast.19), custom_call_target="tpu_custom_call" | custom-call | bytes 1572864 | tf_op jit(solution)/shard_map/rounded/pallas_call | solution.py:104
  1.9 4.1 %collective-permute-start.2 = (bf16[2048,128]{1,0:T(8,128)(2,1)S(1)}, bf16[2048,128]{1,0:T(8,128)(2,1)S(1)}, u32[]{:S(2)}, u32[]{:S(2)}) collective-permute-start(bf16[2048,128]{1,0:T(8,128)(2,1)S(1)} %rounded.1.refs_5_), channel_id=1, source_target_pairs={{0,2},{2,3},{3,1},{1,0},{4,6},{6,7},{7,5},{5,4},{8,10},{10,11},{11... | collective-permute-start | bytes 1572872 | tf_op jit(solution)/shard_map/ppermute | solution.py:60
  6.0 0.0 collective-permute-start.6
  6.0 0.0 copy-done
  6.0 0.0 collective-permute-start.4
  6.0 1.2 %prepare.1 = (bf16[1280,128]{1,0:T(8,128)(2,1)S(1)}, bf16[384,128]{1,0:T(8,128)(2,1)S(1)}, bf16[384,128]{1,0:T(8,128)(2,1)S(1)}) custom-call(bf16[768,128]{1,0:T(8,128)(2,1)} %refs_4_.1, f32[1280,128]{1,0:T(8,128)} %bitcast.25), custom_call_target="tpu_custom_call" | custom-call | bytes 983040 | tf_op jit(solution)/shard_map/prepare/pallas_call | solution.py:138
  7.2 1.6 %collective-permute-start.9 = (bf16[1280,128]{1,0:T(8,128)(2,1)S(1)}, bf16[1280,128]{1,0:T(8,128)(2,1)S(1)}, u32[]{:S(2)}, u32[]{:S(2)}) collective-permute-start(bf16[1280,128]{1,0:T(8,128)(2,1)S(1)} %get-tuple-element.40), channel_id=1, source_target_pairs={{0,8},{8,0},{16,24},{24,16},{1,9},{9,1},{17,25},{25,17},{2,10},{10... | collective-permute-start | bytes 983048 | tf_op jit(solution)/shard_map/ppermute | solution.py:431
  8.8 0.7 %collective-permute-start = (bf16[384,128]{1,0:T(8,128)(2,1)S(1)}, bf16[384,128]{1,0:T(8,128)(2,1)S(1)}, u32[]{:S(2)}, u32[]{:S(2)}) collective-permute-start(bf16[384,128]{1,0:T(8,128)(2,1)S(1)} %get-tuple-element.29), channel_id=1, source_target_pairs={{0,0},{1,1},{2,4},{3,5},{4,2},{5,3},{6,6},{7,7},{8,8},{9,9},{10,12... | collective-permute-start | bytes 294920 | tf_op jit(solution)/shard_map/ppermute | solution.py:471
  9.4 0.0 collective-permute-done.4.refs_6_
  9.4 2.0 %collective-permute-start.1 = (bf16[384,128]{1,0:T(8,128)(2,1)S(1)}, bf16[384,128]{1,0:T(8,128)(2,1)S(1)}, u32[]{:S(2)}, u32[]{:S(2)}) collective-permute-start(bf16[384,128]{1,0:T(8,128)(2,1)S(1)} %get-tuple-element.30), channel_id=1, source_target_pairs={{0,1},{1,0},{2,5},{3,4},{4,3},{5,2},{6,7},{7,6},{8,9},{9,8},{10,13... | collective-permute-start | bytes 294920 | tf_op jit(solution)/shard_map/ppermute | solution.py:471
  11.4 10.0 %inner.1 = (f32[2048,128]{1,0:T(8,128)}, f32[2048,128]{1,0:T(8,128)}, f32[2048,128]{1,0:T(8,128)}, f32[768,128]{1,0:T(8,128)S(1)}, bf16[768,128]{1,0:T(8,128)(2,1)S(1)}) custom-call(bf16[1536,2048]{1,0:T(8,128)(2,1)} %refs_0_.1, f32[2048,128]{1,0:T(8,128)} %bitcast.20, f32[2048,128]{1,0:T(8,128)} %bitcast.23, f32[2048,128]{1,0:T(8,128)} %bitcast.24, ...), custom_call_target="tpu_custom_call" | custom-call | flops 1610612736 | bytes 12582912 | tf_op jit(solution)/shard_map/inner/pallas_call | solution.py:255
  21.4 0.0 collective-permute-done.2.refs_6_
  21.5 1.3 %collective-permute-start.7 = (bf16[2048,128]{1,0:T(8,128)(2,1)S(1)}, bf16[2048,128]{1,0:T(8,128)(2,1)S(1)}, u32[]{:S(2)}, u32[]{:S(2)}) collective-permute-start(bf16[2048,128]{1,0:T(8,128)(2,1)S(1)} %collective-permute-done.2.refs_6_), channel_id=1, source_target_pairs={{1,0},{2,3},{5,4},{6,7},{9,8},{10,11},{13,12},{14,15},{17,16},{18,... | collective-permute-start | bytes 1572872 | tf_op jit(solution)/shard_map/ppermute | solution.py:63
  22.8 7.6 %collective-permute-done.6.refs_7_ = bf16[2048,128]{1,0:T(8,128)(2,1)S(1)} collective-permute-done((bf16[2048,128]{1,0:T(8,128)(2,1)S(1)}, bf16[2048,128]{1,0:T(8,128)(2,1)S(1)}, u32[]{:S(2)}, u32[]{:S(2)}) %collective-permute-start.6) | collective-permute-done | bytes 524320 | tf_op jit(solution)/shard_map/ppermute | solution.py:61
  30.3 0.7 %collective-permute-start.8 = (bf16[2048,128]{1,0:T(8,128)(2,1)S(1)}, bf16[2048,128]{1,0:T(8,128)(2,1)S(1)}, u32[]{:S(2)}, u32[]{:S(2)}) collective-permute-start(bf16[2048,128]{1,0:T(8,128)(2,1)S(1)} %rounded.1.refs_5_), channel_id=1, source_target_pairs={{1,2},{2,1},{5,6},{6,5},{9,10},{10,9},{13,14},{14,13},{17,18},{18,... | collective-permute-start | bytes 1572872 | tf_op jit(solution)/shard_map/ppermute | solution.py:65
  31.0 0.0 collective-permute-done.9
  31.0 0.1 add_convert_fusion.sum_ref
  31.1 1.6 %collective-permute-start.10 = (bf16[1280,128]{1,0:T(8,128)(2,1)S(1)}, bf16[1280,128]{1,0:T(8,128)(2,1)S(1)}, u32[]{:S(2)}, u32[]{:S(2)}) collective-permute-start(bf16[1280,128]{1,0:T(8,128)(2,1)S(1)} %add_convert_fusion.sum_ref), channel_id=1, source_target_pairs={{0,16},{8,24},{16,0},{24,8},{1,17},{9,25},{17,1},{25,9},{2,18},{10... | collective-permute-start | bytes 983048 | tf_op jit(solution)/shard_map/ppermute | solution.py:431
  32.7 0.0 collective-permute-done.refs_0_
  32.7 0.0 collective-permute-start.5
  32.7 0.0 collective-permute-done.1.refs_1_
  32.8 0.8 %collective-permute-start.3 = (bf16[768,128]{1,0:T(8,128)(2,1)S(1)}, bf16[768,128]{1,0:T(8,128)(2,1)S(1)}, u32[]{:S(2)}, u32[]{:S(2)}) collective-permute-start(bf16[768,128]{1,0:T(8,128)(2,1)S(1)} %pack.1), channel_id=1, source_target_pairs={{0,4},{4,0},{1,5},{5,1},{2,6},{6,2},{3,7},{7,3},{8,12},{12,8},{9,1... | collective-permute-start | bytes 589832 | tf_op jit(solution)/shard_map/ppermute | solution.py:479
  34.2 0.0 collective-permute-done.5.refs_3_
  34.2 0.4 collective-permute-done.3.refs_2_
  34.6 1.9 %arrived.1 = (f32[384,2048]{1,0:T(8,128)S(1)}, bf16[384,128]{1,0:T(8,128)(2,1)S(1)}, f32[1280,128]{1,0:T(8,128)S(1)}, f32[1280,128]{1,0:T(8,128)S(1)}, bf16[768,128]{1,0:T(8,128)(2,1)}) custom-call(bf16[384,128]{1,0:T(8,128)(2,1)S(1)} %collective-permute-done.refs_0_, bf16[384,128]{1,0:T(8,128)(2,1)S(1)} %collective-permute-done.1.refs_1_, ...), custom_call_target="tpu_custom_call" | custom-call | flops 603979776 | bytes 3145728 | tf_op jit(solution)/shard_map/arrived/pallas_call | solution.py:341
  36.5 4.3 %collective-permute-done.10.other_ref = bf16[1280,128]{1,0:T(8,128)(2,1)S(1)} collective-permute-done((bf16[1280,128]{1,0:T(8,128)(2,1)S(1)}, bf16[1280,128]{1,0:T(8,128)(2,1)S(1)}, u32[]{:S(2)}, u32[]{:S(2)}) %collective-permute-start.10) | collective-permute-done | bytes 327712 | tf_op jit(solution)/shard_map/ppermute | solution.py:431
  40.8 1.2 %merge.1 = (f32[1280,128]{1,0:T(8,128)}, f32[1280,128]{1,0:T(8,128)}) custom-call(bf16[1280,128]{1,0:T(8,128)(2,1)S(1)} %add_convert_fusion.sum_ref, bf16[1280,128]{1,0:T(8,128)(2,1)S(1)} %collective-permute-done.10.other_ref, f32[1280,128]{1,0:T(8,128)S(1)} %get-tuple-element.42.held_ref, f32[1280,128]{1,0:T(8,128)S(1)} %get-tuple-element.43.prior_ref), custom_call_target="tpu_custom_call" | custom-call | flops 1310720 | bytes 1310720 | tf_op jit(solution)/shard_map/merge/pallas_call | solution.py:441
  42.0 1.5 %collective-permute-done.7.refs_0_ = bf16[2048,128]{1,0:T(8,128)(2,1)S(1)} collective-permute-done((bf16[2048,128]{1,0:T(8,128)(2,1)S(1)}, bf16[2048,128]{1,0:T(8,128)(2,1)S(1)}, u32[]{:S(2)}, u32[]{:S(2)}) %collective-permute-start.7) | collective-permute-done | bytes 524320 | tf_op jit(solution)/shard_map/ppermute | solution.py:63
  43.5 0.0 collective-permute-done.8.refs_1_
  43.5 1.4 %finish.1 = bf16[384,2048]{1,0:T(8,128)(2,1)} custom-call(f32[384,2048]{1,0:T(8,128)S(1)} %get-tuple-element.36.sum_ref, bf16[384,128]{1,0:T(8,128)(2,1)S(1)} %get-tuple-element.37.block_ref, bf16[2048,128]{1,0:T(8,128)(2,1)S(1)} %collective-permute-done.7.refs_0_, bf16[2048,128]{1,0:T(8,128)(2,1)S(1)} %collective-permute-done.8.refs_1_), custom_call_target="tpu_custom_call" | custom-call | flops 201326592 | bytes 4718592 | tf_op jit(solution)/shard_map/finish/pallas_call | solution.py:392
  (1 shorter events, 0.0 us)
Async XLA Ops:
  0.6 5.4 %copy-start = (bf16[768,128]{1,0:T(8,128)(2,1)S(1)}, bf16[768,128]{1,0:T(8,128)(2,1)}, u32[]{:S(2)}) copy-start(bf16[768,128]{1,0:T(8,128)(2,1)} %refs_4_.1) | copy-start | bytes 589828
  1.9 19.5 %collective-permute-start.2 = (bf16[2048,128]{1,0:T(8,128)(2,1)S(1)}, bf16[2048,128]{1,0:T(8,128)(2,1)S(1)}, u32[]{:S(2)}, u32[]{:S(2)}) collective-permute-start(bf16[2048,128]{1,0:T(8,128)(2,1)S(1)} %rounded.1.refs_5_), channel_id=1, source_target_pairs={{0,2},{2,3},{3,1},{1,0},{4,6},{6,7},{7,5},{5,4},{8,10},{10,11},{11... | collective-permute-start | bytes 1572872 | tf_op jit(solution)/shard_map/ppermute | solution.py:60
  6.0 24.3 %collective-permute-start.6 = (bf16[2048,128]{1,0:T(8,128)(2,1)S(1)}, bf16[2048,128]{1,0:T(8,128)(2,1)S(1)}, u32[]{:S(2)}, u32[]{:S(2)}) collective-permute-start(bf16[2048,128]{1,0:T(8,128)(2,1)S(1)} %rounded.1.refs_5_), channel_id=1, source_target_pairs={{0,1},{1,3},{3,2},{2,0},{4,5},{5,7},{7,6},{6,4},{8,9},{9,11},{11,1... | collective-permute-start | bytes 1572872 | tf_op jit(solution)/shard_map/ppermute | solution.py:61
  6.0 3.4 %collective-permute-start.4 = (bf16[768,128]{1,0:T(8,128)(2,1)S(1)}, bf16[768,128]{1,0:T(8,128)(2,1)S(1)}, u32[]{:S(2)}, u32[]{:S(2)}) collective-permute-start(bf16[768,128]{1,0:T(8,128)(2,1)S(1)} %copy-done), channel_id=1, source_target_pairs={{0,4},{4,0},{1,5},{5,1},{2,6},{6,2},{3,7},{7,3},{8,12},{12,8},{9,1... | collective-permute-start | bytes 589832 | tf_op jit(solution)/shard_map/ppermute | solution.py:80
  7.2 23.8 %collective-permute-start.9 = (bf16[1280,128]{1,0:T(8,128)(2,1)S(1)}, bf16[1280,128]{1,0:T(8,128)(2,1)S(1)}, u32[]{:S(2)}, u32[]{:S(2)}) collective-permute-start(bf16[1280,128]{1,0:T(8,128)(2,1)S(1)} %get-tuple-element.40), channel_id=1, source_target_pairs={{0,8},{8,0},{16,24},{24,16},{1,9},{9,1},{17,25},{25,17},{2,10},{10... | collective-permute-start | bytes 983048 | tf_op jit(solution)/shard_map/ppermute | solution.py:431
  8.8 24.0 %collective-permute-start = (bf16[384,128]{1,0:T(8,128)(2,1)S(1)}, bf16[384,128]{1,0:T(8,128)(2,1)S(1)}, u32[]{:S(2)}, u32[]{:S(2)}) collective-permute-start(bf16[384,128]{1,0:T(8,128)(2,1)S(1)} %get-tuple-element.29), channel_id=1, source_target_pairs={{0,0},{1,1},{2,4},{3,5},{4,2},{5,3},{6,6},{7,7},{8,8},{9,9},{10,12... | collective-permute-start | bytes 294920 | tf_op jit(solution)/shard_map/ppermute | solution.py:471
  9.4 23.3 %collective-permute-start.1 = (bf16[384,128]{1,0:T(8,128)(2,1)S(1)}, bf16[384,128]{1,0:T(8,128)(2,1)S(1)}, u32[]{:S(2)}, u32[]{:S(2)}) collective-permute-start(bf16[384,128]{1,0:T(8,128)(2,1)S(1)} %get-tuple-element.30), channel_id=1, source_target_pairs={{0,1},{1,0},{2,5},{3,4},{4,3},{5,2},{6,7},{7,6},{8,9},{9,8},{10,13... | collective-permute-start | bytes 294920 | tf_op jit(solution)/shard_map/ppermute | solution.py:471
  21.5 22.0 %collective-permute-start.7 = (bf16[2048,128]{1,0:T(8,128)(2,1)S(1)}, bf16[2048,128]{1,0:T(8,128)(2,1)S(1)}, u32[]{:S(2)}, u32[]{:S(2)}) collective-permute-start(bf16[2048,128]{1,0:T(8,128)(2,1)S(1)} %collective-permute-done.2.refs_6_), channel_id=1, source_target_pairs={{1,0},{2,3},{5,4},{6,7},{9,8},{10,11},{13,12},{14,15},{17,16},{18,... | collective-permute-start | bytes 1572872 | tf_op jit(solution)/shard_map/ppermute | solution.py:63
  30.3 13.1 %collective-permute-start.8 = (bf16[2048,128]{1,0:T(8,128)(2,1)S(1)}, bf16[2048,128]{1,0:T(8,128)(2,1)S(1)}, u32[]{:S(2)}, u32[]{:S(2)}) collective-permute-start(bf16[2048,128]{1,0:T(8,128)(2,1)S(1)} %rounded.1.refs_5_), channel_id=1, source_target_pairs={{1,2},{2,1},{5,6},{6,5},{9,10},{10,9},{13,14},{14,13},{17,18},{18,... | collective-permute-start | bytes 1572872 | tf_op jit(solution)/shard_map/ppermute | solution.py:65
  31.1 9.6 %collective-permute-start.10 = (bf16[1280,128]{1,0:T(8,128)(2,1)S(1)}, bf16[1280,128]{1,0:T(8,128)(2,1)S(1)}, u32[]{:S(2)}, u32[]{:S(2)}) collective-permute-start(bf16[1280,128]{1,0:T(8,128)(2,1)S(1)} %add_convert_fusion.sum_ref), channel_id=1, source_target_pairs={{0,16},{8,24},{16,0},{24,8},{1,17},{9,25},{17,1},{25,9},{2,18},{10... | collective-permute-start | bytes 983048 | tf_op jit(solution)/shard_map/ppermute | solution.py:431
  32.7 1.5 %collective-permute-start.5 = (bf16[768,128]{1,0:T(8,128)(2,1)S(1)}, bf16[768,128]{1,0:T(8,128)(2,1)S(1)}, u32[]{:S(2)}, u32[]{:S(2)}) collective-permute-start(bf16[768,128]{1,0:T(8,128)(2,1)S(1)} %get-tuple-element.33), channel_id=1, source_target_pairs={{0,4},{4,0},{1,5},{5,1},{2,6},{6,2},{3,7},{7,3},{8,12},{12,8},{9,1... | collective-permute-start | bytes 589832 | tf_op jit(solution)/shard_map/ppermute | solution.py:478
  32.8 1.9 %collective-permute-start.3 = (bf16[768,128]{1,0:T(8,128)(2,1)S(1)}, bf16[768,128]{1,0:T(8,128)(2,1)S(1)}, u32[]{:S(2)}, u32[]{:S(2)}) collective-permute-start(bf16[768,128]{1,0:T(8,128)(2,1)S(1)} %pack.1), channel_id=1, source_target_pairs={{0,4},{4,0},{1,5},{5,1},{2,6},{6,2},{3,7},{7,3},{8,12},{12,8},{9,1... | collective-permute-start | bytes 589832 | tf_op jit(solution)/shard_map/ppermute | solution.py:479
